TPU v7x, 32 devices: a whole 2x2x4 slice. The times are simulated.
32 devices in a mesh: ctx: 16 (over z, y, core), exp: 2 (over x).
Axes of the slice: x: 2, y: 2, z: 4, core: 2. Of those that a mesh axis runs over, the one named last changes fastest.
Arguments:
- residual: bfloat16 [1024, 2048], P('ctx', 'exp'), may hold values from -60 to 60
- queries: bfloat16 [1024, 512], P('ctx', 'exp'), may hold values from -6.5 to 6.5
- keys: bfloat16 [1024, 512], P('ctx', 'exp'), may hold values from -6.5 to 6.5
- values: bfloat16 [1024, 512], P('ctx', 'exp'), may hold values from -6 to 6
- out_proj: bfloat16 [512, 2048], P(None, 'exp'), may hold values from -0.5 to 0.5
- norm_gain: float32 [2048], replicated, may hold values from 0.1 to 1.9
- w_gate: bfloat16 [2, 2048, 8192], P('exp', None, 'ctx'), may hold values from -0.125 to 0.125
- w_up: bfloat16 [2, 2048, 8192], P('exp', None, 'ctx'), may hold values from -0.125 to 0.125
- w_down: bfloat16 [2, 8192, 2048], P('exp', 'ctx'), may hold values from -0.0625 to 0.0625
- routes: int32 [1024, 1], P('ctx'), may hold values from 0 to 1; in each aligned block of 64 rows (0 to 63, 64 to 127, ...) at most 32 rows name the same one
- block_mask: int32 [8, 8], replicated, may hold values from 0 to 1, as said below
Outputs:
- mixed: bfloat16 [2, 512, 2048], P('exp', 'ctx')
Inputs may be any that keep to these rules, and one draw needn't show every extreme that they name: `routes`: each stored row is named by exactly 32 of the 64 rows of one index of ctx. `block_mask`: every diagonal entry is 1.
All inputs are finite; a program needn't handle non-finite values.
Results may differ from a plain program's by a relative error of at most 0.006.
Values may be sent and summed in bfloat16 or wider, within the bound.
No kernel may reach another device: no remote copies, remote signals or barrier semaphores. Data moves between devices by JAX's collectives and lax.ppermute only.
A program may use at most 64 MiB of HBM per device.

v0:
```python
import math

import jax
import jax.numpy as jnp
from jax import lax
from jax.sharding import PartitionSpec as P

HD = 128
BLK = 128


def body(
    residual, queries, keys, values, out_proj, norm_gain, w_gate, w_up, w_down, routes, block_mask
):
    local_tokens = residual.shape[0]
    local_width = queries.shape[1]
    heads_here = local_width // HD
    blocks_all = block_mask.shape[0]
    expert_count = lax.axis_size("exp")
    per_expert = local_tokens // expert_count
    scaling = 1.0 / math.sqrt(HD)
    ctx_place = lax.axis_index("ctx")
    query_pos = ctx_place * local_tokens + jnp.arange(local_tokens, dtype=jnp.int32)
    query_blocks = jax.nn.one_hot(query_pos // BLK, blocks_all, dtype=jnp.float32)
    query_mask = jnp.dot(query_blocks, block_mask.astype(jnp.float32))
    query_three = queries.reshape(local_tokens, heads_here, HD)
    key_piece = lax.all_gather(keys, "ctx", axis=0, tiled=True)
    value_piece = lax.all_gather(values, "ctx", axis=0, tiled=True)
    count_here = key_piece.shape[0]
    key_pos = jnp.arange(count_here, dtype=jnp.int32)
    key_blocks = jax.nn.one_hot(key_pos // BLK, blocks_all, dtype=jnp.float32)
    allowed = jnp.dot(query_mask, key_blocks.T) > 0.5
    top_old = jnp.full((heads_here, local_tokens), -1e30, jnp.float32)
    key_three = key_piece.reshape(count_here, heads_here, HD)
    value_three = value_piece.reshape(count_here, heads_here, HD)
    scores = (
        jnp.einsum("qhd,khd->hqk", query_three, key_three, preferred_element_type=jnp.float32)
        * scaling
    )
    scores = jnp.where(allowed[None], scores, -1e30)
    top_new = jnp.maximum(top_old, jnp.max(scores, axis=2))
    exponent = jnp.where(allowed[None], jnp.exp(scores - top_new[:, :, None]), 0.0)
    total_new = jnp.sum(exponent, axis=2)
    product = jnp.einsum(
        "hqk,khd->hqd",
        exponent.astype(jnp.bfloat16),
        value_three,
        preferred_element_type=jnp.float32,
    )
    attended = (product / total_new[:, :, None]).astype(jnp.bfloat16)
    attended = attended.transpose(1, 0, 2).reshape(local_tokens, local_width)
    projected = jnp.dot(
        lax.all_gather(attended, "exp", axis=1, tiled=True),
        out_proj,
        preferred_element_type=jnp.float32,
    )
    hidden = (residual.astype(jnp.float32) + projected).astype(jnp.bfloat16)
    target = routes[:, 0]
    token_ids = jnp.arange(local_tokens, dtype=jnp.int32)
    earlier = (target[:, None] == target[None, :]) & (token_ids[None, :] < token_ids[:, None])
    ranking = jnp.sum(earlier.astype(jnp.int32), axis=1)
    slot_of = target * per_expert + ranking
    slot_ids = jnp.arange(expert_count * per_expert, dtype=jnp.int32)
    placing = (slot_of[None, :] == slot_ids[:, None]).astype(jnp.bfloat16)
    send_buffer = jnp.dot(placing, hidden, preferred_element_type=jnp.float32).astype(jnp.bfloat16)
    send_buffer = send_buffer.reshape(expert_count, per_expert, hidden.shape[1])
    own_rows = lax.all_to_all(send_buffer, "exp", split_axis=0, concat_axis=2, tiled=True)[0]
    values_f = own_rows.astype(jnp.float32)
    meansq = jnp.mean(values_f * values_f, axis=1, keepdims=True)
    normed_own = (values_f * lax.rsqrt(meansq + 1e-05) * norm_gain).astype(jnp.bfloat16)
    normed_rows = lax.all_gather(normed_own, "ctx", axis=0, tiled=True)
    gate_v = jnp.dot(normed_rows, w_gate[0], preferred_element_type=jnp.float32)
    up_v = jnp.dot(normed_rows, w_up[0], preferred_element_type=jnp.float32)
    activ = (jax.nn.silu(gate_v) * up_v).astype(jnp.bfloat16)
    terms = jnp.dot(activ, w_down[0], preferred_element_type=jnp.float32)
    summed = lax.psum_scatter(terms, "ctx", scatter_dimension=0, tiled=True)
    return (own_rows.astype(jnp.float32) + summed).astype(jnp.bfloat16)[None]


def solution(mesh):
    in_specs = (
        P("ctx", "exp"),
        P("ctx", "exp"),
        P("ctx", "exp"),
        P("ctx", "exp"),
        P(None, "exp"),
        P(),
        P("exp", None, "ctx"),
        P("exp", None, "ctx"),
        P("exp", "ctx", None),
        P("ctx", None),
        P(),
    )
    out_specs = P("exp", "ctx", None)
    return jax.shard_map(body, mesh=mesh, in_specs=in_specs, out_specs=out_specs, check_vma=False)
```

profile of v0, /device:TPU:0, one launch (start us, length us, event | category | flops | bytes accessed | tf_op | source)
XLA Modules:
  0.0 200.0 jit_solution(3554734577280564735)
XLA Ops:
  6.5 0.0 copy-start
  6.5 0.0 copy-start.3
  6.5 0.0 copy-start.2
  6.5 0.0 all-gather.2.cloned.1.call-start
  6.6 1.0 convert_reduce_fusion
  7.6 0.7 multiply_add_fusion
  8.2 24.8 %all_gather.12 = bf16[1024,256]{1,0:T(8,128)(2,1)S(1)} all-gather(bf16[64,256]{1,0:T(8,128)(2,1)} %param.13), channel_id=1, replica_groups=mesh['ctx'=16,'exp'=2] {'ctx'}, dimensions={0}, use_global_device_ids=true | all-gather | bytes 557056 | tf_op jit(solution)/shard_map/all_gather | solution.py:27
  33.0 0.2 copy.28
  33.2 1.1 convolution_compare_fusion
  34.4 0.0 copy-done.3
  34.4 0.3 fusion.45
  34.7 0.0 copy-start.1
  34.7 0.0 copy-done.2
  34.7 19.0 %all_gather.13 = bf16[1024,256]{1,0:T(8,128)(2,1)S(1)} all-gather(bf16[64,256]{1,0:T(8,128)(2,1)S(1)} %copy-done.2), channel_id=1, replica_groups=mesh['ctx'=16,'exp'=2] {'ctx'}, dimensions={0}, use_global_device_ids=true | all-gather | bytes 557056 | tf_op jit(solution)/shard_map/all_gather | solution.py:28
  53.7 1.0 copy.31
  54.7 0.3 fusion.22
  55.0 0.0 copy-start.4
  55.0 1.4 fusion.16
  56.4 4.6 %all_gather.14 = bf16[64,512]{1,0:T(8,128)(2,1)S(1)} all-gather(bf16[64,256]{1,0:T(8,128)(2,1)S(1)} %bitcast.64), channel_id=1, replica_groups=mesh['ctx'=16,'exp'=2] {'exp'}, dimensions={1}, use_global_device_ids=true | all-gather | bytes 98304 | tf_op jit(solution)/shard_map/all_gather | solution.py:53
  61.0 0.0 copy-done.1
  61.0 1.7 convolution_convert_fusion
  62.7 7.0 %all_to_all.4 = bf16[2,32,1024]{2,1,0:T(8,128)(2,1)S(1)} all-to-all(bf16[2,32,1024]{2,1,0:T(8,128)(2,1)S(1)} %bitcast.62), channel_id=1, replica_groups=mesh['ctx'=16,'exp'=2] {'exp'}, dimensions={0} | all-to-all | bytes 262144 | tf_op jit(solution)/shard_map/all_to_all | solution.py:67
  69.7 0.1 fusion.24
  69.9 0.2 copy.34
  70.1 0.1 copy.39
  70.2 0.0 copy-done.4
  70.2 0.7 multiply_convert_fusion
  71.0 0.0 all-gather.2.cloned.1.call-update
  71.0 0.0 reduce-scatter.2.cloned.1.call-start
  71.0 39.0 %all-gather.2.cloned.1.call-done = bf16[512,2048]{1,0:T(8,128)(2,1)} async-done(((bf16[32,2048]{1,0:T(8,128)(2,1)}), bf16[512,2048]{1,0:T(8,128)(2,1)}) %all-gather.2.cloned.1.call-update) | async-done | bytes 2097168 | tf_op jit(solution)/shard_map/all_gather | solution.py:71
  110.0 3.5 %fusion.4 = f32[512,512]{1,0:T(8,128)S(1)} fusion(bf16[512,2048]{1,0:T(8,128)(2,1)} %all-gather.2.cloned.1.call-done, bf16[1,2048,512]{2,1,0:T(8,128)(2,1)} %param.17), kind=kOutput, calls=%fused_computation.4 | convolution fusion | flops 1073741824 | bytes 5242880 | tf_op jit(solution)/shard_map/dot_general | solution.py:72
  113.5 0.0 copy-done
  113.5 6.6 %fusion = f32[512,2048]{1,0:T(8,128)} fusion(bf16[1,512,2048]{2,1,0:T(8,128)(2,1)S(1)} %copy-done, bf16[512,2048]{1,0:T(8,128)(2,1)} %all-gather.2.cloned.1.call-done, bf16[1,2048,512]{2,1,0:T(8,128)(2,1)} %param.18, f32[512,512]{1,0:T(8,128)S(1)} %fusion.4), kind=kOutput, calls=%fused_computation | convolution fusion | flops 2149056512 | bytes 11534336 | tf_op jit(solution)/shard_map/dot_general | solution.py:75
  120.1 0.0 reduce-scatter.2.cloned.1.call-update
  120.1 71.4 %reduce-scatter.2.cloned.1.call-done = f32[32,2048]{1,0:T(8,128)} async-done(((f32[512,2048]{1,0:T(8,128)}), f32[32,2048]{1,0:T(8,128)}) %reduce-scatter.2.cloned.1.call-update) | async-done | bytes 262160 | tf_op jit(solution)/shard_map/reduce_scatter | solution.py:76
  191.5 1.6 fusion.31
  (6 shorter events, 0.1 us)
Async XLA Ops:
  6.5 107.0 %copy-start = (bf16[1,512,2048]{2,1,0:T(8,128)(2,1)S(1)}, bf16[1,512,2048]{2,1,0:T(8,128)(2,1)}, u32[]{:S(2)}) copy-start(bf16[1,512,2048]{2,1,0:T(8,128)(2,1)} %param.19) | copy-start | bytes 6291460
  6.5 27.8 %copy-start.3 = (bf16[64,256]{1,0:T(8,128)(2,1)S(1)}, bf16[64,256]{1,0:T(8,128)(2,1)}, u32[]{:S(2)}) copy-start(bf16[64,256]{1,0:T(8,128)(2,1)} %param.12) | copy-start | bytes 98308
  6.5 28.2 %copy-start.2 = (bf16[64,256]{1,0:T(8,128)(2,1)S(1)}, bf16[64,256]{1,0:T(8,128)(2,1)}, u32[]{:S(2)}) copy-start(bf16[64,256]{1,0:T(8,128)(2,1)} %param.14) | copy-start | bytes 98308
  6.5 103.5 %all-gather.2.cloned.1.call-start = ((), (), s32[]{:S(2)}) async-start(), calls=%async_computation.2 | async-start | bytes 2228224 | tf_op jit(solution)/shard_map/all_gather | solution.py:71
  34.7 26.3 %copy-start.1 = (bf16[64,1024]{1,0:T(8,128)(2,1)S(1)}, bf16[64,1024]{1,0:T(8,128)(2,1)}, u32[]{:S(2)}) copy-start(bf16[64,1024]{1,0:T(8,128)(2,1)} %param.11) | copy-start | bytes 393220
  55.0 15.2 %copy-start.4 = (f32[2048]{0:T(1024)S(1)}, f32[2048]{0:T(1024)}, u32[]{:S(2)}) copy-start(f32[2048]{0:T(1024)} %param.16) | copy-start | bytes 24580
  71.0 120.5 %reduce-scatter.2.cloned.1.call-start = ((), (), s32[]{:S(2)}) async-start(), calls=%async_computation.3 | async-start | bytes 4456448 | tf_op jit(solution)/shard_map/reduce_scatter | solution.py:76
Sparse Core Ops, SparseCore 0:
  71.1 38.8 all-gather.1
  120.2 71.2 reduce-scatter.1
where the time goes:
time: 200 us
  waiting for transfers between devices  110 us (55%)
  blocking collectives  55.4 us (28%)
  matrix products  14.6 us (7%)
  between operations  13.5 us (7%)
  other arithmetic  4.48 us (2%)
    reduce_scatter x1, waiting for transfers between devices, body(): summed = lax.psum_scatter(terms, 'ctx', scatter_dimension=0, tiled=True)  71.4 us
    all_gather x1, waiting for transfers between devices, body(): normed_rows = lax.all_gather(normed_own, 'ctx', axis=0, tiled=True)  39 us
    all_gather x1, blocking collectives, body(): key_piece = lax.all_gather(keys, 'ctx', axis=0, tiled=True)  24.8 us
    all_gather x1, blocking collectives, body(): value_piece = lax.all_gather(values, 'ctx', axis=0, tiled=True)  19 us
    all_to_all x1, blocking collectives, body(): lax.all_to_all(send_buffer, 'exp', split_axis=0, concat_axis=2, tiled=True)  7.03 us
    dot_general x1, matrix products, body(): terms = jnp.dot(activ, w_down[0], preferred_element_type=jnp.float32)  6.6 us
    all_gather x1, blocking collectives, body(): lax.all_gather(attended, 'exp', axis=1, tiled=True)  4.59 us
  transfers between devices with their start and end apart: 2, of which 2 were waited for; matrix products, arithmetic and copies ran while one was open for 0% of the time, Pallas kernels for 0%

commit v1 on v0

v1 whole, which is shorter than its diff:
```python
import math

import jax
import jax.numpy as jnp
from jax import lax
from jax.sharding import PartitionSpec as P

HD = 128
BLK = 128
BF = jnp.bfloat16
F32 = jnp.float32


def dot(a, b):
    return jnp.dot(a, b, preferred_element_type=F32)


def plan(n):
    bits = [1 << k for k in range(n.bit_length() - 2, 0, -1)]
    other = bits[:-2] + bits[-2:][::-1]
    return [(a, b) for a, b in zip(bits, other)]


def offsets(stages, which):
    out = [0]
    for masks in stages:
        out = out + [o ^ masks[which] for o in out]
    return out


def body(
    residual, queries, keys, values, out_proj, norm_gain, w_gate, w_up, w_down, routes, block_mask
):
    local = residual.shape[0]
    n = lax.axis_size("ctx")
    experts = lax.axis_size("exp")
    per = local // experts
    me = lax.axis_index("ctx")
    exp_me = lax.axis_index("exp")
    core = me & 1
    stages = plan(n)
    perms = [[(i, i ^ masks[i & 1]) for i in range(n)] for masks in stages]
    width = queries.shape[1] // 2
    heads = width // HD

    def swap_core(x):
        return lax.ppermute(x, "ctx", [(i, i ^ 1) for i in range(n)])

    def swap_exp(x):
        return lax.ppermute(x, "exp", [(0, 1), (1, 0)])

    def gather(x):
        for perm in perms:
            x = jnp.concatenate([x, lax.ppermute(x, "ctx", perm)], axis=0)
        return x

    def scatter(x):
        for perm in perms[::-1]:
            half = x.shape[0] // 2
            come = lax.ppermute(x[half:].astype(BF), "ctx", perm)
            x = x[:half] + come.astype(F32)
        return x

    def mine(x):
        return lax.dynamic_slice_in_dim(x, core * width, width, axis=1)

    def others(x):
        return lax.dynamic_slice_in_dim(x, (1 - core) * width, width, axis=1)

    come = swap_core(jnp.concatenate([others(keys), others(values)], axis=1))
    both = jnp.concatenate([jnp.concatenate([mine(keys), mine(values)], axis=1), come], axis=0)
    all_kv = gather(both)

    target = routes[:, 0]
    token_ids = jnp.arange(local, dtype=jnp.int32)
    earlier = (target[:, None] == target[None, :]) & (token_ids[None, :] < token_ids[:, None])
    slot_of = target * per + jnp.sum(earlier.astype(jnp.int32), axis=1)
    placing = (slot_of[None, :] == token_ids[:, None]).astype(BF)
    q_rows = dot(placing, queries).astype(BF)
    res_rows = dot(placing, residual).astype(BF)
    q_both = jnp.concatenate([mine(q_rows), swap_core(others(q_rows))], axis=0)

    if experts == 2:
        res_own = lax.dynamic_slice_in_dim(res_rows, exp_me * per, per, axis=0)
        res_far = swap_exp(lax.dynamic_slice_in_dim(res_rows, (1 - exp_me) * per, per, axis=0))
        rows = out_proj.shape[0] // 2
        near = swap_exp(lax.dynamic_slice_in_dim(out_proj, core * rows, rows, axis=0))
        far = swap_core(near)
    else:
        res_all = lax.all_to_all(
            res_rows.reshape(experts, per, -1), "exp", split_axis=0, concat_axis=2, tiled=True
        )[0]
        proj_all = lax.all_gather(out_proj, "exp", axis=1, tiled=True)
    gate_far = swap_core(w_gate[0])
    up_far = swap_core(w_up[0])
    down_far = swap_core(w_down[0])

    off = jnp.where(
        core == 0,
        jnp.array(offsets(stages, 0), jnp.int32),
        jnp.array(offsets(stages, 1), jnp.int32),
    )
    block_ids = ((me ^ off) * local) // BLK
    blocks = block_mask.shape[0]
    mask_row = lax.dynamic_index_in_dim(block_mask, (me * local) // BLK, axis=0, keepdims=False)
    hit = (block_ids[:, None] == jnp.arange(blocks, dtype=jnp.int32)[None, :]) & (mask_row[None, :] > 0)
    allowed = jnp.repeat(jnp.any(hit, axis=1), 2 * local)[None, :]
    parts = []
    for h in range(heads):
        q_h = q_both[:, h * HD : (h + 1) * HD]
        k_h = all_kv[:, h * HD : (h + 1) * HD]
        v_h = all_kv[:, width + h * HD : width + (h + 1) * HD]
        scores = lax.dot_general(q_h, k_h, (((1,), (1,)), ((), ())), preferred_element_type=F32)
        scores = jnp.where(allowed, scores * (1.0 / math.sqrt(HD)), -1e30)
        top = jnp.max(scores, axis=1, keepdims=True)
        expo = jnp.where(allowed, jnp.exp(scores - top), 0.0)
        total = jnp.sum(expo, axis=1, keepdims=True)
        parts.append((dot(expo.astype(BF), v_h) / total).astype(BF))
    att = jnp.concatenate(parts, axis=1)
    att_far = swap_core(att[local:])
    att_near = att[:local]
    att = jnp.concatenate(
        [jnp.where(core == 0, att_near, att_far), jnp.where(core == 0, att_far, att_near)], axis=1
    )

    if experts == 2:
        first = exp_me == 0
        att_own = lax.dynamic_slice_in_dim(att, exp_me * per, per, axis=0)
        att_come = swap_exp(lax.dynamic_slice_in_dim(att, (1 - exp_me) * per, per, axis=0))
        att_all = jnp.concatenate(
            [jnp.where(first, att_own, att_come), jnp.where(first, att_come, att_own)], axis=1
        )
        near_att = lax.dynamic_slice_in_dim(att_all, core * rows, rows, axis=1)
        far_att = lax.dynamic_slice_in_dim(att_all, (1 - core) * rows, rows, axis=1)
        hid_own = (res_own.astype(F32) + dot(att_all, out_proj)).astype(BF)
        hid_far = (res_far.astype(F32) + (dot(near_att, near) + dot(far_att, far))).astype(BF)
        hidden = jnp.concatenate(
            [jnp.where(first, hid_own, hid_far), jnp.where(first, hid_far, hid_own)], axis=1
        )
    else:
        att_all = lax.all_to_all(
            att.reshape(experts, per, -1), "exp", split_axis=0, concat_axis=2, tiled=True
        )[0]
        hidden = (res_all.astype(F32) + dot(att_all, proj_all)).astype(BF)
    hidden = hidden.astype(F32)
    meansq = jnp.mean(hidden * hidden, axis=1, keepdims=True)
    normed = (hidden * lax.rsqrt(meansq + 1e-05) * norm_gain).astype(BF)

    rows_in = gather(normed)
    act_near = (jax.nn.silu(dot(rows_in, w_gate[0])) * dot(rows_in, w_up[0])).astype(BF)
    act_far = (jax.nn.silu(dot(rows_in, gate_far)) * dot(rows_in, up_far)).astype(BF)
    terms = dot(act_near, w_down[0]) + dot(act_far, down_far)
    return (hidden + scatter(terms)).astype(BF)[None]


def solution(mesh):
    in_specs = (
        P("ctx", "exp"),
        P("ctx", "exp"),
        P("ctx", "exp"),
        P("ctx", "exp"),
        P(None, "exp"),
        P(),
        P("exp", None, "ctx"),
        P("exp", None, "ctx"),
        P("exp", "ctx", None),
        P("ctx", None),
        P(),
    )
    out_specs = P("exp", "ctx", None)
    return jax.shard_map(body, mesh=mesh, in_specs=in_specs, out_specs=out_specs, check_vma=False)
```

time: 200 us -> 97.9 us (0.49)
  blocking collectives: 55.4 us -> 0 us
  waiting for transfers between devices: 110 us -> 56.7 us
  starting transfers between devices: 0.04 us -> 17.3 us
  between operations: 13.5 us -> 0.23 us
  matrix products: 14.6 us -> 17.5 us
    reduce_scatter x1 -> x0, waiting for transfers between devices: 71.4 us -> none  [body(): summed = lax.psum_scatter(terms, 'ctx', scatter_dimension=0, tiled=True)]
    ppermute x0 -> x19, waiting for transfers between devices: none -> 56.7 us  [the longest x6 33.6 us: gather(): x = jnp.concatenate([x, lax.ppermute(x, 'ctx', perm)], axis=0)]
    all_gather x3 -> x0, blocking collectives: 48.4 us -> none  [the longest x1 24.8 us: body(): key_piece = lax.all_gather(keys, 'ctx', axis=0, tiled=True)]
    all_gather x1 -> x0, waiting for transfers between devices: 39 us -> none  [body(): normed_rows = lax.all_gather(normed_own, 'ctx', axis=0, tiled=True)]
    ppermute x0 -> x19, starting transfers between devices: none -> 17.3 us  [the longest x6 7.61 us: gather(): x = jnp.concatenate([x, lax.ppermute(x, 'ctx', perm)], axis=0)]
    all_to_all x1 -> x0, blocking collectives: 7.03 us -> none  [body(): lax.all_to_all(send_buffer, 'exp', split_axis=0, concat_axis=2, tiled=True)]
    dot_general x6 -> x11, matrix products: 14.6 us -> 17.5 us  [the longest x10 17.2 us: dot(): return jnp.dot(a, b, preferred_element_type=F32)]
  transfers between devices with their start and end apart: 2 -> 19, of which waited for: 2 -> 12; matrix products, arithmetic and copies ran while one was open for 0% -> 15% of each run, Pallas kernels for 0% -> 0%
where the time goes in v1:
time: 97.9 us; the launch traced here: 97.5 us
  waiting for transfers between devices  56.7 us (58%)
  matrix products  17.5 us (18%)
  starting transfers between devices  17.3 us (18%)
  other arithmetic  4.65 us (5%)
  local copies, waits for them, and re-layouts  1.07 us (1%)
    ppermute x6, waiting for transfers between devices, gather(): x = jnp.concatenate([x, lax.ppermute(x, 'ctx', perm)], axis=0)  33.6 us
    ppermute x3, waiting for transfers between devices, scatter(): come = lax.ppermute(x[half:].astype(BF), 'ctx', perm)  20 us
    dot_general x10, matrix products, dot(): return jnp.dot(a, b, preferred_element_type=F32)  17.2 us
    ppermute x6, starting transfers between devices, gather(): x = jnp.concatenate([x, lax.ppermute(x, 'ctx', perm)], axis=0)  7.61 us
    ppermute x3, starting transfers between devices, swap_exp(): return lax.ppermute(x, 'exp', [(0, 1), (1, 0)])  5.09 us
    ppermute x3, starting transfers between devices, scatter(): come = lax.ppermute(x[half:].astype(BF), 'ctx', perm)  2.62 us
    ppermute x3, waiting for transfers between devices, swap_exp(): return lax.ppermute(x, 'exp', [(0, 1), (1, 0)])  2.05 us
  transfers between devices with their start and end apart: 19, of which 12 were waited for; matrix products, arithmetic and copies ran while one was open for 15% of the time, Pallas kernels for 0%

profile of v1, /device:TPU:0, one launch (start us, length us, event | category | flops | bytes accessed | tf_op | source)
XLA Modules:
  0.0 97.5 jit_solution(17614101440243251817)
XLA Ops:
  0.0 0.9 convert_reduce_fusion
  0.9 0.7 multiply_add_fusion
  1.6 0.9 convolution_convert_fusion.1
  2.5 0.5 collective-permute-start
  3.0 0.8 constant_dynamic-slice_fusion.2
  3.8 0.1 collective-permute-start.1
  4.0 3.0 %collective-permute-start.8 = (bf16[256,1024]{1,0:T(8,128)(2,1)S(1)}, bf16[256,1024]{1,0:T(8,128)(2,1)S(1)}, u32[]{:S(2)}, u32[]{:S(2)}) collective-permute-start(bf16[256,1024]{1,0:T(8,128)(2,1)S(1)} %constant_dynamic-slice_fusion), channel_id=1, source_target_pairs={{0,1},{1,0},{2,3},{3,2},{4,5},{5,4},{6,7},{7,6},{8,9},{9,8},{10,11... | collective-permute-start | bytes 1572872 | tf_op jit(solution)/shard_map/ppermute | solution.py:50
  7.0 0.7 and_select_fusion
  7.6 0.7 compare_bitcast_fusion
  8.4 2.7 %collective-permute-start.2 = (bf16[128,256]{1,0:T(8,128)(2,1)S(1)}, bf16[128,256]{1,0:T(8,128)(2,1)S(1)}, u32[]{:S(2)}, u32[]{:S(2)}) collective-permute-start(bf16[128,256]{1,0:T(8,128)(2,1)S(1)} %pad_maximum_fusion.6), channel_id=1, source_target_pairs={{0,16},{2,18},{4,20},{6,22},{8,24},{10,26},{12,28},{14,30},{16,0},... | collective-permute-start | bytes 196616 | tf_op jit(solution)/shard_map/ppermute | solution.py:54
  11.0 0.2 fusion.37
  11.2 3.6 %collective-permute-done.2 = bf16[128,256]{1,0:T(8,128)(2,1)S(1)} collective-permute-done((bf16[128,256]{1,0:T(8,128)(2,1)S(1)}, bf16[128,256]{1,0:T(8,128)(2,1)S(1)}, u32[]{:S(2)}, u32[]{:S(2)}) %collective-permute-start.2) | collective-permute-done | bytes 65568 | tf_op jit(solution)/shard_map/ppermute | solution.py:54
  14.8 0.5 collective-permute-start.3
  15.4 5.2 %collective-permute-done.3 = bf16[256,256]{1,0:T(8,128)(2,1)S(1)} collective-permute-done((bf16[256,256]{1,0:T(8,128)(2,1)S(1)}, bf16[256,256]{1,0:T(8,128)(2,1)S(1)}, u32[]{:S(2)}, u32[]{:S(2)}) %collective-permute-start.3) | collective-permute-done | bytes 131104 | tf_op jit(solution)/shard_map/ppermute | solution.py:54
  20.7 1.6 %collective-permute-start.4 = (bf16[512,256]{1,0:T(8,128)(2,1)S(1)}, bf16[512,256]{1,0:T(8,128)(2,1)S(1)}, u32[]{:S(2)}, u32[]{:S(2)}) collective-permute-start(bf16[512,256]{1,0:T(8,128)(2,1)S(1)} %pad_maximum_fusion.2), channel_id=1, source_target_pairs={{0,4},{2,10},{4,0},{6,14},{8,12},{10,2},{12,8},{14,6},{16,20},{18,... | collective-permute-start | bytes 786440 | tf_op jit(solution)/shard_map/ppermute | solution.py:54
  22.3 4.8 %collective-permute-done.4 = bf16[512,256]{1,0:T(8,128)(2,1)S(1)} collective-permute-done((bf16[512,256]{1,0:T(8,128)(2,1)S(1)}, bf16[512,256]{1,0:T(8,128)(2,1)S(1)}, u32[]{:S(2)}, u32[]{:S(2)}) %collective-permute-start.4) | collective-permute-done | bytes 262176 | tf_op jit(solution)/shard_map/ppermute | solution.py:54
  27.2 0.3 fusion.58
  27.5 0.2 fusion.5
  27.7 0.3 fusion.4
  28.1 0.2 convolution_convert_fusion
  28.3 1.0 %collective-permute-done.5 = bf16[64,128]{1,0:T(8,128)(2,1)S(1)} collective-permute-done((bf16[64,128]{1,0:T(8,128)(2,1)S(1)}, bf16[64,128]{1,0:T(8,128)(2,1)S(1)}, u32[]{:S(2)}, u32[]{:S(2)}) %collective-permute-start.5) | collective-permute-done | bytes 16416 | tf_op jit(solution)/shard_map/ppermute | solution.py:47
  29.3 0.4 collective-permute-start.6
  29.7 1.7 %collective-permute-start.7 = (bf16[32,1024]{1,0:T(8,128)(2,1)S(1)}, bf16[32,1024]{1,0:T(8,128)(2,1)S(1)}, u32[]{:S(2)}, u32[]{:S(2)}) collective-permute-start(bf16[32,1024]{1,0:T(8,128)(2,1)S(1)} %constant_dynamic-slice_fusion.1), channel_id=1, source_target_pairs={{0,1},{1,0},{2,3},{3,2},{4,5},{5,4},{6,7},{7,6},{8,9},{9,8},{10,11... | collective-permute-start | bytes 196616 | tf_op jit(solution)/shard_map/ppermute | solution.py:50
  31.4 1.8 %collective-permute-done.6 = bf16[32,256]{1,0:T(8,128)(2,1)S(1)} collective-permute-done((bf16[32,256]{1,0:T(8,128)(2,1)S(1)}, bf16[32,256]{1,0:T(8,128)(2,1)S(1)}, u32[]{:S(2)}, u32[]{:S(2)}) %collective-permute-start.6) | collective-permute-done | bytes 16416 | tf_op jit(solution)/shard_map/ppermute | solution.py:50
  33.2 0.3 fusion.2
  33.5 0.2 fusion.28
  33.7 0.3 collective-permute-done.7
  34.0 0.2 broadcast_select_fusion.1
  34.2 0.1 fusion.7
  34.4 0.1 fusion.9
  34.5 1.2 %collective-permute-start.10 = (bf16[32,2048]{1,0:T(8,128)(2,1)S(1)}, bf16[32,2048]{1,0:T(8,128)(2,1)S(1)}, u32[]{:S(2)}, u32[]{:S(2)}) collective-permute-start(bf16[32,2048]{1,0:T(8,128)(2,1)S(1)} %fusion.9), channel_id=1, source_target_pairs={{0,16},{2,18},{4,20},{6,22},{8,24},{10,26},{12,28},{14,30},{16,0},... | collective-permute-start | bytes 393224 | tf_op jit(solution)/shard_map/ppermute | solution.py:54
  35.6 7.2 %collective-permute-done.10 = bf16[32,2048]{1,0:T(8,128)(2,1)S(1)} collective-permute-done((bf16[32,2048]{1,0:T(8,128)(2,1)S(1)}, bf16[32,2048]{1,0:T(8,128)(2,1)S(1)}, u32[]{:S(2)}, u32[]{:S(2)}) %collective-permute-start.10) | collective-permute-done | bytes 131104 | tf_op jit(solution)/shard_map/ppermute | solution.py:54
  42.9 1.2 %collective-permute-start.15 = (bf16[512,2048]{1,0:T(8,128)(2,1)}, bf16[512,2048]{1,0:T(8,128)(2,1)}, u32[]{:S(2)}, u32[]{:S(2)}) collective-permute-start(bf16[512,2048]{1,0:T(8,128)(2,1)} %bitcast.5), channel_id=1, source_target_pairs={{0,2},{2,0},{4,6},{6,4},{8,10},{10,8},{12,14},{14,12},{16,18},{18,... | collective-permute-start | bytes 6291464 | tf_op jit(solution)/shard_map/ppermute | solution.py:47
  44.2 5.1 %collective-permute-done.11 = bf16[64,2048]{1,0:T(8,128)(2,1)S(1)} collective-permute-done((bf16[64,2048]{1,0:T(8,128)(2,1)S(1)}, bf16[64,2048]{1,0:T(8,128)(2,1)S(1)}, u32[]{:S(2)}, u32[]{:S(2)}) %collective-permute-start.11) | collective-permute-done | bytes 262176 | tf_op jit(solution)/shard_map/ppermute | solution.py:54
  49.3 1.6 %collective-permute-start.12 = (bf16[128,2048]{1,0:T(8,128)(2,1)S(1)}, bf16[128,2048]{1,0:T(8,128)(2,1)S(1)}, u32[]{:S(2)}, u32[]{:S(2)}) collective-permute-start(bf16[128,2048]{1,0:T(8,128)(2,1)S(1)} %pad_maximum_fusion.1), channel_id=1, source_target_pairs={{0,4},{2,10},{4,0},{6,14},{8,12},{10,2},{12,8},{14,6},{16,20},{18,... | collective-permute-start | bytes 1572872 | tf_op jit(solution)/shard_map/ppermute | solution.py:54
  50.9 7.7 %collective-permute-done.12 = bf16[128,2048]{1,0:T(8,128)(2,1)S(1)} collective-permute-done((bf16[128,2048]{1,0:T(8,128)(2,1)S(1)}, bf16[128,2048]{1,0:T(8,128)(2,1)S(1)}, u32[]{:S(2)}, u32[]{:S(2)}) %collective-permute-start.12) | collective-permute-done | bytes 524320 | tf_op jit(solution)/shard_map/ppermute | solution.py:54
  58.6 2.5 %fusion.51 = f32[256,512]{1,0:T(8,128)S(1)} fusion(bf16[1,2048,512]{2,1,0:T(8,128)(2,1)} %param.19, bf16[128,2048]{1,0:T(8,128)(2,1)S(1)} %collective-permute-done.12, bf16[64,2048]{1,0:T(8,128)(2,1)S(1)} %collective-permute-done.11, bf16[32,2048]{1,0:T(8,128)(2,1)S(1)} %collective-permute-done.10, bf16[32,2048]{1,0:T(8,128)(2,1)S(1)} %fusion.9), kind=kOutput, calls=%fused_computation.113 | convolution fusion | flops 541065216 | bytes 3670016 | tf_op jit(solution)/shard_map/dot_general | solution.py:15
  61.1 4.9 %fusion.12 = f32[256,2048]{1,0:T(8,128)} fusion(f32[256,512]{1,0:T(8,128)S(1)} %fusion.51, bf16[1,512,2048]{2,1,0:T(8,128)(2,1)} %param.21, bf16[1,2048,512]{2,1,0:T(8,128)(2,1)} %param.20, bf16[128,2048]{1,0:T(8,128)(2,1)S(1)} %collective-permute-done.12, bf16[64,2048]{1,0:T(8,128)(2,1)S(1)} %collective-permute-done.11, ...), kind=kOutput, calls=%fused_computation.30 | convolution fusion | flops 1078722560 | bytes 7864320 | tf_op jit(solution)/shard_map/dot_general | solution.py:15
  66.0 3.1 %fusion.56 = f32[256,512]{1,0:T(8,128)} fusion(bf16[2048,512]{1,0:T(8,128)(2,1)} %collective-permute-done.14, bf16[128,2048]{1,0:T(8,128)(2,1)S(1)} %collective-permute-done.12, bf16[64,2048]{1,0:T(8,128)(2,1)S(1)} %collective-permute-done.11, bf16[32,2048]{1,0:T(8,128)(2,1)S(1)} %collective-permute-done.10, bf16[32,2048]{1,0:T(8,128)(2,1)S(1)} %fusion.9), kind=kOutput, calls=%fused_computation.118 | convolution fusion | flops 541065216 | bytes 3670016 | tf_op jit(solution)/shard_map/dot_general | solution.py:15
  69.1 4.7 %convolution_add_fusion = f32[256,2048]{1,0:T(8,128)S(1)} fusion(f32[256,2048]{1,0:T(8,128)} %fusion.12, bf16[512,2048]{1,0:T(8,128)(2,1)} %collective-permute-done.15, f32[256,512]{1,0:T(8,128)} %fusion.56, bf16[2048,512]{1,0:T(8,128)(2,1)} %collective-permute-done.13, bf16[128,2048]{1,0:T(8,128)(2,1)} %copy-done.4, bf16[64,2048]{1,0:T(8,128)(2,1)} %copy-done.1, ...), kind=kOutput, calls=%fused_computation | convolution fusion | flops 1079246848 | bytes 9961472 | tf_op jit(solution)/shard_map/dot_general | solution.py:15
  73.9 1.6 %collective-permute-start.16 = (bf16[128,2048]{1,0:T(8,128)(2,1)S(1)}, bf16[128,2048]{1,0:T(8,128)(2,1)S(1)}, u32[]{:S(2)}, u32[]{:S(2)}) collective-permute-start(bf16[128,2048]{1,0:T(8,128)(2,1)S(1)} %slice.69), channel_id=1, source_target_pairs={{0,4},{2,10},{4,0},{6,14},{8,12},{10,2},{12,8},{14,6},{16,20},{18,... | collective-permute-start | bytes 1572872 | tf_op jit(solution)/shard_map/ppermute | solution.py:60
  75.5 7.7 %collective-permute-done.16 = bf16[128,2048]{1,0:T(8,128)(2,1)S(1)} collective-permute-done((bf16[128,2048]{1,0:T(8,128)(2,1)S(1)}, bf16[128,2048]{1,0:T(8,128)(2,1)S(1)}, u32[]{:S(2)}, u32[]{:S(2)}) %collective-permute-start.16) | collective-permute-done | bytes 524320 | tf_op jit(solution)/shard_map/ppermute | solution.py:60
  83.1 0.1 slice_add_fusion
  83.3 0.1 collective-permute-start.17
  83.4 6.4 %collective-permute-done.17 = bf16[64,2048]{1,0:T(8,128)(2,1)S(1)} collective-permute-done((bf16[64,2048]{1,0:T(8,128)(2,1)S(1)}, bf16[64,2048]{1,0:T(8,128)(2,1)S(1)}, u32[]{:S(2)}, u32[]{:S(2)}) %collective-permute-start.17) | collective-permute-done | bytes 262176 | tf_op jit(solution)/shard_map/ppermute | solution.py:60
  89.8 1.0 collective-permute-start.18
  90.8 6.0 %collective-permute-done.18 = bf16[32,2048]{1,0:T(8,128)(2,1)S(1)} collective-permute-done((bf16[32,2048]{1,0:T(8,128)(2,1)S(1)}, bf16[32,2048]{1,0:T(8,128)(2,1)S(1)}, u32[]{:S(2)}, u32[]{:S(2)}) %collective-permute-start.18) | collective-permute-done | bytes 131104 | tf_op jit(solution)/shard_map/ppermute | solution.py:60
  96.8 0.7 fusion.20
  (46 shorter events, 0.7 us)
Async XLA Ops:
  0.0 3.9 %copy-start = (bf16[512,1024]{1,0:T(8,128)(2,1)S(1)}, bf16[512,1024]{1,0:T(8,128)(2,1)}, u32[]{:S(2)}) copy-start(bf16[512,1024]{1,0:T(8,128)(2,1)} %param.17) | copy-start | bytes 3145732
  2.5 24.7 %collective-permute-start = (bf16[64,128]{1,0:T(8,128)(2,1)S(1)}, bf16[64,128]{1,0:T(8,128)(2,1)S(1)}, u32[]{:S(2)}, u32[]{:S(2)}) collective-permute-start(bf16[64,128]{1,0:T(8,128)(2,1)S(1)} %get-tuple-element.12), channel_id=1, source_target_pairs={{0,2},{2,0},{4,6},{6,4},{8,10},{10,8},{12,14},{14,12},{16,18},{18,... | collective-permute-start | bytes 49160 | tf_op jit(solution)/shard_map/ppermute | solution.py:47
  3.8 4.5 %collective-permute-start.1 = (bf16[64,256]{1,0:T(8,128)(2,1)S(1)}, bf16[64,256]{1,0:T(8,128)(2,1)S(1)}, u32[]{:S(2)}, u32[]{:S(2)}) collective-permute-start(bf16[64,256]{1,0:T(8,128)(2,1)S(1)} %pad_maximum_fusion.9), channel_id=1, source_target_pairs={{0,2},{2,0},{4,6},{6,4},{8,10},{10,8},{12,14},{14,12},{16,18},{18,... | collective-permute-start | bytes 98312 | tf_op jit(solution)/shard_map/ppermute | solution.py:47
  4.0 27.4 %collective-permute-start.8 = (bf16[256,1024]{1,0:T(8,128)(2,1)S(1)}, bf16[256,1024]{1,0:T(8,128)(2,1)S(1)}, u32[]{:S(2)}, u32[]{:S(2)}) collective-permute-start(bf16[256,1024]{1,0:T(8,128)(2,1)S(1)} %constant_dynamic-slice_fusion), channel_id=1, source_target_pairs={{0,1},{1,0},{2,3},{3,2},{4,5},{5,4},{6,7},{7,6},{8,9},{9,8},{10,11... | collective-permute-start | bytes 1572872 | tf_op jit(solution)/shard_map/ppermute | solution.py:50
  8.4 6.4 %collective-permute-start.2 = (bf16[128,256]{1,0:T(8,128)(2,1)S(1)}, bf16[128,256]{1,0:T(8,128)(2,1)S(1)}, u32[]{:S(2)}, u32[]{:S(2)}) collective-permute-start(bf16[128,256]{1,0:T(8,128)(2,1)S(1)} %pad_maximum_fusion.6), channel_id=1, source_target_pairs={{0,16},{2,18},{4,20},{6,22},{8,24},{10,26},{12,28},{14,30},{16,0},... | collective-permute-start | bytes 196616 | tf_op jit(solution)/shard_map/ppermute | solution.py:54
  14.8 13.3 %copy-start.2 = (bf16[64,1024]{1,0:T(8,128)(2,1)S(1)}, bf16[64,1024]{1,0:T(8,128)(2,1)}, u32[]{:S(2)}) copy-start(bf16[64,1024]{1,0:T(8,128)(2,1)} %param.13) | copy-start | bytes 393220
  14.8 5.9 %collective-permute-start.3 = (bf16[256,256]{1,0:T(8,128)(2,1)S(1)}, bf16[256,256]{1,0:T(8,128)(2,1)S(1)}, u32[]{:S(2)}, u32[]{:S(2)}) collective-permute-start(bf16[256,256]{1,0:T(8,128)(2,1)S(1)} %pad_maximum_fusion.4), channel_id=1, source_target_pairs={{0,8},{2,6},{4,12},{6,2},{8,0},{10,14},{12,4},{14,10},{16,24},{18,... | collective-permute-start | bytes 393224 | tf_op jit(solution)/shard_map/ppermute | solution.py:54
  20.7 6.4 %collective-permute-start.4 = (bf16[512,256]{1,0:T(8,128)(2,1)S(1)}, bf16[512,256]{1,0:T(8,128)(2,1)S(1)}, u32[]{:S(2)}, u32[]{:S(2)}) collective-permute-start(bf16[512,256]{1,0:T(8,128)(2,1)S(1)} %pad_maximum_fusion.2), channel_id=1, source_target_pairs={{0,4},{2,10},{4,0},{6,14},{8,12},{10,2},{12,8},{14,6},{16,20},{18,... | collective-permute-start | bytes 786440 | tf_op jit(solution)/shard_map/ppermute | solution.py:54
  28.0 6.3 %copy-start.3 = (f32[2048]{0:T(1024)S(1)}, f32[2048]{0:T(1024)}, u32[]{:S(2)}) copy-start(f32[2048]{0:T(1024)} %param.18) | copy-start | bytes 24580
  28.1 1.2 %collective-permute-start.5 = (bf16[64,128]{1,0:T(8,128)(2,1)S(1)}, bf16[64,128]{1,0:T(8,128)(2,1)S(1)}, u32[]{:S(2)}, u32[]{:S(2)}) collective-permute-start(bf16[64,128]{1,0:T(8,128)(2,1)S(1)} %slice.46), channel_id=1, source_target_pairs={{0,2},{2,0},{4,6},{6,4},{8,10},{10,8},{12,14},{14,12},{16,18},{18,... | collective-permute-start | bytes 49160 | tf_op jit(solution)/shard_map/ppermute | solution.py:47
  29.3 3.9 %collective-permute-start.6 = (bf16[32,256]{1,0:T(8,128)(2,1)S(1)}, bf16[32,256]{1,0:T(8,128)(2,1)S(1)}, u32[]{:S(2)}, u32[]{:S(2)}) collective-permute-start(bf16[32,256]{1,0:T(8,128)(2,1)S(1)} %fusion.25), channel_id=1, source_target_pairs={{0,1},{1,0},{2,3},{3,2},{4,5},{5,4},{6,7},{7,6},{8,9},{9,8},{10,11... | collective-permute-start | bytes 49160 | tf_op jit(solution)/shard_map/ppermute | solution.py:50
  29.7 4.3 %collective-permute-start.7 = (bf16[32,1024]{1,0:T(8,128)(2,1)S(1)}, bf16[32,1024]{1,0:T(8,128)(2,1)S(1)}, u32[]{:S(2)}, u32[]{:S(2)}) collective-permute-start(bf16[32,1024]{1,0:T(8,128)(2,1)S(1)} %constant_dynamic-slice_fusion.1), channel_id=1, source_target_pairs={{0,1},{1,0},{2,3},{3,2},{4,5},{5,4},{6,7},{7,6},{8,9},{9,8},{10,11... | collective-permute-start | bytes 196616 | tf_op jit(solution)/shard_map/ppermute | solution.py:50
  31.4 2.6 %collective-permute-start.9 = (bf16[256,1024]{1,0:T(8,128)(2,1)S(1)}, bf16[256,1024]{1,0:T(8,128)(2,1)S(1)}, u32[]{:S(2)}, u32[]{:S(2)}) collective-permute-start(bf16[256,1024]{1,0:T(8,128)(2,1)S(1)} %collective-permute-done.8), channel_id=1, source_target_pairs={{0,2},{2,0},{4,6},{6,4},{8,10},{10,8},{12,14},{14,12},{16,18},{18,... | collective-permute-start | bytes 1572872 | tf_op jit(solution)/shard_map/ppermute | solution.py:47
  34.5 8.4 %collective-permute-start.10 = (bf16[32,2048]{1,0:T(8,128)(2,1)S(1)}, bf16[32,2048]{1,0:T(8,128)(2,1)S(1)}, u32[]{:S(2)}, u32[]{:S(2)}) collective-permute-start(bf16[32,2048]{1,0:T(8,128)(2,1)S(1)} %fusion.9), channel_id=1, source_target_pairs={{0,16},{2,18},{4,20},{6,22},{8,24},{10,26},{12,28},{14,30},{16,0},... | collective-permute-start | bytes 393224 | tf_op jit(solution)/shard_map/ppermute | solution.py:54
  35.6 30.3 %collective-permute-start.14 = (bf16[2048,512]{1,0:T(8,128)(2,1)}, bf16[2048,512]{1,0:T(8,128)(2,1)}, u32[]{:S(2)}, u32[]{:S(2)}) collective-permute-start(bf16[2048,512]{1,0:T(8,128)(2,1)} %bitcast.4), channel_id=1, source_target_pairs={{0,2},{2,0},{4,6},{6,4},{8,10},{10,8},{12,14},{14,12},{16,18},{18,... | collective-permute-start | bytes 6291464 | tf_op jit(solution)/shard_map/ppermute | solution.py:47
  42.9 6.4 %collective-permute-start.11 = (bf16[64,2048]{1,0:T(8,128)(2,1)S(1)}, bf16[64,2048]{1,0:T(8,128)(2,1)S(1)}, u32[]{:S(2)}, u32[]{:S(2)}) collective-permute-start(bf16[64,2048]{1,0:T(8,128)(2,1)S(1)} %pad_maximum_fusion.3), channel_id=1, source_target_pairs={{0,8},{2,6},{4,12},{6,2},{8,0},{10,14},{12,4},{14,10},{16,24},{18,... | collective-permute-start | bytes 786440 | tf_op jit(solution)/shard_map/ppermute | solution.py:54
  42.9 26.2 %collective-permute-start.15 = (bf16[512,2048]{1,0:T(8,128)(2,1)}, bf16[512,2048]{1,0:T(8,128)(2,1)}, u32[]{:S(2)}, u32[]{:S(2)}) collective-permute-start(bf16[512,2048]{1,0:T(8,128)(2,1)} %bitcast.5), channel_id=1, source_target_pairs={{0,2},{2,0},{4,6},{6,4},{8,10},{10,8},{12,14},{14,12},{16,18},{18,... | collective-permute-start | bytes 6291464 | tf_op jit(solution)/shard_map/ppermute | solution.py:47
  44.2 24.9 %collective-permute-start.13 = (bf16[2048,512]{1,0:T(8,128)(2,1)}, bf16[2048,512]{1,0:T(8,128)(2,1)}, u32[]{:S(2)}, u32[]{:S(2)}) collective-permute-start(bf16[2048,512]{1,0:T(8,128)(2,1)} %bitcast.3), channel_id=1, source_target_pairs={{0,2},{2,0},{4,6},{6,4},{8,10},{10,8},{12,14},{14,12},{16,18},{18,... | collective-permute-start | bytes 6291464 | tf_op jit(solution)/shard_map/ppermute | solution.py:47
  49.3 16.7 %copy-start.1 = (bf16[64,2048]{1,0:T(8,128)(2,1)}, bf16[64,2048]{1,0:T(8,128)(2,1)S(1)}, u32[]{:S(2)}) copy-start(bf16[64,2048]{1,0:T(8,128)(2,1)S(1)} %collective-permute-done.11) | copy-start | bytes 786436
  49.3 9.2 %collective-permute-start.12 = (bf16[128,2048]{1,0:T(8,128)(2,1)S(1)}, bf16[128,2048]{1,0:T(8,128)(2,1)S(1)}, u32[]{:S(2)}, u32[]{:S(2)}) collective-permute-start(bf16[128,2048]{1,0:T(8,128)(2,1)S(1)} %pad_maximum_fusion.1), channel_id=1, source_target_pairs={{0,4},{2,10},{4,0},{6,14},{8,12},{10,2},{12,8},{14,6},{16,20},{18,... | collective-permute-start | bytes 1572872 | tf_op jit(solution)/shard_map/ppermute | solution.py:54
  58.6 7.4 %copy-start.4 = (bf16[128,2048]{1,0:T(8,128)(2,1)}, bf16[128,2048]{1,0:T(8,128)(2,1)S(1)}, u32[]{:S(2)}) copy-start(bf16[128,2048]{1,0:T(8,128)(2,1)S(1)} %collective-permute-done.12) | copy-start | bytes 1572868
  73.9 9.2 %collective-permute-start.16 = (bf16[128,2048]{1,0:T(8,128)(2,1)S(1)}, bf16[128,2048]{1,0:T(8,128)(2,1)S(1)}, u32[]{:S(2)}, u32[]{:S(2)}) collective-permute-start(bf16[128,2048]{1,0:T(8,128)(2,1)S(1)} %slice.69), channel_id=1, source_target_pairs={{0,4},{2,10},{4,0},{6,14},{8,12},{10,2},{12,8},{14,6},{16,20},{18,... | collective-permute-start | bytes 1572872 | tf_op jit(solution)/shard_map/ppermute | solution.py:60
  83.3 6.5 %collective-permute-start.17 = (bf16[64,2048]{1,0:T(8,128)(2,1)S(1)}, bf16[64,2048]{1,0:T(8,128)(2,1)S(1)}, u32[]{:S(2)}, u32[]{:S(2)}) collective-permute-start(bf16[64,2048]{1,0:T(8,128)(2,1)S(1)} %slice.70), channel_id=1, source_target_pairs={{0,8},{2,6},{4,12},{6,2},{8,0},{10,14},{12,4},{14,10},{16,24},{18,... | collective-permute-start | bytes 786440 | tf_op jit(solution)/shard_map/ppermute | solution.py:60
  89.8 6.9 %collective-permute-start.18 = (bf16[32,2048]{1,0:T(8,128)(2,1)S(1)}, bf16[32,2048]{1,0:T(8,128)(2,1)S(1)}, u32[]{:S(2)}, u32[]{:S(2)}) collective-permute-start(bf16[32,2048]{1,0:T(8,128)(2,1)S(1)} %slice.71), channel_id=1, source_target_pairs={{0,16},{2,18},{4,20},{6,22},{8,24},{10,26},{12,28},{14,30},{16,0},... | collective-permute-start | bytes 393224 | tf_op jit(solution)/shard_map/ppermute | solution.py:60

commit v2 on v1

v2 whole, which is shorter than its diff:
```python
import functools
import math

import jax
import jax.numpy as jnp
from jax import lax
from jax.experimental import pallas as pl
from jax.experimental.pallas import tpu as pltpu
from jax.sharding import PartitionSpec as P

HD = 128
BLK = 128
VMEM_LIMIT = 48 * 2**20
BF = jnp.bfloat16
F32 = jnp.float32


def dot(a, b):
    return jnp.dot(a, b, preferred_element_type=F32)


def distances(bits):
    out = [0]
    for bit in bits:
        out = out + [o ^ bit for o in out]
    return out


def pairs_from(bits):
    return [bits[k : k + 2] for k in range(0, len(bits), 2)]


def gathered(stages):
    out = [0]
    for bits in stages:
        out = [o ^ d for d in distances(bits) for o in out]
    return out


def scattered(stages):
    if not stages:
        return [0]
    return [d ^ o for d in distances(stages[0]) for o in scattered(stages[1:])]


def prepare_kernel(me, mask, keys, values, queries, targets, kv, q_rows, placing, allowed, *, far):
    local, width = keys.shape
    kv[:, :width] = keys[...]
    kv[:, width:] = values[...]
    target = targets[...]
    experts = far["experts"]
    per = local // experts
    row = lax.broadcasted_iota(jnp.int32, (local, local), 0)
    col = lax.broadcasted_iota(jnp.int32, (local, local), 1)
    named = lax.broadcasted_iota(jnp.int32, (experts, local), 0) == target
    before = dot(named.astype(BF), (row < col).astype(BF))
    rank = jnp.sum(jnp.where(named, before, 0.0), axis=0, keepdims=True).astype(jnp.int32)
    place = (row == target * per + rank).astype(BF)
    placing[...] = place
    q_rows[...] = dot(place, queries[...]).astype(BF)
    block = lax.broadcasted_iota(jnp.int32, allowed.shape, 1) // local
    mine = (me[0] * local) // BLK
    chosen = jnp.zeros(allowed.shape, jnp.int32)
    for b, distance in enumerate(far["distances"]):
        chosen = jnp.where(block == b, mask[mine, ((me[0] ^ distance) * local) // BLK], chosen)
    allowed[...] = chosen


def prepare(me, mask, keys, values, queries, routes, experts, order):
    local, width = keys.shape
    smem, vmem = pl.BlockSpec(memory_space=pltpu.SMEM), pl.BlockSpec(memory_space=pltpu.VMEM)
    return pl.pallas_call(
        functools.partial(prepare_kernel, far=dict(experts=experts, distances=order)),
        out_shape=(
            jax.ShapeDtypeStruct((local, 2 * width), BF),
            jax.ShapeDtypeStruct(queries.shape, BF),
            jax.ShapeDtypeStruct((local, local), BF),
            jax.ShapeDtypeStruct((1, len(order) * local), jnp.int32),
        ),
        in_specs=[smem] * 2 + [vmem] * 4,
        out_specs=[vmem] * 4,
    )(me[None], mask, keys, values, queries, routes.reshape(1, local))


def expert_rows(x, near, far):
    total = None
    for gate, up, down in (near, far):
        act = (jax.nn.silu(dot(x, gate[...])) * dot(x, up[...])).astype(BF)
        part = dot(act, down[...])
        total = part if total is None else total + part
    return total


def expert_kernel(
    att_at, res_at, att, res_hbm, proj_hbm, gain, gate0, up0, down0, gate1, up1, down1,
    own, keep, send, att_rows, hidden, normed, res, proj, gates, ups, downs, sems,
):
    blocks, per, feats = res.shape
    sources, _, width = att.shape
    sources //= blocks
    pieces = send.shape[0] + 1
    size = blocks * per // pieces
    rows = 2 * size
    tile = math.gcd(feats, 512)
    cols = [slice(c, c + tile) for c in range(0, feats, tile)]
    moves = [
        pltpu.make_async_copy(src, dst, sems.at[i])
        for i, (src, dst) in enumerate(
            (
                (proj_hbm, proj), (res_hbm, res), (gate0, gates.at[0]), (up0, ups.at[0]),
                (gate1, gates.at[1]), (up1, ups.at[1]), (down0, downs.at[0]), (down1, downs.at[1]),
            )
        )
    ]
    for move in moves:
        move.start()
    for b in range(blocks):
        for s in range(sources):
            att_rows[b * per : (b + 1) * per, s * width : (s + 1) * width] = att[
                att_at[b] * sources + s
            ]
    moves[0].wait()
    moves[1].wait()
    spans = [slice(k, k + rows) for k in range(0, blocks * per, rows)]
    for span in spans:
        squares = 0.0
        for c in cols:
            projected = dot(att_rows[span, :], proj[:, c])
            added = jnp.concatenate(
                [res[res_at[b], :, c] for b in range(span.start // per, span.stop // per)], axis=0
            )
            part = (added.astype(F32) + projected).astype(BF)
            hidden[span, c] = part
            part = part.astype(F32)
            squares = squares + jnp.sum(part * part, axis=1, keepdims=True)
        scale = lax.rsqrt(squares / feats + 1e-05)
        for c in cols:
            normed[span, c] = (hidden[span, c].astype(F32) * scale * gain[:, c]).astype(BF)
    own[...] = hidden[:per, :].astype(F32)
    acts = []
    for side in (0, 1):
        moves[2 + 2 * side].wait()
        moves[3 + 2 * side].wait()
        for span in spans:
            x = normed[span, :]
            acts.append((jax.nn.silu(dot(x, gates[side])) * dot(x, ups[side])).astype(BF))
    moves[6].wait()
    moves[7].wait()
    for k in range(len(spans)):
        for c in cols:
            total = dot(acts[k], downs[0, :, c]) + dot(acts[len(spans) + k], downs[1, :, c])
            for piece in (0, 1):
                part = total[piece * size : (piece + 1) * size]
                if 2 * k + piece == 0:
                    keep[:, c] = part
                else:
                    send[2 * k + piece - 1, :, c] = part.astype(BF)


def expert(att_at, res_at, att, res, proj, gain, near, far):
    blocks, per, feats = res.shape
    units = near[0].shape[1]
    rows = blocks * per
    smem, vmem = pl.BlockSpec(memory_space=pltpu.SMEM), pl.BlockSpec(memory_space=pltpu.VMEM)
    hbm = pl.BlockSpec(memory_space=pl.ANY)
    return pl.pallas_call(
        expert_kernel,
        out_shape=(
            jax.ShapeDtypeStruct((per, feats), F32),
            jax.ShapeDtypeStruct((rows // 4, feats), F32),
            jax.ShapeDtypeStruct((3, rows // 4, feats), BF),
        ),
        in_specs=[smem] * 2 + [vmem] + [hbm] * 2 + [vmem] + [hbm] * 6,
        out_specs=[vmem] * 3,
        scratch_shapes=[
            pltpu.VMEM((rows, proj.shape[0]), BF),
            pltpu.VMEM((rows, feats), BF),
            pltpu.VMEM((rows, feats), BF),
            pltpu.VMEM(res.shape, BF),
            pltpu.VMEM(proj.shape, BF),
            pltpu.VMEM((2, feats, units), BF),
            pltpu.VMEM((2, feats, units), BF),
            pltpu.VMEM((2, units, feats), BF),
            pltpu.SemaphoreType.DMA((8,)),
        ],
        compiler_params=pltpu.CompilerParams(vmem_limit_bytes=VMEM_LIMIT),
        cost_estimate=pl.CostEstimate(
            flops=12 * rows * feats * units, bytes_accessed=12 * feats * units, transcendentals=0
        ),
    )(att_at, res_at, att, res, proj, gain[None], *near, *far)


def body(
    residual, queries, keys, values, out_proj, norm_gain, w_gate, w_up, w_down, routes, block_mask
):
    local = residual.shape[0]
    n = lax.axis_size("ctx")
    experts = lax.axis_size("exp")
    per = local // experts
    me = lax.axis_index("ctx")
    exp_me = lax.axis_index("exp")
    core = me & 1
    bits = [1 << k for k in range(1, n.bit_length() - 1)]
    kv_stages = [pair[::-1] for pair in pairs_from(bits[::-1])]
    sum_stages = pairs_from(bits)
    one, two = bits[::-1], bits[:1:-1] + bits[:2]
    res_masks = list(zip(one, two))

    def by_core(even, odd):
        return jnp.where(core == 0, even, odd)

    def move(x, even, odd=None):
        masks = (even, even if odd is None else odd)
        return lax.ppermute(x, "ctx", [(i, i ^ masks[i & 1]) for i in range(n)])

    def swap_core(x):
        return move(x, 1)

    def swap_exp(x):
        return lax.ppermute(x, "exp", [(0, 1), (1, 0)])

    def gather(x, stages):
        for bits in stages:
            x = jnp.concatenate([x] + [move(x, d) for d in distances(bits)[1:]], axis=0)
        return x

    def scatter(keep, send):
        for k, stage in enumerate(sum_stages):
            if k:
                pieces = jnp.split(keep, 1 << len(stage), axis=0)
                keep, send = pieces[0], [piece.astype(BF) for piece in pieces[1:]]
            for piece, distance in zip(send, distances(stage)[1:]):
                keep = keep + move(piece, distance).astype(F32)
        return keep

    kv_order = gathered(kv_stages)
    width = keys.shape[1]
    heads = width // HD
    all_kv, q_rows, placing, allowed = prepare(
        me, block_mask, keys, values, queries, routes, experts, kv_order + [o ^ 1 for o in kv_order]
    )
    allowed = allowed > 0
    all_kv = gather(all_kv, kv_stages[:1])
    rows = out_proj.shape[0] // 2
    proj_go = lax.dynamic_slice_in_dim(out_proj, core * rows, rows, axis=0)
    all_kv, proj_go = lax.optimization_barrier((all_kv, proj_go))
    all_kv = gather(all_kv, kv_stages[1:-1])
    last = [move(x, d) for d in distances(kv_stages[-1])[1:] for x in jnp.split(all_kv, 2, axis=0)]
    all_kv = jnp.concatenate([all_kv] + last, axis=0)
    far_kv = swap_core(all_kv)

    near_w = (w_gate[0], w_up[0], w_down[0])
    far_w = tuple(swap_core(w) for w in near_w)
    direct = experts == 2 and per % 32 == 0
    if direct:
        first = exp_me == 0

        def both_halves(mine, theirs):
            return jnp.concatenate(
                [jnp.where(first, mine, theirs), jnp.where(first, theirs, mine)], axis=1
            )

        own_rows = lax.dynamic_slice_in_dim(placing, exp_me * per, per, axis=0)
        res_both = both_halves(residual, swap_exp(residual))
        res_all = dot(own_rows, res_both).astype(BF)
        for masks in res_masks:
            res_all = jnp.concatenate([res_all, move(res_all, *masks)], axis=0)
        proj_near = swap_exp(proj_go)
        proj_far = swap_core(proj_near)
        proj_come = jnp.concatenate([by_core(proj_near, proj_far), by_core(proj_far, proj_near)], axis=0)
        proj_all = both_halves(out_proj, proj_come)
    else:
        res_rows = dot(placing, residual).astype(BF)
        res_all = lax.all_to_all(
            res_rows.reshape(experts, per, -1), "exp", split_axis=0, concat_axis=2, tiled=True
        )[0]
        proj_all = lax.all_gather(out_proj, "exp", axis=1, tiled=True)

    all_kv = jnp.concatenate([all_kv, far_kv], axis=0)
    parts = []
    for h in range(heads):
        cols = slice(h * HD, (h + 1) * HD)
        k_h, v_h = all_kv[:, :width][:, cols], all_kv[:, width:][:, cols]
        scores = lax.dot_general(
            q_rows[:, cols], k_h, (((1,), (1,)), ((), ())), preferred_element_type=F32
        )
        scores = jnp.where(allowed, scores * (1.0 / math.sqrt(HD)), -1e30)
        top = jnp.max(scores, axis=1, keepdims=True)
        expo = jnp.where(allowed, jnp.exp(scores - top), 0.0)
        total = jnp.sum(expo, axis=1, keepdims=True)
        parts.append((dot(expo.astype(BF), v_h) / total).astype(BF))
    att = jnp.concatenate(parts, axis=1).reshape(experts, per, width)

    if direct:
        groups = [[(2 * k + c) * experts + e for k in range(n // 2) for e in range(experts)] for c in (0, 1)]
        go = jnp.broadcast_to(att[None], (n // 2, experts, per, width)).reshape(-1, per, width)
        att_all = lax.all_to_all(
            go, ("ctx", "exp"), split_axis=0, concat_axis=0, axis_index_groups=groups, tiled=True
        )
        order = scattered(sum_stages)
        places = [gathered([[masks[c]] for masks in res_masks]) for c in (0, 1)]
        res_at = by_core(*(jnp.array([place.index(o) for o in order], jnp.int32) for place in places))
        hidden, keep, send = expert(
            (me ^ jnp.array(order, jnp.int32)) >> 1, res_at, att_all,
            res_all.reshape(n // 2, per, -1), proj_all, norm_gain, near_w, far_w,
        )
        summed = scatter(keep, [send[k] for k in range(3)])
    else:
        att_all = lax.all_to_all(att, "exp", split_axis=0, concat_axis=2, tiled=True)[0]
        hidden = (res_all.astype(F32) + dot(att_all, proj_all)).astype(BF).astype(F32)
        meansq = jnp.mean(hidden * hidden, axis=1, keepdims=True)
        normed = (hidden * lax.rsqrt(meansq + 1e-05) * norm_gain).astype(BF)
        order = scattered(sum_stages)
        found = gather(normed, sum_stages).reshape(n // 2, per, -1)
        found = jnp.stack([found[gathered(sum_stages).index(o)] for o in order]).reshape(n // 2 * per, -1)
        pieces = jnp.split(expert_rows(found, near_w, far_w), 4, axis=0)
        summed = scatter(pieces[0], [piece.astype(BF) for piece in pieces[1:]])
    return (hidden + summed).astype(BF)[None]


def solution(mesh):
    in_specs = (
        P("ctx", "exp"),
        P("ctx", "exp"),
        P("ctx", "exp"),
        P("ctx", "exp"),
        P(None, "exp"),
        P(),
        P("exp", None, "ctx"),
        P("exp", None, "ctx"),
        P("exp", "ctx", None),
        P("ctx", None),
        P(),
    )
    out_specs = P("exp", "ctx", None)
    return jax.shard_map(body, mesh=mesh, in_specs=in_specs, out_specs=out_specs, check_vma=False)
```

time: 97.9 us -> 79.3 us (0.81)
  waiting for transfers between devices: 56.7 us -> 36.8 us
  matrix products: 17.5 us -> 1.27 us
  Pallas kernels: 0 us -> 8.59 us
  starting transfers between devices: 17.3 us -> 24 us
  other arithmetic: 4.65 us -> 5.92 us
    ppermute x16 -> x17, waiting for transfers between devices: 54.7 us -> 30.1 us  [move(): return lax.ppermute(x, 'ctx', [(i, i ^ masks[i & 1]) for i in range(n)])]
    dot_general x10 -> x3, matrix products: 17.2 us -> 0.65 us  [dot(): return jnp.dot(a, b, preferred_element_type=F32)]
    pallas_call x0 -> x2, Pallas kernels: none -> 8.59 us  [the longest x1 6.85 us: expert(): pl.pallas_call(expert_kernel, out_shape=(jax.ShapeDtypeStruct((per, feats...]
    all_to_all x0 -> x1, waiting for transfers between devices: none -> 5.87 us  [body(): lax.all_to_all(go, ('ctx', 'exp'), split_axis=0, concat_axis=0, axis_inde...]
    ppermute x16 -> x17, starting transfers between devices: 12.2 us -> 17.1 us  [move(): return lax.ppermute(x, 'ctx', [(i, i ^ masks[i & 1]) for i in range(n)])]
    all_to_all x0 -> x1, starting transfers between devices: none -> 3.81 us  [body(): lax.all_to_all(go, ('ctx', 'exp'), split_axis=0, concat_axis=0, axis_inde...]
    concatenate x7, other arithmetic: 0.1 us -> 2.26 us  [the longest x3 1.18 us: body(): res_all = jnp.concatenate([res_all, move(res_all, *masks)], axis=0)]
    ppermute x3 -> x2, starting transfers between devices: 5.09 us -> 3.1 us  [swap_exp(): return lax.ppermute(x, 'exp', [(0, 1), (1, 0)])]
  transfers between devices with their start and end apart: 19 -> 20, of which waited for: 12 -> 10; matrix products, arithmetic and copies ran while one was open for 15% -> 11% of each run, Pallas kernels for 0% -> 0%
where the time goes in v2:
time: 79.3 us; the launch traced here: 78.9 us
  waiting for transfers between devices  36.8 us (46%)
  starting transfers between devices  24 us (30%)
  Pallas kernels  8.59 us (11%)
  other arithmetic  5.92 us (7%)
  local copies, waits for them, and re-layouts  2.04 us (3%)
  matrix products  1.27 us (2%)
    ppermute x17, waiting for transfers between devices, move(): return lax.ppermute(x, 'ctx', [(i, i ^ masks[i & 1]) for i in range(n)])  30.1 us
    ppermute x17, starting transfers between devices, move(): return lax.ppermute(x, 'ctx', [(i, i ^ masks[i & 1]) for i in range(n)])  17.1 us
    pallas_call x1, Pallas kernels, expert(): pl.pallas_call(expert_kernel, out_shape=(jax.ShapeDtypeStruct((per, feats...  6.85 us
    all_to_all x1, waiting for transfers between devices, body(): lax.all_to_all(go, ('ctx', 'exp'), split_axis=0, concat_axis=0, axis_inde...  5.87 us
    all_to_all x1, starting transfers between devices, body(): lax.all_to_all(go, ('ctx', 'exp'), split_axis=0, concat_axis=0, axis_inde...  3.81 us
    ppermute x2, starting transfers between devices, swap_exp(): return lax.ppermute(x, 'exp', [(0, 1), (1, 0)])  3.1 us
    select_n x2, other arithmetic, by_core(): return jnp.where(core == 0, even, odd)  1.95 us
    pallas_call x1, Pallas kernels, prepare(): pl.pallas_call(functools.partial(prepare_kernel, far=dict(experts=experts...  1.74 us
  transfers between devices with their start and end apart: 20, of which 10 were waited for; matrix products, arithmetic and copies ran while one was open for 11% of the time, Pallas kernels for 0%

profile of v2, /device:TPU:0, one launch (start us, length us, event | category | flops | bytes accessed | tf_op | source)
XLA Modules:
  0.0 78.9 jit_solution(5963599015561464598)
XLA Ops:
  0.0 1.7 %shard_map.136 = (bf16[64,512]{1,0:T(8,128)(2,1)}, bf16[64,256]{1,0:T(8,128)(2,1)}, bf16[64,64]{1,0:T(8,128)(2,1)}, s32[1,1024]{1,0:T(1,128)}) custom-call(s32[1]{0:T(128)} %bitcast.me, s32[8,8]{1,0:T(8,128)} %mask.1, bf16[64,256]{1,0:T(8,128)(2,1)} %keys.1, bf16[64,256]{1,0:T(8,128)(2,1)} %values.1, bf16[64,256]{1,0:T(8,128)(2,1)} %queries.1, s32[1,64]{1,0:T(1,128)} %bitcast.24), custom_call_target="tpu_custom_call" | custom-call | tf_op jit(solution)/shard_map/pallas_call | solution.py:72
  1.7 5.1 %collective-permute-start.2 = (bf16[64,512]{1,0:T(8,128)(2,1)}, bf16[64,512]{1,0:T(8,128)(2,1)S(1)}, u32[]{:S(2)}, u32[]{:S(2)}) collective-permute-start(bf16[64,512]{1,0:T(8,128)(2,1)} %get-tuple-element.16), channel_id=1, source_target_pairs={{0,24},{2,26},{4,28},{6,30},{8,16},{10,18},{12,20},{14,22},{16,8},... | collective-permute-start | bytes 196616 | tf_op jit(solution)/shard_map/ppermute | solution.py:214
  6.9 0.0 collective-permute-start.1
  6.9 0.6 collective-permute-start
  7.5 1.6 %collective-permute-start.6 = (bf16[64,1024]{1,0:T(8,128)(2,1)}, bf16[64,1024]{1,0:T(8,128)(2,1)S(1)}, u32[]{:S(2)}, u32[]{:S(2)}) collective-permute-start(bf16[64,1024]{1,0:T(8,128)(2,1)} %param.14), channel_id=1, source_target_pairs={{0,1},{1,0},{2,3},{3,2},{4,5},{5,4},{6,7},{7,6},{8,9},{9,8},{10,11... | collective-permute-start | bytes 393224 | tf_op jit(solution)/shard_map/ppermute | solution.py:220
  9.1 0.7 broadcast_select_fusion.6
  9.8 1.1 %constant_dynamic-slice_fusion = bf16[256,1024]{1,0:T(8,128)(2,1)S(1)} fusion(bf16[512,1024]{1,0:T(8,128)(2,1)} %param.18, s32[]{:T(128)S(6)} %select_n.65), kind=kLoop, calls=%fused_computation.61 | loop fusion | bytes 1048580 | tf_op jit(solution)/shard_map/dynamic_slice | solution.py:245
  10.9 0.6 collective-permute-start.13
  11.5 1.2 %collective-permute-done.1 = bf16[64,512]{1,0:T(8,128)(2,1)S(1)} collective-permute-done((bf16[64,512]{1,0:T(8,128)(2,1)}, bf16[64,512]{1,0:T(8,128)(2,1)S(1)}, u32[]{:S(2)}, u32[]{:S(2)}) %collective-permute-start.1) | collective-permute-done | bytes 65568 | tf_op jit(solution)/shard_map/ppermute | solution.py:214
  12.7 0.9 %pad_maximum_fusion.5 = bf16[256,512]{1,0:T(8,128)(2,1)S(1)} fusion(bf16[64,512]{1,0:T(8,128)(2,1)S(1)} %collective-permute-done.2, bf16[64,512]{1,0:T(8,128)(2,1)S(1)} %collective-permute-done.1, bf16[64,512]{1,0:T(8,128)(2,1)S(1)} %collective-permute-done, bf16[64,512]{1,0:T(8,128)(2,1)} %get-tuple-element.16), kind=kLoop, calls=%fused_computation.27 | loop fusion | flops 1048576 | bytes 524288 | tf_op jit(solution)/shard_map/concatenate | solution.py:224
  13.6 1.6 %collective-permute-start.4 = (bf16[128,512]{1,0:T(8,128)(2,1)S(1)}, bf16[128,512]{1,0:T(8,128)(2,1)S(1)}, u32[]{:S(2)}, u32[]{:S(2)}) collective-permute-start(bf16[128,512]{1,0:T(8,128)(2,1)S(1)} %get-tuple-element.34), channel_id=1, source_target_pairs={{0,4},{2,6},{4,0},{6,2},{8,12},{10,14},{12,8},{14,10},{16,20},{18,... | collective-permute-start | bytes 393224 | tf_op jit(solution)/shard_map/ppermute | solution.py:214
  15.1 0.5 collective-permute-start.3
  15.7 0.2 convolution_convert_fusion
  15.9 1.6 %collective-permute-start.7 = (bf16[32,2048]{1,0:T(8,128)(2,1)S(1)}, bf16[32,2048]{1,0:T(8,128)(2,1)S(1)}, u32[]{:S(2)}, u32[]{:S(2)}) collective-permute-start(bf16[32,2048]{1,0:T(8,128)(2,1)S(1)} %convolution_convert_fusion), channel_id=1, source_target_pairs={{0,16},{2,18},{4,20},{6,22},{8,24},{10,26},{12,28},{14,30},{16,0},... | collective-permute-start | bytes 393224 | tf_op jit(solution)/shard_map/ppermute | solution.py:214
  17.5 2.5 %collective-permute-done.4 = bf16[128,512]{1,0:T(8,128)(2,1)S(1)} collective-permute-done((bf16[128,512]{1,0:T(8,128)(2,1)S(1)}, bf16[128,512]{1,0:T(8,128)(2,1)S(1)}, u32[]{:S(2)}, u32[]{:S(2)}) %collective-permute-start.4) | collective-permute-done | bytes 131104 | tf_op jit(solution)/shard_map/ppermute | solution.py:214
  20.0 1.5 %collective-permute-start.10 = (bf16[256,1024]{1,0:T(8,128)(2,1)S(1)}, bf16[256,1024]{1,0:T(8,128)(2,1)}, u32[]{:S(2)}, u32[]{:S(2)}) collective-permute-start(bf16[256,1024]{1,0:T(8,128)(2,1)S(1)} %constant_dynamic-slice_fusion), channel_id=1, source_target_pairs={{0,1},{1,0},{2,3},{3,2},{4,5},{5,4},{6,7},{7,6},{8,9},{9,8},{10,11... | collective-permute-start | bytes 1572872 | tf_op jit(solution)/shard_map/ppermute | solution.py:220
  21.6 0.1 collective-permute-start.5
  21.6 2.5 %collective-permute-done.7 = bf16[32,2048]{1,0:T(8,128)(2,1)S(1)} collective-permute-done((bf16[32,2048]{1,0:T(8,128)(2,1)S(1)}, bf16[32,2048]{1,0:T(8,128)(2,1)S(1)}, u32[]{:S(2)}, u32[]{:S(2)}) %collective-permute-start.7) | collective-permute-done | bytes 131104 | tf_op jit(solution)/shard_map/ppermute | solution.py:214
  24.2 0.1 collective-permute-start.8
  24.3 6.3 %collective-permute-done.8 = bf16[64,2048]{1,0:T(8,128)(2,1)S(1)} collective-permute-done((bf16[64,2048]{1,0:T(8,128)(2,1)S(1)}, bf16[64,2048]{1,0:T(8,128)(2,1)S(1)}, u32[]{:S(2)}, u32[]{:S(2)}) %collective-permute-start.8) | collective-permute-done | bytes 262176 | tf_op jit(solution)/shard_map/ppermute | solution.py:214
  30.7 0.8 %collective-permute-done.10 = bf16[256,1024]{1,0:T(8,128)(2,1)} collective-permute-done((bf16[256,1024]{1,0:T(8,128)(2,1)S(1)}, bf16[256,1024]{1,0:T(8,128)(2,1)}, u32[]{:S(2)}, u32[]{:S(2)}) %collective-permute-start.10) | collective-permute-done | bytes 524320 | tf_op jit(solution)/shard_map/ppermute | solution.py:220
  31.5 1.8 %collective-permute-start.9 = (bf16[128,2048]{1,0:T(8,128)(2,1)S(1)}, bf16[128,2048]{1,0:T(8,128)(2,1)}, u32[]{:S(2)}, u32[]{:S(2)}) collective-permute-start(bf16[128,2048]{1,0:T(8,128)(2,1)S(1)} %pad_maximum_fusion.4), channel_id=1, source_target_pairs={{0,4},{2,10},{4,0},{6,14},{8,12},{10,2},{12,8},{14,6},{16,20},{18,... | collective-permute-start | bytes 1572872 | tf_op jit(solution)/shard_map/ppermute | solution.py:214
  33.4 0.3 fusion.34
  33.7 0.3 fusion.35
  34.0 0.3 fusion.13
  34.2 0.2 fusion.3
  34.5 0.2 fusion.2
  34.8 0.8 broadcast_in_dim.54
  35.5 3.8 %all-to-all-start = ((bf16[16,32,256]{2,1,0:T(8,128)(2,1)}), bf16[16,32,256]{2,1,0:T(8,128)(2,1)S(1)}, u32[]{:S(2)}, u32[]{:S(2)}) async-start(bf16[16,32,256]{2,1,0:T(8,128)(2,1)} %bitcast.3), calls=%async_computation | async-start | bytes 524288 | tf_op jit(solution)/shard_map/all_to_all | solution.py:297
  39.4 0.0 copy-start.1
  39.4 1.5 %collective-permute-done.9 = bf16[128,2048]{1,0:T(8,128)(2,1)} collective-permute-done((bf16[128,2048]{1,0:T(8,128)(2,1)S(1)}, bf16[128,2048]{1,0:T(8,128)(2,1)}, u32[]{:S(2)}, u32[]{:S(2)}) %collective-permute-start.9) | collective-permute-done | bytes 524320 | tf_op jit(solution)/shard_map/ppermute | solution.py:214
  40.8 1.1 %pad_maximum_fusion.1 = bf16[256,2048]{1,0:T(8,128)(2,1)S(1)} fusion(bf16[128,2048]{1,0:T(8,128)(2,1)} %collective-permute-done.9, bf16[64,2048]{1,0:T(8,128)(2,1)S(1)} %collective-permute-done.8, bf16[32,2048]{1,0:T(8,128)(2,1)S(1)} %collective-permute-done.7, bf16[32,2048]{1,0:T(8,128)(2,1)S(1)} %convolution_convert_fusion), kind=kLoop, calls=%fused_computation.10 | loop fusion | flops 4194304 | bytes 2097152 | tf_op jit(solution)/shard_map/concatenate | solution.py:267
  42.0 1.3 %broadcast_select_fusion.3 = (bf16[256,1024]{1,0:T(8,128)(2,1)S(1)}, bf16[256,1024]{1,0:T(8,128)(2,1)S(1)}) fusion(bf16[256,1024]{1,0:T(8,128)(2,1)} %collective-permute-done.10, bf16[256,1024]{1,0:T(8,128)(2,1)} %collective-permute-done.11, pred[]{:T(512)S(6)} %eq.8), kind=kLoop, calls=%fused_computation.18 | loop fusion | flops 524288 | bytes 2097153 | tf_op jit(solution)/shard_map/jit(_where)/select_n | solution.py:210
  43.2 0.6 broadcast_select_fusion.1
  43.8 0.0 copy-start
  43.8 0.2 pad_maximum_fusion.proj_hbm
  44.0 5.9 %all-to-all-done.att = bf16[16,32,256]{2,1,0:T(8,128)(2,1)S(1)} async-done(((bf16[16,32,256]{2,1,0:T(8,128)(2,1)}), bf16[16,32,256]{2,1,0:T(8,128)(2,1)S(1)}, u32[]{:S(2)}, u32[]{:S(2)}) %all-to-all-start) | async-done | bytes 262176 | tf_op jit(solution)/shard_map/all_to_all | solution.py:297
  49.9 6.9 %shard_map.137 = (f32[32,2048]{1,0:T(8,128)S(1)}, f32[64,2048]{1,0:T(8,128)S(1)}, bf16[3,64,2048]{2,1,0:T(8,128)(2,1)S(1)}) custom-call(s32[8]{0:T(128)S(1)} %get-tuple-element.41.att_at, s32[8]{0:T(128)S(1)} %get-tuple-element.40.res_at, bf16[16,32,256]{2,1,0:T(8,128)(2,1)S(1)} %all-to-all-done.att, bf16[8,32,2048]{2,1,0:T(8,128)(2,1)S(1)} %bitcast.17, ...), custom_call_target="tpu_custom_call" | custom-call | flops 3221225472 | bytes 12582912 | tf_op jit(solution)/shard_map/pallas_call | solution.py:166
  56.8 0.1 slice_bitcast_fusion.2
  56.8 1.0 %collective-permute-start.15 = (bf16[64,2048]{1,0:T(8,128)(2,1)S(1)}, bf16[64,2048]{1,0:T(8,128)(2,1)S(1)}, u32[]{:S(2)}, u32[]{:S(2)}) collective-permute-start(bf16[64,2048]{1,0:T(8,128)(2,1)S(1)} %get-tuple-element.29), channel_id=1, source_target_pairs={{0,4},{2,6},{4,0},{6,2},{8,12},{10,14},{12,8},{14,10},{16,20},{18,... | collective-permute-start | bytes 786440 | tf_op jit(solution)/shard_map/ppermute | solution.py:214
  57.8 1.6 %collective-permute-start.17 = (bf16[64,2048]{1,0:T(8,128)(2,1)S(1)}, bf16[64,2048]{1,0:T(8,128)(2,1)S(1)}, u32[]{:S(2)}, u32[]{:S(2)}) collective-permute-start(bf16[64,2048]{1,0:T(8,128)(2,1)S(1)} %get-tuple-element.30), channel_id=1, source_target_pairs={{0,12},{2,14},{4,8},{6,10},{8,4},{10,6},{12,0},{14,2},{16,28},{18,... | collective-permute-start | bytes 786440 | tf_op jit(solution)/shard_map/ppermute | solution.py:214
  59.5 0.9 %collective-permute-start.16 = (bf16[64,2048]{1,0:T(8,128)(2,1)S(1)}, bf16[64,2048]{1,0:T(8,128)(2,1)S(1)}, u32[]{:S(2)}, u32[]{:S(2)}) collective-permute-start(bf16[64,2048]{1,0:T(8,128)(2,1)S(1)} %get-tuple-element.31), channel_id=1, source_target_pairs={{0,8},{2,10},{4,12},{6,14},{8,0},{10,2},{12,4},{14,6},{16,24},{18,... | collective-permute-start | bytes 786440 | tf_op jit(solution)/shard_map/ppermute | solution.py:214
  60.4 9.0 %collective-permute-done.15 = bf16[64,2048]{1,0:T(8,128)(2,1)S(1)} collective-permute-done((bf16[64,2048]{1,0:T(8,128)(2,1)S(1)}, bf16[64,2048]{1,0:T(8,128)(2,1)S(1)}, u32[]{:S(2)}, u32[]{:S(2)}) %collective-permute-start.15) | collective-permute-done | bytes 262176 | tf_op jit(solution)/shard_map/ppermute | solution.py:214
  69.4 1.2 %collective-permute-done.16 = bf16[64,2048]{1,0:T(8,128)(2,1)S(1)} collective-permute-done((bf16[64,2048]{1,0:T(8,128)(2,1)S(1)}, bf16[64,2048]{1,0:T(8,128)(2,1)S(1)}, u32[]{:S(2)}, u32[]{:S(2)}) %collective-permute-start.16) | collective-permute-done | bytes 262176 | tf_op jit(solution)/shard_map/ppermute | solution.py:214
  70.7 0.1 convert_add_fusion
  70.8 1.6 %collective-permute-start.18 = (bf16[32,2048]{1,0:T(8,128)(2,1)S(1)}, bf16[32,2048]{1,0:T(8,128)(2,1)S(1)}, u32[]{:S(2)}, u32[]{:S(2)}) collective-permute-start(bf16[32,2048]{1,0:T(8,128)(2,1)S(1)} %split.27), channel_id=1, source_target_pairs={{0,16},{2,18},{4,20},{6,22},{8,24},{10,26},{12,28},{14,30},{16,0},... | collective-permute-start | bytes 393224 | tf_op jit(solution)/shard_map/ppermute | solution.py:214
  72.4 5.8 %collective-permute-done.18 = bf16[32,2048]{1,0:T(8,128)(2,1)S(1)} collective-permute-done((bf16[32,2048]{1,0:T(8,128)(2,1)S(1)}, bf16[32,2048]{1,0:T(8,128)(2,1)S(1)}, u32[]{:S(2)}, u32[]{:S(2)}) %collective-permute-start.18) | collective-permute-done | bytes 131104 | tf_op jit(solution)/shard_map/ppermute | solution.py:214
  78.2 0.7 fusion.19
  (35 shorter events, 0.3 us)
Async XLA Ops:
  0.0 15.7 %copy-start.2 = (bf16[64,1024]{1,0:T(8,128)(2,1)S(1)}, bf16[64,1024]{1,0:T(8,128)(2,1)}, u32[]{:S(2)}) copy-start(bf16[64,1024]{1,0:T(8,128)(2,1)} %param.14) | copy-start | bytes 393220
  1.7 13.9 %copy-start.5 = (bf16[64,64]{1,0:T(8,128)(2,1)S(1)}, bf16[64,64]{1,0:T(8,128)(2,1)}, u32[]{:S(2)}) copy-start(bf16[64,64]{1,0:T(8,128)(2,1)} %get-tuple-element.18) | copy-start | bytes 24580
  1.7 15.8 %copy-start.4 = (s32[1,1024]{1,0:T(1,128)S(1)}, s32[1,1024]{1,0:T(1,128)}, u32[]{:S(2)}) copy-start(s32[1,1024]{1,0:T(1,128)} %get-tuple-element.14) | copy-start | bytes 12292
  1.7 9.2 %collective-permute-start.2 = (bf16[64,512]{1,0:T(8,128)(2,1)}, bf16[64,512]{1,0:T(8,128)(2,1)S(1)}, u32[]{:S(2)}, u32[]{:S(2)}) collective-permute-start(bf16[64,512]{1,0:T(8,128)(2,1)} %get-tuple-element.16), channel_id=1, source_target_pairs={{0,24},{2,26},{4,28},{6,30},{8,16},{10,18},{12,20},{14,22},{16,8},... | collective-permute-start | bytes 196616 | tf_op jit(solution)/shard_map/ppermute | solution.py:214
  6.9 5.8 %collective-permute-start.1 = (bf16[64,512]{1,0:T(8,128)(2,1)}, bf16[64,512]{1,0:T(8,128)(2,1)S(1)}, u32[]{:S(2)}, u32[]{:S(2)}) collective-permute-start(bf16[64,512]{1,0:T(8,128)(2,1)} %get-tuple-element.16), channel_id=1, source_target_pairs={{0,16},{2,18},{4,20},{6,22},{8,24},{10,26},{12,28},{14,30},{16,0},... | collective-permute-start | bytes 196616 | tf_op jit(solution)/shard_map/ppermute | solution.py:214
  6.9 5.8 %collective-permute-start = (bf16[64,512]{1,0:T(8,128)(2,1)}, bf16[64,512]{1,0:T(8,128)(2,1)S(1)}, u32[]{:S(2)}, u32[]{:S(2)}) collective-permute-start(bf16[64,512]{1,0:T(8,128)(2,1)} %get-tuple-element.16), channel_id=1, source_target_pairs={{0,8},{2,10},{4,12},{6,14},{8,0},{10,2},{12,4},{14,6},{16,24},{18,... | collective-permute-start | bytes 196616 | tf_op jit(solution)/shard_map/ppermute | solution.py:214
  7.5 8.2 %collective-permute-start.6 = (bf16[64,1024]{1,0:T(8,128)(2,1)}, bf16[64,1024]{1,0:T(8,128)(2,1)S(1)}, u32[]{:S(2)}, u32[]{:S(2)}) collective-permute-start(bf16[64,1024]{1,0:T(8,128)(2,1)} %param.14), channel_id=1, source_target_pairs={{0,1},{1,0},{2,3},{3,2},{4,5},{5,4},{6,7},{7,6},{8,9},{9,8},{10,11... | collective-permute-start | bytes 393224 | tf_op jit(solution)/shard_map/ppermute | solution.py:220
  9.1 40.8 %collective-permute-start.12 = (bf16[2048,512]{1,0:T(8,128)(2,1)}, bf16[2048,512]{1,0:T(8,128)(2,1)}, u32[]{:S(2)}, u32[]{:S(2)}) collective-permute-start(bf16[2048,512]{1,0:T(8,128)(2,1)} %bitcast.19), channel_id=1, source_target_pairs={{0,2},{2,0},{4,6},{6,4},{8,10},{10,8},{12,14},{14,12},{16,18},{18,... | collective-permute-start | bytes 6291464 | tf_op jit(solution)/shard_map/ppermute | solution.py:214
  10.9 39.0 %collective-permute-start.13 = (bf16[2048,512]{1,0:T(8,128)(2,1)}, bf16[2048,512]{1,0:T(8,128)(2,1)}, u32[]{:S(2)}, u32[]{:S(2)}) collective-permute-start(bf16[2048,512]{1,0:T(8,128)(2,1)} %bitcast.21), channel_id=1, source_target_pairs={{0,2},{2,0},{4,6},{6,4},{8,10},{10,8},{12,14},{14,12},{16,18},{18,... | collective-permute-start | bytes 6291464 | tf_op jit(solution)/shard_map/ppermute | solution.py:214
  13.6 6.5 %collective-permute-start.4 = (bf16[128,512]{1,0:T(8,128)(2,1)S(1)}, bf16[128,512]{1,0:T(8,128)(2,1)S(1)}, u32[]{:S(2)}, u32[]{:S(2)}) collective-permute-start(bf16[128,512]{1,0:T(8,128)(2,1)S(1)} %get-tuple-element.34), channel_id=1, source_target_pairs={{0,4},{2,6},{4,0},{6,2},{8,12},{10,14},{12,8},{14,10},{16,20},{18,... | collective-permute-start | bytes 393224 | tf_op jit(solution)/shard_map/ppermute | solution.py:214
  15.1 6.4 %collective-permute-start.3 = (bf16[128,512]{1,0:T(8,128)(2,1)S(1)}, bf16[128,512]{1,0:T(8,128)(2,1)S(1)}, u32[]{:S(2)}, u32[]{:S(2)}) collective-permute-start(bf16[128,512]{1,0:T(8,128)(2,1)S(1)} %get-tuple-element.35), channel_id=1, source_target_pairs={{0,4},{2,6},{4,0},{6,2},{8,12},{10,14},{12,8},{14,10},{16,20},{18,... | collective-permute-start | bytes 393224 | tf_op jit(solution)/shard_map/ppermute | solution.py:214
  15.9 8.3 %collective-permute-start.7 = (bf16[32,2048]{1,0:T(8,128)(2,1)S(1)}, bf16[32,2048]{1,0:T(8,128)(2,1)S(1)}, u32[]{:S(2)}, u32[]{:S(2)}) collective-permute-start(bf16[32,2048]{1,0:T(8,128)(2,1)S(1)} %convolution_convert_fusion), channel_id=1, source_target_pairs={{0,16},{2,18},{4,20},{6,22},{8,24},{10,26},{12,28},{14,30},{16,0},... | collective-permute-start | bytes 393224 | tf_op jit(solution)/shard_map/ppermute | solution.py:214
  20.0 11.5 %collective-permute-start.10 = (bf16[256,1024]{1,0:T(8,128)(2,1)S(1)}, bf16[256,1024]{1,0:T(8,128)(2,1)}, u32[]{:S(2)}, u32[]{:S(2)}) collective-permute-start(bf16[256,1024]{1,0:T(8,128)(2,1)S(1)} %constant_dynamic-slice_fusion), channel_id=1, source_target_pairs={{0,1},{1,0},{2,3},{3,2},{4,5},{5,4},{6,7},{7,6},{8,9},{9,8},{10,11... | collective-permute-start | bytes 1572872 | tf_op jit(solution)/shard_map/ppermute | solution.py:220
  21.5 11.8 %copy-start.3 = (bf16[64,256]{1,0:T(8,128)(2,1)S(1)}, bf16[64,256]{1,0:T(8,128)(2,1)}, u32[]{:S(2)}) copy-start(bf16[64,256]{1,0:T(8,128)(2,1)} %get-tuple-element.15) | copy-start | bytes 98308
  21.6 11.8 %collective-permute-start.5 = (bf16[512,512]{1,0:T(8,128)(2,1)S(1)}, bf16[512,512]{1,0:T(8,128)(2,1)S(1)}, u32[]{:S(2)}, u32[]{:S(2)}) collective-permute-start(bf16[512,512]{1,0:T(8,128)(2,1)S(1)} %pad_maximum_fusion.3), channel_id=1, source_target_pairs={{0,2},{2,0},{4,6},{6,4},{8,10},{10,8},{12,14},{14,12},{16,18},{18,... | collective-permute-start | bytes 1572872 | tf_op jit(solution)/shard_map/ppermute | solution.py:214
  24.2 6.4 %collective-permute-start.8 = (bf16[64,2048]{1,0:T(8,128)(2,1)S(1)}, bf16[64,2048]{1,0:T(8,128)(2,1)S(1)}, u32[]{:S(2)}, u32[]{:S(2)}) collective-permute-start(bf16[64,2048]{1,0:T(8,128)(2,1)S(1)} %pad_maximum_fusion.6), channel_id=1, source_target_pairs={{0,8},{2,6},{4,12},{6,2},{8,0},{10,14},{12,4},{14,10},{16,24},{18,... | collective-permute-start | bytes 786440 | tf_op jit(solution)/shard_map/ppermute | solution.py:214
  30.6 19.3 %collective-permute-start.14 = (bf16[512,2048]{1,0:T(8,128)(2,1)}, bf16[512,2048]{1,0:T(8,128)(2,1)}, u32[]{:S(2)}, u32[]{:S(2)}) collective-permute-start(bf16[512,2048]{1,0:T(8,128)(2,1)} %bitcast.8.down0), channel_id=1, source_target_pairs={{0,2},{2,0},{4,6},{6,4},{8,10},{10,8},{12,14},{14,12},{16,18},{18,... | collective-permute-start | bytes 6291464 | tf_op jit(solution)/shard_map/ppermute | solution.py:214
  31.5 9.3 %collective-permute-start.9 = (bf16[128,2048]{1,0:T(8,128)(2,1)S(1)}, bf16[128,2048]{1,0:T(8,128)(2,1)}, u32[]{:S(2)}, u32[]{:S(2)}) collective-permute-start(bf16[128,2048]{1,0:T(8,128)(2,1)S(1)} %pad_maximum_fusion.4), channel_id=1, source_target_pairs={{0,4},{2,10},{4,0},{6,14},{8,12},{10,2},{12,8},{14,6},{16,20},{18,... | collective-permute-start | bytes 1572872 | tf_op jit(solution)/shard_map/ppermute | solution.py:214
  33.3 8.6 %collective-permute-start.11 = (bf16[256,1024]{1,0:T(8,128)(2,1)}, bf16[256,1024]{1,0:T(8,128)(2,1)}, u32[]{:S(2)}, u32[]{:S(2)}) collective-permute-start(bf16[256,1024]{1,0:T(8,128)(2,1)} %collective-permute-done.10), channel_id=1, source_target_pairs={{0,2},{2,0},{4,6},{6,4},{8,10},{10,8},{12,14},{14,12},{16,18},{18,... | collective-permute-start | bytes 1572872 | tf_op jit(solution)/shard_map/ppermute | solution.py:214
  35.5 14.4 %all-to-all-start = ((bf16[16,32,256]{2,1,0:T(8,128)(2,1)}), bf16[16,32,256]{2,1,0:T(8,128)(2,1)S(1)}, u32[]{:S(2)}, u32[]{:S(2)}) async-start(bf16[16,32,256]{2,1,0:T(8,128)(2,1)} %bitcast.3), calls=%async_computation | async-start | bytes 524288 | tf_op jit(solution)/shard_map/all_to_all | solution.py:297
  39.4 3.9 %copy-start.1 = (bf16[512,1024]{1,0:T(8,128)(2,1)S(1)}, bf16[512,1024]{1,0:T(8,128)(2,1)}, u32[]{:S(2)}) copy-start(bf16[512,1024]{1,0:T(8,128)(2,1)} %param.18) | copy-start | bytes 3145732
  43.8 6.1 %copy-start = (f32[2048]{0:T(1024)S(1)}, f32[2048]{0:T(1024)}, u32[]{:S(2)}) copy-start(f32[2048]{0:T(1024)} %param.19) | copy-start | bytes 24580
  56.8 12.6 %collective-permute-start.15 = (bf16[64,2048]{1,0:T(8,128)(2,1)S(1)}, bf16[64,2048]{1,0:T(8,128)(2,1)S(1)}, u32[]{:S(2)}, u32[]{:S(2)}) collective-permute-start(bf16[64,2048]{1,0:T(8,128)(2,1)S(1)} %get-tuple-element.29), channel_id=1, source_target_pairs={{0,4},{2,6},{4,0},{6,2},{8,12},{10,14},{12,8},{14,10},{16,20},{18,... | collective-permute-start | bytes 786440 | tf_op jit(solution)/shard_map/ppermute | solution.py:214
  57.8 11.6 %collective-permute-start.17 = (bf16[64,2048]{1,0:T(8,128)(2,1)S(1)}, bf16[64,2048]{1,0:T(8,128)(2,1)S(1)}, u32[]{:S(2)}, u32[]{:S(2)}) collective-permute-start(bf16[64,2048]{1,0:T(8,128)(2,1)S(1)} %get-tuple-element.30), channel_id=1, source_target_pairs={{0,12},{2,14},{4,8},{6,10},{8,4},{10,6},{12,0},{14,2},{16,28},{18,... | collective-permute-start | bytes 786440 | tf_op jit(solution)/shard_map/ppermute | solution.py:214
  59.5 11.2 %collective-permute-start.16 = (bf16[64,2048]{1,0:T(8,128)(2,1)S(1)}, bf16[64,2048]{1,0:T(8,128)(2,1)S(1)}, u32[]{:S(2)}, u32[]{:S(2)}) collective-permute-start(bf16[64,2048]{1,0:T(8,128)(2,1)S(1)} %get-tuple-element.31), channel_id=1, source_target_pairs={{0,8},{2,10},{4,12},{6,14},{8,0},{10,2},{12,4},{14,6},{16,24},{18,... | collective-permute-start | bytes 786440 | tf_op jit(solution)/shard_map/ppermute | solution.py:214
  70.8 7.3 %collective-permute-start.18 = (bf16[32,2048]{1,0:T(8,128)(2,1)S(1)}, bf16[32,2048]{1,0:T(8,128)(2,1)S(1)}, u32[]{:S(2)}, u32[]{:S(2)}) collective-permute-start(bf16[32,2048]{1,0:T(8,128)(2,1)S(1)} %split.27), channel_id=1, source_target_pairs={{0,16},{2,18},{4,20},{6,22},{8,24},{10,26},{12,28},{14,30},{16,0},... | collective-permute-start | bytes 393224 | tf_op jit(solution)/shard_map/ppermute | solution.py:214

commit v3 on v2

--- a/solution.py
+++ b/solution.py
@@ -224,14 +224,17 @@
             x = jnp.concatenate([x] + [move(x, d) for d in distances(bits)[1:]], axis=0)
         return x
 
-    def scatter(keep, send):
-        for k, stage in enumerate(sum_stages):
-            if k:
-                pieces = jnp.split(keep, 1 << len(stage), axis=0)
-                keep, send = pieces[0], [piece.astype(BF) for piece in pieces[1:]]
-            for piece, distance in zip(send, distances(stage)[1:]):
-                keep = keep + move(piece, distance).astype(F32)
-        return keep
+    def scatter(keep, send, stages):
+        parts = 1 << len(stages[1]) if len(stages) > 1 else 1
+        sums = []
+        for part in reversed(range(parts)):
+            total = jnp.split(keep, parts, axis=0)[part]
+            for piece, distance in reversed(list(zip(send, distances(stages[0])[1:]))):
+                total = total + move(jnp.split(piece, parts, axis=0)[part], distance).astype(F32)
+            sums.insert(0, total)
+        if parts == 1:
+            return sums[0]
+        return scatter(sums[0], [total.astype(BF) for total in sums[1:]], stages[1:])
 
     kv_order = gathered(kv_stages)
     width = keys.shape[1]
@@ -240,17 +243,17 @@
         me, block_mask, keys, values, queries, routes, experts, kv_order + [o ^ 1 for o in kv_order]
     )
     allowed = allowed > 0
-    all_kv = gather(all_kv, kv_stages[:1])
     rows = out_proj.shape[0] // 2
     proj_go = lax.dynamic_slice_in_dim(out_proj, core * rows, rows, axis=0)
-    all_kv, proj_go = lax.optimization_barrier((all_kv, proj_go))
+    all_kv = gather(all_kv, kv_stages[:1])
+    if experts == 2:
+        all_kv, res_come = lax.optimization_barrier((all_kv, swap_exp(residual)))
     all_kv = gather(all_kv, kv_stages[1:-1])
     last = [move(x, d) for d in distances(kv_stages[-1])[1:] for x in jnp.split(all_kv, 2, axis=0)]
     all_kv = jnp.concatenate([all_kv] + last, axis=0)
     far_kv = swap_core(all_kv)
 
     near_w = (w_gate[0], w_up[0], w_down[0])
-    far_w = tuple(swap_core(w) for w in near_w)
     direct = experts == 2 and per % 32 == 0
     if direct:
         first = exp_me == 0
@@ -261,14 +264,10 @@
             )
 
         own_rows = lax.dynamic_slice_in_dim(placing, exp_me * per, per, axis=0)
-        res_both = both_halves(residual, swap_exp(residual))
+        res_both = both_halves(residual, res_come)
         res_all = dot(own_rows, res_both).astype(BF)
-        for masks in res_masks:
-            res_all = jnp.concatenate([res_all, move(res_all, *masks)], axis=0)
+        res_all = jnp.concatenate([res_all, move(res_all, *res_masks[0])], axis=0)
         proj_near = swap_exp(proj_go)
-        proj_far = swap_core(proj_near)
-        proj_come = jnp.concatenate([by_core(proj_near, proj_far), by_core(proj_far, proj_near)], axis=0)
-        proj_all = both_halves(out_proj, proj_come)
     else:
         res_rows = dot(placing, residual).astype(BF)
         res_all = lax.all_to_all(
@@ -292,8 +291,16 @@
     att = jnp.concatenate(parts, axis=1).reshape(experts, per, width)
 
     if direct:
+        att, res_all = lax.optimization_barrier((att, res_all))
+        go = jnp.broadcast_to(att[None], (n // 2, experts, per, width)).reshape(-1, per, width)
+        go, go_w, proj_near = lax.optimization_barrier((go, near_w, proj_near))
+        proj_far = swap_core(proj_near)
+        proj_come = jnp.concatenate([by_core(proj_near, proj_far), by_core(proj_far, proj_near)], axis=0)
+        proj_all = both_halves(out_proj, proj_come)
+        far_w = tuple(swap_core(w) for w in go_w)
+        for masks in res_masks[1:]:
+            res_all = jnp.concatenate([res_all, move(res_all, *masks)], axis=0)
         groups = [[(2 * k + c) * experts + e for k in range(n // 2) for e in range(experts)] for c in (0, 1)]
-        go = jnp.broadcast_to(att[None], (n // 2, experts, per, width)).reshape(-1, per, width)
         att_all = lax.all_to_all(
             go, ("ctx", "exp"), split_axis=0, concat_axis=0, axis_index_groups=groups, tiled=True
         )
@@ -304,17 +311,18 @@
             (me ^ jnp.array(order, jnp.int32)) >> 1, res_at, att_all,
             res_all.reshape(n // 2, per, -1), proj_all, norm_gain, near_w, far_w,
         )
-        summed = scatter(keep, [send[k] for k in range(3)])
+        summed = scatter(keep, [send[k] for k in range(3)], sum_stages)
     else:
         att_all = lax.all_to_all(att, "exp", split_axis=0, concat_axis=2, tiled=True)[0]
         hidden = (res_all.astype(F32) + dot(att_all, proj_all)).astype(BF).astype(F32)
         meansq = jnp.mean(hidden * hidden, axis=1, keepdims=True)
         normed = (hidden * lax.rsqrt(meansq + 1e-05) * norm_gain).astype(BF)
         order = scattered(sum_stages)
+        far_w = tuple(swap_core(w) for w in near_w)
         found = gather(normed, sum_stages).reshape(n // 2, per, -1)
         found = jnp.stack([found[gathered(sum_stages).index(o)] for o in order]).reshape(n // 2 * per, -1)
         pieces = jnp.split(expert_rows(found, near_w, far_w), 4, axis=0)
-        summed = scatter(pieces[0], [piece.astype(BF) for piece in pieces[1:]])
+        summed = scatter(pieces[0], [piece.astype(BF) for piece in pieces[1:]], sum_stages)
     return (hidden + summed).astype(BF)[None]
 
 

time: 79.3 us -> 72.3 us (0.912)
  waiting for transfers between devices: 36.8 us -> 24.6 us
  starting transfers between devices: 24 us -> 31.5 us
  other arithmetic: 5.92 us -> 3.59 us
    ppermute x17 -> x20, starting transfers between devices: 17.1 us -> 23.9 us  [move(): return lax.ppermute(x, 'ctx', [(i, i ^ masks[i & 1]) for i in range(n)])]
    all_to_all x1, waiting for transfers between devices: 5.87 us -> 0.01 us  [body(): lax.all_to_all(go, ('ctx', 'exp'), split_axis=0, concat_axis=0, axis_inde...]
    ppermute x17 -> x20, waiting for transfers between devices: 30.1 us -> 24.4 us  [move(): return lax.ppermute(x, 'ctx', [(i, i ^ masks[i & 1]) for i in range(n)])]
    select_n x2, other arithmetic: 1.95 us -> 0.08 us  [by_core(): return jnp.where(core == 0, even, odd)]
    all_to_all x1, starting transfers between devices: 3.81 us -> 5.59 us  [body(): lax.all_to_all(go, ('ctx', 'exp'), split_axis=0, concat_axis=0, axis_inde...]
    concatenate x3 -> x2, other arithmetic: 1.18 us -> 0.1 us  [body(): res_all = jnp.concatenate([res_all, move(res_all, *masks)], axis=0)]
    ppermute x2, starting transfers between devices: 3.1 us -> 2.09 us  [swap_exp(): return lax.ppermute(x, 'exp', [(0, 1), (1, 0)])]
  transfers between devices with their start and end apart: 20 -> 23, of which waited for: 10 -> 11; matrix products, arithmetic and copies ran while one was open for 11% -> 7% of each run, Pallas kernels for 0% -> 0%
where the time goes in v3:
time: 72.3 us; the launch traced here: 71.9 us
  starting transfers between devices  31.5 us (44%)
  waiting for transfers between devices  24.6 us (34%)
  Pallas kernels  8.59 us (12%)
  other arithmetic  3.59 us (5%)
  local copies, waits for them, and re-layouts  2.01 us (3%)
  matrix products  1.28 us (2%)
    ppermute x20, waiting for transfers between devices, move(): return lax.ppermute(x, 'ctx', [(i, i ^ masks[i & 1]) for i in range(n)])  24.4 us
    ppermute x20, starting transfers between devices, move(): return lax.ppermute(x, 'ctx', [(i, i ^ masks[i & 1]) for i in range(n)])  23.9 us
    pallas_call x1, Pallas kernels, expert(): pl.pallas_call(expert_kernel, out_shape=(jax.ShapeDtypeStruct((per, feats...  6.85 us
    all_to_all x1, starting transfers between devices, body(): lax.all_to_all(go, ('ctx', 'exp'), split_axis=0, concat_axis=0, axis_inde...  5.59 us
    ppermute x2, starting transfers between devices, swap_exp(): return lax.ppermute(x, 'exp', [(0, 1), (1, 0)])  2.09 us
    pallas_call x1, Pallas kernels, prepare(): pl.pallas_call(functools.partial(prepare_kernel, far=dict(experts=experts...  1.74 us
  transfers between devices with their start and end apart: 23, of which 11 were waited for; matrix products, arithmetic and copies ran while one was open for 7% of the time, Pallas kernels for 0%

profile of v3, /device:TPU:0, one launch (start us, length us, event | category | flops | bytes accessed | tf_op | source)
XLA Modules:
  0.0 71.9 jit_solution(16194165176324706063)
XLA Ops:
  0.0 1.7 %shard_map.136 = (bf16[64,512]{1,0:T(8,128)(2,1)}, bf16[64,256]{1,0:T(8,128)(2,1)}, bf16[64,64]{1,0:T(8,128)(2,1)}, s32[1,1024]{1,0:T(1,128)}) custom-call(s32[1]{0:T(128)} %bitcast.me, s32[8,8]{1,0:T(8,128)} %mask.1, bf16[64,256]{1,0:T(8,128)(2,1)} %keys.1, bf16[64,256]{1,0:T(8,128)(2,1)} %values.1, bf16[64,256]{1,0:T(8,128)(2,1)} %queries.1, s32[1,64]{1,0:T(1,128)} %bitcast.26), custom_call_target="tpu_custom_call" | custom-call | tf_op jit(solution)/shard_map/pallas_call | solution.py:72
  1.7 5.0 %collective-permute-start.2 = (bf16[64,512]{1,0:T(8,128)(2,1)}, bf16[64,512]{1,0:T(8,128)(2,1)S(1)}, u32[]{:S(2)}, u32[]{:S(2)}) collective-permute-start(bf16[64,512]{1,0:T(8,128)(2,1)} %get-tuple-element.23), channel_id=1, source_target_pairs={{0,24},{2,26},{4,28},{6,30},{8,16},{10,18},{12,20},{14,22},{16,8},... | collective-permute-start | bytes 196616 | tf_op jit(solution)/shard_map/ppermute | solution.py:214
  6.8 0.6 collective-permute-start
  7.4 1.6 %collective-permute-start.3 = (bf16[64,1024]{1,0:T(8,128)(2,1)}, bf16[64,1024]{1,0:T(8,128)(2,1)S(1)}, u32[]{:S(2)}, u32[]{:S(2)}) collective-permute-start(bf16[64,1024]{1,0:T(8,128)(2,1)} %param.14), channel_id=1, source_target_pairs={{0,1},{1,0},{2,3},{3,2},{4,5},{5,4},{6,7},{7,6},{8,9},{9,8},{10,11... | collective-permute-start | bytes 393224 | tf_op jit(solution)/shard_map/ppermute | solution.py:220
  9.1 1.1 %constant_dynamic-slice_fusion = bf16[256,1024]{1,0:T(8,128)(2,1)S(1)} fusion(bf16[512,1024]{1,0:T(8,128)(2,1)} %param.18, s32[]{:T(128)S(6)} %select_n.73), kind=kLoop, calls=%fused_computation.60 | loop fusion | bytes 1048580 | tf_op jit(solution)/shard_map/dynamic_slice | solution.py:247
  10.2 0.4 collective-permute-start.8
  10.6 0.7 compare_reduce_fusion
  11.3 1.3 %collective-permute-done.1 = bf16[64,512]{1,0:T(8,128)(2,1)S(1)} collective-permute-done((bf16[64,512]{1,0:T(8,128)(2,1)}, bf16[64,512]{1,0:T(8,128)(2,1)S(1)}, u32[]{:S(2)}, u32[]{:S(2)}) %collective-permute-start.1) | collective-permute-done | bytes 65568 | tf_op jit(solution)/shard_map/ppermute | solution.py:214
  12.6 0.9 %pad_maximum_fusion.5 = bf16[256,512]{1,0:T(8,128)(2,1)S(1)} fusion(bf16[64,512]{1,0:T(8,128)(2,1)S(1)} %collective-permute-done.2, bf16[64,512]{1,0:T(8,128)(2,1)S(1)} %collective-permute-done.1, bf16[64,512]{1,0:T(8,128)(2,1)S(1)} %collective-permute-done, bf16[64,512]{1,0:T(8,128)(2,1)} %get-tuple-element.23), kind=kLoop, calls=%fused_computation.22 | loop fusion | flops 1048576 | bytes 524288 | tf_op jit(solution)/shard_map/concatenate | solution.py:224
  13.5 0.2 collective-permute-done.3
  13.7 1.8 %collective-permute-start.5 = (bf16[128,512]{1,0:T(8,128)(2,1)S(1)}, bf16[128,512]{1,0:T(8,128)(2,1)S(1)}, u32[]{:S(2)}, u32[]{:S(2)}) collective-permute-start(bf16[128,512]{1,0:T(8,128)(2,1)S(1)} %get-tuple-element.51), channel_id=1, source_target_pairs={{0,4},{2,6},{4,0},{6,2},{8,12},{10,14},{12,8},{14,10},{16,20},{18,... | collective-permute-start | bytes 393224 | tf_op jit(solution)/shard_map/ppermute | solution.py:214
  15.5 0.3 collective-permute-start.4
  15.8 0.2 convolution_convert_fusion
  16.0 2.4 %collective-permute-start.7 = (bf16[32,2048]{1,0:T(8,128)(2,1)S(1)}, bf16[32,2048]{1,0:T(8,128)(2,1)S(1)}, u32[]{:S(2)}, u32[]{:S(2)}) collective-permute-start(bf16[32,2048]{1,0:T(8,128)(2,1)S(1)} %convolution_convert_fusion), channel_id=1, source_target_pairs={{0,16},{2,18},{4,20},{6,22},{8,24},{10,26},{12,28},{14,30},{16,0},... | collective-permute-start | bytes 393224 | tf_op jit(solution)/shard_map/ppermute | solution.py:214
  18.3 1.7 %collective-permute-done.5 = bf16[128,512]{1,0:T(8,128)(2,1)S(1)} collective-permute-done((bf16[128,512]{1,0:T(8,128)(2,1)S(1)}, bf16[128,512]{1,0:T(8,128)(2,1)S(1)}, u32[]{:S(2)}, u32[]{:S(2)}) %collective-permute-start.5) | collective-permute-done | bytes 131104 | tf_op jit(solution)/shard_map/ppermute | solution.py:214
  20.1 1.4 %collective-permute-done.4 = bf16[128,512]{1,0:T(8,128)(2,1)S(1)} collective-permute-done((bf16[128,512]{1,0:T(8,128)(2,1)S(1)}, bf16[128,512]{1,0:T(8,128)(2,1)S(1)}, u32[]{:S(2)}, u32[]{:S(2)}) %collective-permute-start.4) | collective-permute-done | bytes 131104 | tf_op jit(solution)/shard_map/ppermute | solution.py:214
  21.5 0.1 collective-permute-start.6
  21.7 2.0 %collective-permute-done.7 = bf16[32,2048]{1,0:T(8,128)(2,1)S(1)} collective-permute-done((bf16[32,2048]{1,0:T(8,128)(2,1)S(1)}, bf16[32,2048]{1,0:T(8,128)(2,1)S(1)}, u32[]{:S(2)}, u32[]{:S(2)}) %collective-permute-start.7) | collective-permute-done | bytes 131104 | tf_op jit(solution)/shard_map/ppermute | solution.py:214
  23.8 0.3 fusion.32
  24.1 0.3 fusion.33
  24.4 0.3 fusion.11
  24.7 0.2 fusion.3
  24.9 0.2 fusion.2
  25.2 0.7 %broadcast_in_dim.52 = bf16[8,2,32,256]{3,2,1,0:T(8,128)(2,1)} broadcast(bf16[2,32,256]{2,1,0:T(8,128)(2,1)S(1)} %bitcast.25), dimensions={1,2,3} | broadcast | bytes 294912 | tf_op jit(solution)/shard_map/broadcast_in_dim | solution.py:295
  26.0 0.5 collective-permute-start.13
  26.5 1.7 %collective-permute-start.11 = (bf16[256,1024]{1,0:T(8,128)(2,1)S(1)}, bf16[256,1024]{1,0:T(8,128)(2,1)S(1)}, u32[]{:S(2)}, u32[]{:S(2)}) collective-permute-start(bf16[256,1024]{1,0:T(8,128)(2,1)S(1)} %collective-permute-done.8), channel_id=1, source_target_pairs={{0,2},{2,0},{4,6},{6,4},{8,10},{10,8},{12,14},{14,12},{16,18},{18,... | collective-permute-start | bytes 1572872 | tf_op jit(solution)/shard_map/ppermute | solution.py:214
  28.2 5.6 %all-to-all-start = ((bf16[16,32,256]{2,1,0:T(8,128)(2,1)}), bf16[16,32,256]{2,1,0:T(8,128)(2,1)S(1)}, u32[]{:S(2)}, u32[]{:S(2)}) async-start(bf16[16,32,256]{2,1,0:T(8,128)(2,1)} %bitcast.3), calls=%async_computation | async-start | bytes 524288 | tf_op jit(solution)/shard_map/all_to_all | solution.py:304
  33.9 2.0 %collective-permute-start.10 = (bf16[128,2048]{1,0:T(8,128)(2,1)S(1)}, bf16[128,2048]{1,0:T(8,128)(2,1)S(1)}, u32[]{:S(2)}, u32[]{:S(2)}) collective-permute-start(bf16[128,2048]{1,0:T(8,128)(2,1)S(1)} %pad_maximum_fusion.4), channel_id=1, source_target_pairs={{0,4},{2,10},{4,0},{6,14},{8,12},{10,2},{12,8},{14,6},{16,20},{18,... | collective-permute-start | bytes 1572872 | tf_op jit(solution)/shard_map/ppermute | solution.py:214
  35.9 0.1 broadcast_select_fusion.3
  36.0 0.5 broadcast_select_fusion.1
  36.5 0.2 pad_maximum_fusion.proj_hbm
  36.7 9.0 %collective-permute-done.10 = bf16[128,2048]{1,0:T(8,128)(2,1)S(1)} collective-permute-done((bf16[128,2048]{1,0:T(8,128)(2,1)S(1)}, bf16[128,2048]{1,0:T(8,128)(2,1)S(1)}, u32[]{:S(2)}, u32[]{:S(2)}) %collective-permute-start.10) | collective-permute-done | bytes 524320 | tf_op jit(solution)/shard_map/ppermute | solution.py:214
  45.7 0.1 pad_maximum_fusion.1
  45.8 6.8 %shard_map.137 = (f32[32,2048]{1,0:T(8,128)S(1)}, f32[64,2048]{1,0:T(8,128)S(1)}, bf16[3,64,2048]{2,1,0:T(8,128)(2,1)S(1)}) custom-call(s32[8]{0:T(128)S(1)} %xor_shift-right-arithmetic_fusion.att_at, s32[8]{0:T(128)S(1)} %broadcast_select_fusion.6.res_at, bf16[16,32,256]{2,1,0:T(8,128)(2,1)S(1)} %all-to-all-done.att, bf16[8,32,2048]{2,1,0:T(8,128)(2,1)S(1)} %bitcast.23, ...), custom_call_target="tpu_custom_call" | custom-call | flops 3221225472 | bytes 12582912 | tf_op jit(solution)/shard_map/pallas_call | solution.py:166
  52.7 1.2 %collective-permute-start.20 = (bf16[32,2048]{1,0:T(8,128)(2,1)S(1)}, bf16[32,2048]{1,0:T(8,128)(2,1)S(1)}, u32[]{:S(2)}, u32[]{:S(2)}) collective-permute-start(bf16[32,2048]{1,0:T(8,128)(2,1)S(1)} %get-tuple-element.44), channel_id=1, source_target_pairs={{0,4},{2,6},{4,0},{6,2},{8,12},{10,14},{12,8},{14,10},{16,20},{18,... | collective-permute-start | bytes 393224 | tf_op jit(solution)/shard_map/ppermute | solution.py:214
  54.0 1.3 %collective-permute-start.19 = (bf16[32,2048]{1,0:T(8,128)(2,1)S(1)}, bf16[32,2048]{1,0:T(8,128)(2,1)S(1)}, u32[]{:S(2)}, u32[]{:S(2)}) collective-permute-start(bf16[32,2048]{1,0:T(8,128)(2,1)S(1)} %get-tuple-element.45), channel_id=1, source_target_pairs={{0,8},{2,10},{4,12},{6,14},{8,0},{10,2},{12,4},{14,6},{16,24},{18,... | collective-permute-start | bytes 393224 | tf_op jit(solution)/shard_map/ppermute | solution.py:214
  55.2 1.0 %collective-permute-start.18 = (bf16[32,2048]{1,0:T(8,128)(2,1)S(1)}, bf16[32,2048]{1,0:T(8,128)(2,1)S(1)}, u32[]{:S(2)}, u32[]{:S(2)}) collective-permute-start(bf16[32,2048]{1,0:T(8,128)(2,1)S(1)} %get-tuple-element.46), channel_id=1, source_target_pairs={{0,12},{2,14},{4,8},{6,10},{8,4},{10,6},{12,0},{14,2},{16,28},{18,... | collective-permute-start | bytes 393224 | tf_op jit(solution)/shard_map/ppermute | solution.py:214
  56.3 1.9 %collective-permute-start.15 = (bf16[32,2048]{1,0:T(8,128)(2,1)S(1)}, bf16[32,2048]{1,0:T(8,128)(2,1)S(1)}, u32[]{:S(2)}, u32[]{:S(2)}) collective-permute-start(bf16[32,2048]{1,0:T(8,128)(2,1)S(1)} %get-tuple-element.43), channel_id=1, source_target_pairs={{0,12},{2,14},{4,8},{6,10},{8,4},{10,6},{12,0},{14,2},{16,28},{18,... | collective-permute-start | bytes 393224 | tf_op jit(solution)/shard_map/ppermute | solution.py:214
  58.2 1.1 %collective-permute-start.17 = (bf16[32,2048]{1,0:T(8,128)(2,1)S(1)}, bf16[32,2048]{1,0:T(8,128)(2,1)S(1)}, u32[]{:S(2)}, u32[]{:S(2)}) collective-permute-start(bf16[32,2048]{1,0:T(8,128)(2,1)S(1)} %get-tuple-element.47), channel_id=1, source_target_pairs={{0,4},{2,6},{4,0},{6,2},{8,12},{10,14},{12,8},{14,10},{16,20},{18,... | collective-permute-start | bytes 393224 | tf_op jit(solution)/shard_map/ppermute | solution.py:214
  59.3 0.5 collective-permute-start.16
  59.8 0.5 collective-permute-done.19
  60.2 3.3 %collective-permute-done.18 = bf16[32,2048]{1,0:T(8,128)(2,1)S(1)} collective-permute-done((bf16[32,2048]{1,0:T(8,128)(2,1)S(1)}, bf16[32,2048]{1,0:T(8,128)(2,1)S(1)}, u32[]{:S(2)}, u32[]{:S(2)}) %collective-permute-start.18) | collective-permute-done | bytes 131104 | tf_op jit(solution)/shard_map/ppermute | solution.py:214
  63.5 0.1 add_convert_fusion.1
  63.6 2.4 %collective-permute-start.21 = (bf16[32,2048]{1,0:T(8,128)(2,1)S(1)}, bf16[32,2048]{1,0:T(8,128)(2,1)S(1)}, u32[]{:S(2)}, u32[]{:S(2)}) collective-permute-start(bf16[32,2048]{1,0:T(8,128)(2,1)S(1)} %add_convert_fusion.1), channel_id=1, source_target_pairs={{0,16},{2,18},{4,20},{6,22},{8,24},{10,26},{12,28},{14,30},{16,0},... | collective-permute-start | bytes 393224 | tf_op jit(solution)/shard_map/ppermute | solution.py:214
  66.0 0.3 collective-permute-done.15
  66.3 1.6 %collective-permute-done.17 = bf16[32,2048]{1,0:T(8,128)(2,1)S(1)} collective-permute-done((bf16[32,2048]{1,0:T(8,128)(2,1)S(1)}, bf16[32,2048]{1,0:T(8,128)(2,1)S(1)}, u32[]{:S(2)}, u32[]{:S(2)}) %collective-permute-start.17) | collective-permute-done | bytes 131104 | tf_op jit(solution)/shard_map/ppermute | solution.py:214
  67.9 3.3 %collective-permute-done.16 = bf16[32,2048]{1,0:T(8,128)(2,1)S(1)} collective-permute-done((bf16[32,2048]{1,0:T(8,128)(2,1)S(1)}, bf16[32,2048]{1,0:T(8,128)(2,1)S(1)}, u32[]{:S(2)}, u32[]{:S(2)}) %collective-permute-start.16) | collective-permute-done | bytes 131104 | tf_op jit(solution)/shard_map/ppermute | solution.py:214
  71.2 0.8 %fusion.17 = bf16[1,32,2048]{2,1,0:T(8,128)(2,1)} fusion(f32[32,2048]{1,0:T(8,128)S(1)} %get-tuple-element.34, bf16[32,2048]{1,0:T(8,128)(2,1)S(1)} %collective-permute-done.21, bf16[32,2048]{1,0:T(8,128)(2,1)S(1)} %collective-permute-done.17, bf16[32,2048]{1,0:T(8,128)(2,1)S(1)} %collective-permute-done.16, ...), kind=kLoop, calls=%fused_computation.35 | loop fusion | flops 655360 | bytes 1179648 | tf_op jit(solution)/shard_map/broadcast_in_dim | solution.py:326
  (51 shorter events, 0.4 us)
Async XLA Ops:
  0.0 15.8 %copy-start.6 = (bf16[64,1024]{1,0:T(8,128)(2,1)S(1)}, bf16[64,1024]{1,0:T(8,128)(2,1)}, u32[]{:S(2)}) copy-start(bf16[64,1024]{1,0:T(8,128)(2,1)} %param.14) | copy-start | bytes 393220
  1.7 14.1 %copy-start.8 = (bf16[64,64]{1,0:T(8,128)(2,1)S(1)}, bf16[64,64]{1,0:T(8,128)(2,1)}, u32[]{:S(2)}) copy-start(bf16[64,64]{1,0:T(8,128)(2,1)} %get-tuple-element.25) | copy-start | bytes 24580
  1.7 9.6 %collective-permute-start.2 = (bf16[64,512]{1,0:T(8,128)(2,1)}, bf16[64,512]{1,0:T(8,128)(2,1)S(1)}, u32[]{:S(2)}, u32[]{:S(2)}) collective-permute-start(bf16[64,512]{1,0:T(8,128)(2,1)} %get-tuple-element.23), channel_id=1, source_target_pairs={{0,24},{2,26},{4,28},{6,30},{8,16},{10,18},{12,20},{14,22},{16,8},... | collective-permute-start | bytes 196616 | tf_op jit(solution)/shard_map/ppermute | solution.py:214
  6.8 5.8 %collective-permute-start.1 = (bf16[64,512]{1,0:T(8,128)(2,1)}, bf16[64,512]{1,0:T(8,128)(2,1)S(1)}, u32[]{:S(2)}, u32[]{:S(2)}) collective-permute-start(bf16[64,512]{1,0:T(8,128)(2,1)} %get-tuple-element.23), channel_id=1, source_target_pairs={{0,16},{2,18},{4,20},{6,22},{8,24},{10,26},{12,28},{14,30},{16,0},... | collective-permute-start | bytes 196616 | tf_op jit(solution)/shard_map/ppermute | solution.py:214
  6.8 5.8 %collective-permute-start = (bf16[64,512]{1,0:T(8,128)(2,1)}, bf16[64,512]{1,0:T(8,128)(2,1)S(1)}, u32[]{:S(2)}, u32[]{:S(2)}) collective-permute-start(bf16[64,512]{1,0:T(8,128)(2,1)} %get-tuple-element.23), channel_id=1, source_target_pairs={{0,8},{2,10},{4,12},{6,14},{8,0},{10,2},{12,4},{14,6},{16,24},{18,... | collective-permute-start | bytes 196616 | tf_op jit(solution)/shard_map/ppermute | solution.py:214
  7.4 6.2 %collective-permute-start.3 = (bf16[64,1024]{1,0:T(8,128)(2,1)}, bf16[64,1024]{1,0:T(8,128)(2,1)S(1)}, u32[]{:S(2)}, u32[]{:S(2)}) collective-permute-start(bf16[64,1024]{1,0:T(8,128)(2,1)} %param.14), channel_id=1, source_target_pairs={{0,1},{1,0},{2,3},{3,2},{4,5},{5,4},{6,7},{7,6},{8,9},{9,8},{10,11... | collective-permute-start | bytes 393224 | tf_op jit(solution)/shard_map/ppermute | solution.py:220
  10.2 15.1 %collective-permute-start.8 = (bf16[256,1024]{1,0:T(8,128)(2,1)S(1)}, bf16[256,1024]{1,0:T(8,128)(2,1)S(1)}, u32[]{:S(2)}, u32[]{:S(2)}) collective-permute-start(bf16[256,1024]{1,0:T(8,128)(2,1)S(1)} %constant_dynamic-slice_fusion), channel_id=1, source_target_pairs={{0,1},{1,0},{2,3},{3,2},{4,5},{5,4},{6,7},{7,6},{8,9},{9,8},{10,11... | collective-permute-start | bytes 1572872 | tf_op jit(solution)/shard_map/ppermute | solution.py:220
  13.7 6.4 %collective-permute-start.5 = (bf16[128,512]{1,0:T(8,128)(2,1)S(1)}, bf16[128,512]{1,0:T(8,128)(2,1)S(1)}, u32[]{:S(2)}, u32[]{:S(2)}) collective-permute-start(bf16[128,512]{1,0:T(8,128)(2,1)S(1)} %get-tuple-element.51), channel_id=1, source_target_pairs={{0,4},{2,6},{4,0},{6,2},{8,12},{10,14},{12,8},{14,10},{16,20},{18,... | collective-permute-start | bytes 393224 | tf_op jit(solution)/shard_map/ppermute | solution.py:214
  15.5 6.0 %collective-permute-start.4 = (bf16[128,512]{1,0:T(8,128)(2,1)S(1)}, bf16[128,512]{1,0:T(8,128)(2,1)S(1)}, u32[]{:S(2)}, u32[]{:S(2)}) collective-permute-start(bf16[128,512]{1,0:T(8,128)(2,1)S(1)} %get-tuple-element.52), channel_id=1, source_target_pairs={{0,4},{2,6},{4,0},{6,2},{8,12},{10,14},{12,8},{14,10},{16,20},{18,... | collective-permute-start | bytes 393224 | tf_op jit(solution)/shard_map/ppermute | solution.py:214
  15.8 8.0 %copy-start.7 = (bf16[64,256]{1,0:T(8,128)(2,1)S(1)}, bf16[64,256]{1,0:T(8,128)(2,1)}, u32[]{:S(2)}) copy-start(bf16[64,256]{1,0:T(8,128)(2,1)} %get-tuple-element.22) | copy-start | bytes 98308
  16.0 7.7 %collective-permute-start.7 = (bf16[32,2048]{1,0:T(8,128)(2,1)S(1)}, bf16[32,2048]{1,0:T(8,128)(2,1)S(1)}, u32[]{:S(2)}, u32[]{:S(2)}) collective-permute-start(bf16[32,2048]{1,0:T(8,128)(2,1)S(1)} %convolution_convert_fusion), channel_id=1, source_target_pairs={{0,16},{2,18},{4,20},{6,22},{8,24},{10,26},{12,28},{14,30},{16,0},... | collective-permute-start | bytes 393224 | tf_op jit(solution)/shard_map/ppermute | solution.py:214
  21.5 2.2 %collective-permute-start.6 = (bf16[512,512]{1,0:T(8,128)(2,1)S(1)}, bf16[512,512]{1,0:T(8,128)(2,1)S(1)}, u32[]{:S(2)}, u32[]{:S(2)}) collective-permute-start(bf16[512,512]{1,0:T(8,128)(2,1)S(1)} %pad_maximum_fusion.3), channel_id=1, source_target_pairs={{0,2},{2,0},{4,6},{6,4},{8,10},{10,8},{12,14},{14,12},{16,18},{18,... | collective-permute-start | bytes 1572872 | tf_op jit(solution)/shard_map/ppermute | solution.py:214
  23.7 10.2 %copy-start.2 = (bf16[64,2048]{1,0:T(8,128)(2,1)}, bf16[64,2048]{1,0:T(8,128)(2,1)S(1)}, u32[]{:S(2)}) copy-start(bf16[64,2048]{1,0:T(8,128)(2,1)S(1)} %pad_maximum_fusion.6) | copy-start | bytes 786436
  23.7 4.5 %copy-start.10 = (s32[8]{0:T(128)S(1)}, s32[8]{0:T(128)}, u32[]{:S(2)}) copy-start(s32[8]{0:T(128)} %constant.37.clone) | copy-start | bytes 100
  23.7 4.5 %copy-start.9 = (s32[8]{0:T(128)S(1)}, s32[8]{0:T(128)}, u32[]{:S(2)}) copy-start(s32[8]{0:T(128)} %constant.36.clone) | copy-start | bytes 100
  25.2 10.8 %copy-start.1 = (bf16[512,1024]{1,0:T(8,128)(2,1)S(1)}, bf16[512,1024]{1,0:T(8,128)(2,1)}, u32[]{:S(2)}) copy-start(bf16[512,1024]{1,0:T(8,128)(2,1)} %param.18) | copy-start | bytes 3145732
  25.9 19.8 %collective-permute-start.12 = (bf16[2048,512]{1,0:T(8,128)(2,1)}, bf16[2048,512]{1,0:T(8,128)(2,1)}, u32[]{:S(2)}, u32[]{:S(2)}) collective-permute-start(bf16[2048,512]{1,0:T(8,128)(2,1)} %bitcast.4.gate0), channel_id=1, source_target_pairs={{0,2},{2,0},{4,6},{6,4},{8,10},{10,8},{12,14},{14,12},{16,18},{18,... | collective-permute-start | bytes 6291464 | tf_op jit(solution)/shard_map/ppermute | solution.py:214
  26.0 19.8 %collective-permute-start.13 = (bf16[2048,512]{1,0:T(8,128)(2,1)}, bf16[2048,512]{1,0:T(8,128)(2,1)}, u32[]{:S(2)}, u32[]{:S(2)}) collective-permute-start(bf16[2048,512]{1,0:T(8,128)(2,1)} %bitcast.5.up0), channel_id=1, source_target_pairs={{0,2},{2,0},{4,6},{6,4},{8,10},{10,8},{12,14},{14,12},{16,18},{18,... | collective-permute-start | bytes 6291464 | tf_op jit(solution)/shard_map/ppermute | solution.py:214
  26.5 19.3 %collective-permute-start.14 = (bf16[512,2048]{1,0:T(8,128)(2,1)}, bf16[512,2048]{1,0:T(8,128)(2,1)}, u32[]{:S(2)}, u32[]{:S(2)}) collective-permute-start(bf16[512,2048]{1,0:T(8,128)(2,1)} %bitcast.6.down0), channel_id=1, source_target_pairs={{0,2},{2,0},{4,6},{6,4},{8,10},{10,8},{12,14},{14,12},{16,18},{18,... | collective-permute-start | bytes 6291464 | tf_op jit(solution)/shard_map/ppermute | solution.py:214
  26.5 7.4 %collective-permute-start.9 = (bf16[64,2048]{1,0:T(8,128)(2,1)S(1)}, bf16[64,2048]{1,0:T(8,128)(2,1)S(1)}, u32[]{:S(2)}, u32[]{:S(2)}) collective-permute-start(bf16[64,2048]{1,0:T(8,128)(2,1)S(1)} %pad_maximum_fusion.6), channel_id=1, source_target_pairs={{0,8},{2,6},{4,12},{6,2},{8,0},{10,14},{12,4},{14,10},{16,24},{18,... | collective-permute-start | bytes 786440 | tf_op jit(solution)/shard_map/ppermute | solution.py:214
  26.5 9.4 %collective-permute-start.11 = (bf16[256,1024]{1,0:T(8,128)(2,1)S(1)}, bf16[256,1024]{1,0:T(8,128)(2,1)S(1)}, u32[]{:S(2)}, u32[]{:S(2)}) collective-permute-start(bf16[256,1024]{1,0:T(8,128)(2,1)S(1)} %collective-permute-done.8), channel_id=1, source_target_pairs={{0,2},{2,0},{4,6},{6,4},{8,10},{10,8},{12,14},{14,12},{16,18},{18,... | collective-permute-start | bytes 1572872 | tf_op jit(solution)/shard_map/ppermute | solution.py:214
  28.2 17.5 %all-to-all-start = ((bf16[16,32,256]{2,1,0:T(8,128)(2,1)}), bf16[16,32,256]{2,1,0:T(8,128)(2,1)S(1)}, u32[]{:S(2)}, u32[]{:S(2)}) async-start(bf16[16,32,256]{2,1,0:T(8,128)(2,1)} %bitcast.3), calls=%async_computation | async-start | bytes 524288 | tf_op jit(solution)/shard_map/all_to_all | solution.py:304
  33.9 2.0 %copy-start.4 = (bf16[64,2048]{1,0:T(8,128)(2,1)}, bf16[64,2048]{1,0:T(8,128)(2,1)S(1)}, u32[]{:S(2)}) copy-start(bf16[64,2048]{1,0:T(8,128)(2,1)S(1)} %collective-permute-done.9) | copy-start | bytes 786436
  33.9 11.8 %collective-permute-start.10 = (bf16[128,2048]{1,0:T(8,128)(2,1)S(1)}, bf16[128,2048]{1,0:T(8,128)(2,1)S(1)}, u32[]{:S(2)}, u32[]{:S(2)}) collective-permute-start(bf16[128,2048]{1,0:T(8,128)(2,1)S(1)} %pad_maximum_fusion.4), channel_id=1, source_target_pairs={{0,4},{2,10},{4,0},{6,14},{8,12},{10,2},{12,8},{14,6},{16,20},{18,... | collective-permute-start | bytes 1572872 | tf_op jit(solution)/shard_map/ppermute | solution.py:214
  36.5 9.2 %copy-start.3 = (bf16[64,2048]{1,0:T(8,128)(2,1)S(1)}, bf16[64,2048]{1,0:T(8,128)(2,1)}, u32[]{:S(2)}) copy-start(bf16[64,2048]{1,0:T(8,128)(2,1)} %copy-done.2) | copy-start | bytes 786436
  36.5 9.2 %copy-start.5 = (bf16[64,2048]{1,0:T(8,128)(2,1)S(1)}, bf16[64,2048]{1,0:T(8,128)(2,1)}, u32[]{:S(2)}) copy-start(bf16[64,2048]{1,0:T(8,128)(2,1)} %copy-done.4) | copy-start | bytes 786436
  36.7 9.1 %copy-start = (f32[2048]{0:T(1024)S(1)}, f32[2048]{0:T(1024)}, u32[]{:S(2)}) copy-start(f32[2048]{0:T(1024)} %param.19) | copy-start | bytes 24580
  52.7 6.5 %collective-permute-start.20 = (bf16[32,2048]{1,0:T(8,128)(2,1)S(1)}, bf16[32,2048]{1,0:T(8,128)(2,1)S(1)}, u32[]{:S(2)}, u32[]{:S(2)}) collective-permute-start(bf16[32,2048]{1,0:T(8,128)(2,1)S(1)} %get-tuple-element.44), channel_id=1, source_target_pairs={{0,4},{2,6},{4,0},{6,2},{8,12},{10,14},{12,8},{14,10},{16,20},{18,... | collective-permute-start | bytes 393224 | tf_op jit(solution)/shard_map/ppermute | solution.py:214
  54.0 6.3 %collective-permute-start.19 = (bf16[32,2048]{1,0:T(8,128)(2,1)S(1)}, bf16[32,2048]{1,0:T(8,128)(2,1)S(1)}, u32[]{:S(2)}, u32[]{:S(2)}) collective-permute-start(bf16[32,2048]{1,0:T(8,128)(2,1)S(1)} %get-tuple-element.45), channel_id=1, source_target_pairs={{0,8},{2,10},{4,12},{6,14},{8,0},{10,2},{12,4},{14,6},{16,24},{18,... | collective-permute-start | bytes 393224 | tf_op jit(solution)/shard_map/ppermute | solution.py:214
  55.2 8.3 %collective-permute-start.18 = (bf16[32,2048]{1,0:T(8,128)(2,1)S(1)}, bf16[32,2048]{1,0:T(8,128)(2,1)S(1)}, u32[]{:S(2)}, u32[]{:S(2)}) collective-permute-start(bf16[32,2048]{1,0:T(8,128)(2,1)S(1)} %get-tuple-element.46), channel_id=1, source_target_pairs={{0,12},{2,14},{4,8},{6,10},{8,4},{10,6},{12,0},{14,2},{16,28},{18,... | collective-permute-start | bytes 393224 | tf_op jit(solution)/shard_map/ppermute | solution.py:214
  56.3 10.0 %collective-permute-start.15 = (bf16[32,2048]{1,0:T(8,128)(2,1)S(1)}, bf16[32,2048]{1,0:T(8,128)(2,1)S(1)}, u32[]{:S(2)}, u32[]{:S(2)}) collective-permute-start(bf16[32,2048]{1,0:T(8,128)(2,1)S(1)} %get-tuple-element.43), channel_id=1, source_target_pairs={{0,12},{2,14},{4,8},{6,10},{8,4},{10,6},{12,0},{14,2},{16,28},{18,... | collective-permute-start | bytes 393224 | tf_op jit(solution)/shard_map/ppermute | solution.py:214
  58.2 9.7 %collective-permute-start.17 = (bf16[32,2048]{1,0:T(8,128)(2,1)S(1)}, bf16[32,2048]{1,0:T(8,128)(2,1)S(1)}, u32[]{:S(2)}, u32[]{:S(2)}) collective-permute-start(bf16[32,2048]{1,0:T(8,128)(2,1)S(1)} %get-tuple-element.47), channel_id=1, source_target_pairs={{0,4},{2,6},{4,0},{6,2},{8,12},{10,14},{12,8},{14,10},{16,20},{18,... | collective-permute-start | bytes 393224 | tf_op jit(solution)/shard_map/ppermute | solution.py:214
  59.3 11.9 %collective-permute-start.16 = (bf16[32,2048]{1,0:T(8,128)(2,1)S(1)}, bf16[32,2048]{1,0:T(8,128)(2,1)S(1)}, u32[]{:S(2)}, u32[]{:S(2)}) collective-permute-start(bf16[32,2048]{1,0:T(8,128)(2,1)S(1)} %get-tuple-element.48), channel_id=1, source_target_pairs={{0,8},{2,10},{4,12},{6,14},{8,0},{10,2},{12,4},{14,6},{16,24},{18,... | collective-permute-start | bytes 393224 | tf_op jit(solution)/shard_map/ppermute | solution.py:214
  63.6 7.6 %collective-permute-start.21 = (bf16[32,2048]{1,0:T(8,128)(2,1)S(1)}, bf16[32,2048]{1,0:T(8,128)(2,1)S(1)}, u32[]{:S(2)}, u32[]{:S(2)}) collective-permute-start(bf16[32,2048]{1,0:T(8,128)(2,1)S(1)} %add_convert_fusion.1), channel_id=1, source_target_pairs={{0,16},{2,18},{4,20},{6,22},{8,24},{10,26},{12,28},{14,30},{16,0},... | collective-permute-start | bytes 393224 | tf_op jit(solution)/shard_map/ppermute | solution.py:214

commit v4 on v3

--- a/solution.py
+++ b/solution.py
@@ -92,8 +92,8 @@
 
 
 def expert_kernel(
-    att_at, res_at, att, res_hbm, proj_hbm, gain, gate0, up0, down0, gate1, up1, down1,
-    own, keep, send, att_rows, hidden, normed, res, proj, gates, ups, downs, sems,
+    att_at, res_at, att, res0, res1, res2, res3, proj, gain, gate0, up0, down0, gate1, up1, down1,
+    own, keep, send, att_rows, hidden, normed, res, gates, ups, downs, sems,
 ):
     blocks, per, feats = res.shape
     sources, _, width = att.shape
@@ -107,20 +107,22 @@
         pltpu.make_async_copy(src, dst, sems.at[i])
         for i, (src, dst) in enumerate(
             (
-                (proj_hbm, proj), (res_hbm, res), (gate0, gates.at[0]), (up0, ups.at[0]),
+                (gate0, gates.at[0]), (up0, ups.at[0]),
                 (gate1, gates.at[1]), (up1, ups.at[1]), (down0, downs.at[0]), (down1, downs.at[1]),
+                (res0, res.at[: blocks // 4]), (res1, res.at[blocks // 4 : blocks // 2]),
+                (res2, res.at[blocks // 2 : 3 * blocks // 4]), (res3, res.at[3 * blocks // 4 :]),
             )
         )
     ]
-    for move in moves:
-        move.start()
+    for k in (6, 7, 8, 9, 0, 1, 2, 3, 4, 5):
+        moves[k].start()
     for b in range(blocks):
         for s in range(sources):
             att_rows[b * per : (b + 1) * per, s * width : (s + 1) * width] = att[
                 att_at[b] * sources + s
             ]
-    moves[0].wait()
-    moves[1].wait()
+    for k in (6, 7, 8, 9):
+        moves[k].wait()
     spans = [slice(k, k + rows) for k in range(0, blocks * per, rows)]
     for span in spans:
         squares = 0.0
@@ -139,13 +141,13 @@
     own[...] = hidden[:per, :].astype(F32)
     acts = []
     for side in (0, 1):
-        moves[2 + 2 * side].wait()
-        moves[3 + 2 * side].wait()
+        moves[2 * side].wait()
+        moves[2 * side + 1].wait()
         for span in spans:
             x = normed[span, :]
             acts.append((jax.nn.silu(dot(x, gates[side])) * dot(x, ups[side])).astype(BF))
-    moves[6].wait()
-    moves[7].wait()
+    moves[4].wait()
+    moves[5].wait()
     for k in range(len(spans)):
         for c in cols:
             total = dot(acts[k], downs[0, :, c]) + dot(acts[len(spans) + k], downs[1, :, c])
@@ -158,7 +160,8 @@
 
 
 def expert(att_at, res_at, att, res, proj, gain, near, far):
-    blocks, per, feats = res.shape
+    quarter, per, feats = res[0].shape
+    blocks = 4 * quarter
     units = near[0].shape[1]
     rows = blocks * per
     smem, vmem = pl.BlockSpec(memory_space=pltpu.SMEM), pl.BlockSpec(memory_space=pltpu.VMEM)
@@ -170,24 +173,23 @@
             jax.ShapeDtypeStruct((rows // 4, feats), F32),
             jax.ShapeDtypeStruct((3, rows // 4, feats), BF),
         ),
-        in_specs=[smem] * 2 + [vmem] + [hbm] * 2 + [vmem] + [hbm] * 6,
+        in_specs=[smem] * 2 + [vmem] + [hbm] * 4 + [vmem] * 2 + [hbm] * 6,
         out_specs=[vmem] * 3,
         scratch_shapes=[
             pltpu.VMEM((rows, proj.shape[0]), BF),
             pltpu.VMEM((rows, feats), BF),
             pltpu.VMEM((rows, feats), BF),
-            pltpu.VMEM(res.shape, BF),
-            pltpu.VMEM(proj.shape, BF),
+            pltpu.VMEM((blocks, per, feats), BF),
             pltpu.VMEM((2, feats, units), BF),
             pltpu.VMEM((2, feats, units), BF),
             pltpu.VMEM((2, units, feats), BF),
-            pltpu.SemaphoreType.DMA((8,)),
+            pltpu.SemaphoreType.DMA((10,)),
         ],
         compiler_params=pltpu.CompilerParams(vmem_limit_bytes=VMEM_LIMIT),
         cost_estimate=pl.CostEstimate(
             flops=12 * rows * feats * units, bytes_accessed=12 * feats * units, transcendentals=0
         ),
-    )(att_at, res_at, att, res, proj, gain[None], *near, *far)
+    )(att_at, res_at, att, *res, proj, gain[None], *near, *far)
 
 
 def body(
@@ -291,15 +293,15 @@
     att = jnp.concatenate(parts, axis=1).reshape(experts, per, width)
 
     if direct:
-        att, res_all = lax.optimization_barrier((att, res_all))
         go = jnp.broadcast_to(att[None], (n // 2, experts, per, width)).reshape(-1, per, width)
-        go, go_w, proj_near = lax.optimization_barrier((go, near_w, proj_near))
+        go, go_w, proj_near, res_all = lax.optimization_barrier((go, near_w, proj_near, res_all))
         proj_far = swap_core(proj_near)
         proj_come = jnp.concatenate([by_core(proj_near, proj_far), by_core(proj_far, proj_near)], axis=0)
         proj_all = both_halves(out_proj, proj_come)
         far_w = tuple(swap_core(w) for w in go_w)
-        for masks in res_masks[1:]:
-            res_all = jnp.concatenate([res_all, move(res_all, *masks)], axis=0)
+        res_come = [move(res_all, *res_masks[1]), move(res_all, *res_masks[2])]
+        res_come.append(move(res_come[0], *res_masks[2]))
+        res_all = [part.reshape(-1, per, part.shape[1]) for part in [res_all] + res_come]
         groups = [[(2 * k + c) * experts + e for k in range(n // 2) for e in range(experts)] for c in (0, 1)]
         att_all = lax.all_to_all(
             go, ("ctx", "exp"), split_axis=0, concat_axis=0, axis_index_groups=groups, tiled=True
@@ -309,7 +311,7 @@
         res_at = by_core(*(jnp.array([place.index(o) for o in order], jnp.int32) for place in places))
         hidden, keep, send = expert(
             (me ^ jnp.array(order, jnp.int32)) >> 1, res_at, att_all,
-            res_all.reshape(n // 2, per, -1), proj_all, norm_gain, near_w, far_w,
+            res_all, proj_all, norm_gain, near_w, far_w,
         )
         summed = scatter(keep, [send[k] for k in range(3)], sum_stages)
     else:

time: 72.3 us -> 71.9 us (level)
  waiting for transfers between devices: 24.6 us -> 22.6 us
  other arithmetic: 3.59 us -> 4.74 us
    ppermute x20 -> x21, waiting for transfers between devices: 24.4 us -> 20 us  [move(): return lax.ppermute(x, 'ctx', [(i, i ^ masks[i & 1]) for i in range(n)])]
    all_to_all x1, waiting for transfers between devices: 0.01 us -> 2.42 us  [body(): lax.all_to_all(go, ('ctx', 'exp'), split_axis=0, concat_axis=0, axis_inde...]
    all_to_all x1, starting transfers between devices: 5.59 us -> 7.11 us  [body(): lax.all_to_all(go, ('ctx', 'exp'), split_axis=0, concat_axis=0, axis_inde...]
    select_n x2, other arithmetic: 0.08 us -> 1.28 us  [by_core(): return jnp.where(core == 0, even, odd)]
    ppermute x20 -> x21, starting transfers between devices: 23.9 us -> 22.9 us  [move(): return lax.ppermute(x, 'ctx', [(i, i ^ masks[i & 1]) for i in range(n)])]
  transfers between devices with their start and end apart: 23 -> 24, of which waited for: 11 -> 13; matrix products, arithmetic and copies ran while one was open for 7% -> 9% of each run, Pallas kernels for 0% -> 0%
where the time goes in v4:
time: 71.9 us; the launch traced here: 71.5 us
  starting transfers between devices  32.1 us (45%)
  waiting for transfers between devices  22.6 us (31%)
  Pallas kernels  8.48 us (12%)
  other arithmetic  4.74 us (7%)
  local copies, waits for them, and re-layouts  2.07 us (3%)
  matrix products  1.28 us (2%)
    ppermute x21, starting transfers between devices, move(): return lax.ppermute(x, 'ctx', [(i, i ^ masks[i & 1]) for i in range(n)])  22.9 us
    ppermute x21, waiting for transfers between devices, move(): return lax.ppermute(x, 'ctx', [(i, i ^ masks[i & 1]) for i in range(n)])  20 us
    all_to_all x1, starting transfers between devices, body(): lax.all_to_all(go, ('ctx', 'exp'), split_axis=0, concat_axis=0, axis_inde...  7.11 us
    pallas_call x1, Pallas kernels, expert(): pl.pallas_call(expert_kernel, out_shape=(jax.ShapeDtypeStruct((per, feats...  6.74 us
    all_to_all x1, waiting for transfers between devices, body(): lax.all_to_all(go, ('ctx', 'exp'), split_axis=0, concat_axis=0, axis_inde...  2.42 us
    ppermute x2, starting transfers between devices, swap_exp(): return lax.ppermute(x, 'exp', [(0, 1), (1, 0)])  2.09 us
    pallas_call x1, Pallas kernels, prepare(): pl.pallas_call(functools.partial(prepare_kernel, far=dict(experts=experts...  1.74 us
  transfers between devices with their start and end apart: 24, of which 13 were waited for; matrix products, arithmetic and copies ran while one was open for 9% of the time, Pallas kernels for 0%

profile of v4, /device:TPU:0, one launch (start us, length us, event | category | flops | bytes accessed | tf_op | source)
XLA Modules:
  0.0 71.5 jit_solution(5576051474926862301)
XLA Ops:
  0.0 1.7 %shard_map.136 = (bf16[64,512]{1,0:T(8,128)(2,1)}, bf16[64,256]{1,0:T(8,128)(2,1)}, bf16[64,64]{1,0:T(8,128)(2,1)}, s32[1,1024]{1,0:T(1,128)}) custom-call(s32[1]{0:T(128)} %bitcast.me, s32[8,8]{1,0:T(8,128)} %mask.1, bf16[64,256]{1,0:T(8,128)(2,1)} %keys.1, bf16[64,256]{1,0:T(8,128)(2,1)} %values.1, bf16[64,256]{1,0:T(8,128)(2,1)} %queries.1, s32[1,64]{1,0:T(1,128)} %bitcast.32), custom_call_target="tpu_custom_call" | custom-call | tf_op jit(solution)/shard_map/pallas_call | solution.py:72
  1.7 5.0 %collective-permute-start.2 = (bf16[64,512]{1,0:T(8,128)(2,1)}, bf16[64,512]{1,0:T(8,128)(2,1)S(1)}, u32[]{:S(2)}, u32[]{:S(2)}) collective-permute-start(bf16[64,512]{1,0:T(8,128)(2,1)} %get-tuple-element.22), channel_id=1, source_target_pairs={{0,24},{2,26},{4,28},{6,30},{8,16},{10,18},{12,20},{14,22},{16,8},... | collective-permute-start | bytes 196616 | tf_op jit(solution)/shard_map/ppermute | solution.py:216
  6.8 0.6 collective-permute-start
  7.4 1.6 %collective-permute-start.3 = (bf16[64,1024]{1,0:T(8,128)(2,1)}, bf16[64,1024]{1,0:T(8,128)(2,1)S(1)}, u32[]{:S(2)}, u32[]{:S(2)}) collective-permute-start(bf16[64,1024]{1,0:T(8,128)(2,1)} %param.14), channel_id=1, source_target_pairs={{0,1},{1,0},{2,3},{3,2},{4,5},{5,4},{6,7},{7,6},{8,9},{9,8},{10,11... | collective-permute-start | bytes 393224 | tf_op jit(solution)/shard_map/ppermute | solution.py:222
  9.1 1.1 %constant_dynamic-slice_fusion = bf16[256,1024]{1,0:T(8,128)(2,1)S(1)} fusion(bf16[512,1024]{1,0:T(8,128)(2,1)} %param.18, s32[]{:T(128)S(6)} %select_n.69), kind=kLoop, calls=%fused_computation.59 | loop fusion | bytes 1048580 | tf_op jit(solution)/shard_map/dynamic_slice | solution.py:249
  10.2 0.4 collective-permute-start.7
  10.6 0.7 compare_reduce_fusion
  11.3 1.3 %collective-permute-done.1 = bf16[64,512]{1,0:T(8,128)(2,1)S(1)} collective-permute-done((bf16[64,512]{1,0:T(8,128)(2,1)}, bf16[64,512]{1,0:T(8,128)(2,1)S(1)}, u32[]{:S(2)}, u32[]{:S(2)}) %collective-permute-start.1) | collective-permute-done | bytes 65568 | tf_op jit(solution)/shard_map/ppermute | solution.py:216
  12.6 0.9 %pad_maximum_fusion.3 = bf16[256,512]{1,0:T(8,128)(2,1)S(1)} fusion(bf16[64,512]{1,0:T(8,128)(2,1)S(1)} %collective-permute-done.2, bf16[64,512]{1,0:T(8,128)(2,1)S(1)} %collective-permute-done.1, bf16[64,512]{1,0:T(8,128)(2,1)S(1)} %collective-permute-done, bf16[64,512]{1,0:T(8,128)(2,1)} %get-tuple-element.22), kind=kLoop, calls=%fused_computation.20 | loop fusion | flops 1048576 | bytes 524288 | tf_op jit(solution)/shard_map/concatenate | solution.py:226
  13.5 0.2 collective-permute-done.3
  13.7 1.8 %collective-permute-start.5 = (bf16[128,512]{1,0:T(8,128)(2,1)S(1)}, bf16[128,512]{1,0:T(8,128)(2,1)S(1)}, u32[]{:S(2)}, u32[]{:S(2)}) collective-permute-start(bf16[128,512]{1,0:T(8,128)(2,1)S(1)} %get-tuple-element.49), channel_id=1, source_target_pairs={{0,4},{2,6},{4,0},{6,2},{8,12},{10,14},{12,8},{14,10},{16,20},{18,... | collective-permute-start | bytes 393224 | tf_op jit(solution)/shard_map/ppermute | solution.py:216
  15.5 0.3 collective-permute-start.4
  15.8 0.2 convolution_convert_fusion
  16.0 2.4 %collective-permute-start.8 = (bf16[32,2048]{1,0:T(8,128)(2,1)S(1)}, bf16[32,2048]{1,0:T(8,128)(2,1)S(1)}, u32[]{:S(2)}, u32[]{:S(2)}) collective-permute-start(bf16[32,2048]{1,0:T(8,128)(2,1)S(1)} %convolution_convert_fusion), channel_id=1, source_target_pairs={{0,16},{2,18},{4,20},{6,22},{8,24},{10,26},{12,28},{14,30},{16,0},... | collective-permute-start | bytes 393224 | tf_op jit(solution)/shard_map/ppermute | solution.py:216
  18.3 1.7 %collective-permute-done.5 = bf16[128,512]{1,0:T(8,128)(2,1)S(1)} collective-permute-done((bf16[128,512]{1,0:T(8,128)(2,1)S(1)}, bf16[128,512]{1,0:T(8,128)(2,1)S(1)}, u32[]{:S(2)}, u32[]{:S(2)}) %collective-permute-start.5) | collective-permute-done | bytes 131104 | tf_op jit(solution)/shard_map/ppermute | solution.py:216
  20.1 1.4 %collective-permute-done.4 = bf16[128,512]{1,0:T(8,128)(2,1)S(1)} collective-permute-done((bf16[128,512]{1,0:T(8,128)(2,1)S(1)}, bf16[128,512]{1,0:T(8,128)(2,1)S(1)}, u32[]{:S(2)}, u32[]{:S(2)}) %collective-permute-start.4) | collective-permute-done | bytes 131104 | tf_op jit(solution)/shard_map/ppermute | solution.py:216
  21.7 2.0 %collective-permute-done.8 = bf16[32,2048]{1,0:T(8,128)(2,1)S(1)} collective-permute-done((bf16[32,2048]{1,0:T(8,128)(2,1)S(1)}, bf16[32,2048]{1,0:T(8,128)(2,1)S(1)}, u32[]{:S(2)}, u32[]{:S(2)}) %collective-permute-start.8) | collective-permute-done | bytes 131104 | tf_op jit(solution)/shard_map/ppermute | solution.py:216
  23.8 0.3 fusion.32
  24.1 0.3 fusion.33
  24.4 0.3 fusion.11
  24.7 0.2 fusion.3
  24.9 0.2 fusion.2
  25.2 0.8 %broadcast_in_dim.54 = bf16[8,2,32,256]{3,2,1,0:T(8,128)(2,1)} broadcast(bf16[2,32,256]{2,1,0:T(8,128)(2,1)S(1)} %bitcast.31), dimensions={1,2,3} | broadcast | bytes 294912 | tf_op jit(solution)/shard_map/broadcast_in_dim | solution.py:296
  26.0 0.5 collective-permute-start.14
  26.5 0.5 collective-permute-start.12
  27.1 7.1 %all-to-all-start = ((bf16[16,32,256]{2,1,0:T(8,128)(2,1)}), bf16[16,32,256]{2,1,0:T(8,128)(2,1)S(1)}, u32[]{:S(2)}, u32[]{:S(2)}) async-start(bf16[16,32,256]{2,1,0:T(8,128)(2,1)} %bitcast.3), calls=%async_computation | async-start | bytes 524288 | tf_op jit(solution)/shard_map/all_to_all | solution.py:306
  34.2 2.0 %collective-permute-start.10 = (bf16[64,2048]{1,0:T(8,128)(2,1)S(1)}, bf16[64,2048]{1,0:T(8,128)(2,1)S(1)}, u32[]{:S(2)}, u32[]{:S(2)}) collective-permute-start(bf16[64,2048]{1,0:T(8,128)(2,1)S(1)} %pad_maximum_fusion.4), channel_id=1, source_target_pairs={{0,4},{2,10},{4,0},{6,14},{8,12},{10,2},{12,8},{14,6},{16,20},{18,... | collective-permute-start | bytes 786440 | tf_op jit(solution)/shard_map/ppermute | solution.py:216
  36.2 0.1 collective-permute-start.11
  36.3 1.3 %broadcast_select_fusion.3 = (bf16[256,1024]{1,0:T(8,128)(2,1)S(1)}, bf16[256,1024]{1,0:T(8,128)(2,1)S(1)}) fusion(bf16[256,1024]{1,0:T(8,128)(2,1)} %copy-done.2, bf16[256,1024]{1,0:T(8,128)(2,1)} %collective-permute-done.12, pred[]{:T(512)S(6)} %eq.8), kind=kLoop, calls=%fused_computation.15 | loop fusion | flops 524288 | bytes 2097153 | tf_op jit(solution)/shard_map/jit(_where)/select_n | solution.py:212
  37.6 0.5 broadcast_select_fusion.1
  38.1 0.2 pad_maximum_fusion.proj
  38.3 4.1 %collective-permute-done.10 = bf16[64,2048]{1,0:T(8,128)(2,1)S(1)} collective-permute-done((bf16[64,2048]{1,0:T(8,128)(2,1)S(1)}, bf16[64,2048]{1,0:T(8,128)(2,1)S(1)}, u32[]{:S(2)}, u32[]{:S(2)}) %collective-permute-start.10) | collective-permute-done | bytes 262176 | tf_op jit(solution)/shard_map/ppermute | solution.py:216
  42.4 2.4 %all-to-all-done.att = bf16[16,32,256]{2,1,0:T(8,128)(2,1)S(1)} async-done(((bf16[16,32,256]{2,1,0:T(8,128)(2,1)}), bf16[16,32,256]{2,1,0:T(8,128)(2,1)S(1)}, u32[]{:S(2)}, u32[]{:S(2)}) %all-to-all-start) | async-done | bytes 262176 | tf_op jit(solution)/shard_map/all_to_all | solution.py:306
  44.8 0.9 %collective-permute-done.11 = bf16[64,2048]{1,0:T(8,128)(2,1)S(1)} collective-permute-done((bf16[64,2048]{1,0:T(8,128)(2,1)S(1)}, bf16[64,2048]{1,0:T(8,128)(2,1)S(1)}, u32[]{:S(2)}, u32[]{:S(2)}) %collective-permute-start.11) | collective-permute-done | bytes 262176 | tf_op jit(solution)/shard_map/ppermute | solution.py:216
  45.8 6.7 %shard_map.137 = (f32[32,2048]{1,0:T(8,128)S(1)}, f32[64,2048]{1,0:T(8,128)S(1)}, bf16[3,64,2048]{2,1,0:T(8,128)(2,1)S(1)}) custom-call(s32[8]{0:T(128)S(1)} %xor_shift-right-arithmetic_fusion.att_at, s32[8]{0:T(128)S(1)} %broadcast_select_fusion.6.res_at, bf16[16,32,256]{2,1,0:T(8,128)(2,1)S(1)} %all-to-all-done.att, bf16[2,32,2048]{2,1,0:T(8,128)(2,1)S(1)} %bitcast.26, ...), custom_call_target="tpu_custom_call" | custom-call | flops 3221225472 | bytes 12582912 | tf_op jit(solution)/shard_map/pallas_call | solution.py:169
  52.6 1.3 %collective-permute-start.21 = (bf16[32,2048]{1,0:T(8,128)(2,1)S(1)}, bf16[32,2048]{1,0:T(8,128)(2,1)S(1)}, u32[]{:S(2)}, u32[]{:S(2)}) collective-permute-start(bf16[32,2048]{1,0:T(8,128)(2,1)S(1)} %get-tuple-element.42), channel_id=1, source_target_pairs={{0,4},{2,6},{4,0},{6,2},{8,12},{10,14},{12,8},{14,10},{16,20},{18,... | collective-permute-start | bytes 393224 | tf_op jit(solution)/shard_map/ppermute | solution.py:216
  53.8 1.1 %collective-permute-start.20 = (bf16[32,2048]{1,0:T(8,128)(2,1)S(1)}, bf16[32,2048]{1,0:T(8,128)(2,1)S(1)}, u32[]{:S(2)}, u32[]{:S(2)}) collective-permute-start(bf16[32,2048]{1,0:T(8,128)(2,1)S(1)} %get-tuple-element.43), channel_id=1, source_target_pairs={{0,8},{2,10},{4,12},{6,14},{8,0},{10,2},{12,4},{14,6},{16,24},{18,... | collective-permute-start | bytes 393224 | tf_op jit(solution)/shard_map/ppermute | solution.py:216
  55.0 1.2 %collective-permute-start.19 = (bf16[32,2048]{1,0:T(8,128)(2,1)S(1)}, bf16[32,2048]{1,0:T(8,128)(2,1)S(1)}, u32[]{:S(2)}, u32[]{:S(2)}) collective-permute-start(bf16[32,2048]{1,0:T(8,128)(2,1)S(1)} %get-tuple-element.44), channel_id=1, source_target_pairs={{0,12},{2,14},{4,8},{6,10},{8,4},{10,6},{12,0},{14,2},{16,28},{18,... | collective-permute-start | bytes 393224 | tf_op jit(solution)/shard_map/ppermute | solution.py:216
  56.1 1.7 %collective-permute-start.16 = (bf16[32,2048]{1,0:T(8,128)(2,1)S(1)}, bf16[32,2048]{1,0:T(8,128)(2,1)S(1)}, u32[]{:S(2)}, u32[]{:S(2)}) collective-permute-start(bf16[32,2048]{1,0:T(8,128)(2,1)S(1)} %get-tuple-element.41), channel_id=1, source_target_pairs={{0,12},{2,14},{4,8},{6,10},{8,4},{10,6},{12,0},{14,2},{16,28},{18,... | collective-permute-start | bytes 393224 | tf_op jit(solution)/shard_map/ppermute | solution.py:216
  57.9 1.3 %collective-permute-start.18 = (bf16[32,2048]{1,0:T(8,128)(2,1)S(1)}, bf16[32,2048]{1,0:T(8,128)(2,1)S(1)}, u32[]{:S(2)}, u32[]{:S(2)}) collective-permute-start(bf16[32,2048]{1,0:T(8,128)(2,1)S(1)} %get-tuple-element.45), channel_id=1, source_target_pairs={{0,4},{2,6},{4,0},{6,2},{8,12},{10,14},{12,8},{14,10},{16,20},{18,... | collective-permute-start | bytes 393224 | tf_op jit(solution)/shard_map/ppermute | solution.py:216
  59.2 0.5 collective-permute-start.17
  59.6 0.5 collective-permute-done.20
  60.2 3.2 %collective-permute-done.19 = bf16[32,2048]{1,0:T(8,128)(2,1)S(1)} collective-permute-done((bf16[32,2048]{1,0:T(8,128)(2,1)S(1)}, bf16[32,2048]{1,0:T(8,128)(2,1)S(1)}, u32[]{:S(2)}, u32[]{:S(2)}) %collective-permute-start.19) | collective-permute-done | bytes 131104 | tf_op jit(solution)/shard_map/ppermute | solution.py:216
  63.5 2.5 %collective-permute-start.22 = (bf16[32,2048]{1,0:T(8,128)(2,1)S(1)}, bf16[32,2048]{1,0:T(8,128)(2,1)S(1)}, u32[]{:S(2)}, u32[]{:S(2)}) collective-permute-start(bf16[32,2048]{1,0:T(8,128)(2,1)S(1)} %add_convert_fusion.1), channel_id=1, source_target_pairs={{0,16},{2,18},{4,20},{6,22},{8,24},{10,26},{12,28},{14,30},{16,0},... | collective-permute-start | bytes 393224 | tf_op jit(solution)/shard_map/ppermute | solution.py:216
  66.0 0.2 collective-permute-done.16
  66.2 1.2 %collective-permute-done.18 = bf16[32,2048]{1,0:T(8,128)(2,1)S(1)} collective-permute-done((bf16[32,2048]{1,0:T(8,128)(2,1)S(1)}, bf16[32,2048]{1,0:T(8,128)(2,1)S(1)}, u32[]{:S(2)}, u32[]{:S(2)}) %collective-permute-start.18) | collective-permute-done | bytes 131104 | tf_op jit(solution)/shard_map/ppermute | solution.py:216
  67.4 3.4 %collective-permute-done.17 = bf16[32,2048]{1,0:T(8,128)(2,1)S(1)} collective-permute-done((bf16[32,2048]{1,0:T(8,128)(2,1)S(1)}, bf16[32,2048]{1,0:T(8,128)(2,1)S(1)}, u32[]{:S(2)}, u32[]{:S(2)}) %collective-permute-start.17) | collective-permute-done | bytes 131104 | tf_op jit(solution)/shard_map/ppermute | solution.py:216
  70.8 0.8 %fusion.17 = bf16[1,32,2048]{2,1,0:T(8,128)(2,1)} fusion(f32[32,2048]{1,0:T(8,128)S(1)} %get-tuple-element.32, bf16[32,2048]{1,0:T(8,128)(2,1)S(1)} %collective-permute-done.22, bf16[32,2048]{1,0:T(8,128)(2,1)S(1)} %collective-permute-done.18, bf16[32,2048]{1,0:T(8,128)(2,1)S(1)} %collective-permute-done.17, ...), kind=kLoop, calls=%fused_computation.33 | loop fusion | flops 655360 | bytes 1179648 | tf_op jit(solution)/shard_map/broadcast_in_dim | solution.py:328
  (45 shorter events, 0.5 us)
Async XLA Ops:
  0.0 15.8 %copy-start.3 = (bf16[64,1024]{1,0:T(8,128)(2,1)S(1)}, bf16[64,1024]{1,0:T(8,128)(2,1)}, u32[]{:S(2)}) copy-start(bf16[64,1024]{1,0:T(8,128)(2,1)} %param.14) | copy-start | bytes 393220
  1.7 14.1 %copy-start.5 = (bf16[64,64]{1,0:T(8,128)(2,1)S(1)}, bf16[64,64]{1,0:T(8,128)(2,1)}, u32[]{:S(2)}) copy-start(bf16[64,64]{1,0:T(8,128)(2,1)} %get-tuple-element.24) | copy-start | bytes 24580
  1.7 9.6 %collective-permute-start.2 = (bf16[64,512]{1,0:T(8,128)(2,1)}, bf16[64,512]{1,0:T(8,128)(2,1)S(1)}, u32[]{:S(2)}, u32[]{:S(2)}) collective-permute-start(bf16[64,512]{1,0:T(8,128)(2,1)} %get-tuple-element.22), channel_id=1, source_target_pairs={{0,24},{2,26},{4,28},{6,30},{8,16},{10,18},{12,20},{14,22},{16,8},... | collective-permute-start | bytes 196616 | tf_op jit(solution)/shard_map/ppermute | solution.py:216
  6.8 5.8 %collective-permute-start.1 = (bf16[64,512]{1,0:T(8,128)(2,1)}, bf16[64,512]{1,0:T(8,128)(2,1)S(1)}, u32[]{:S(2)}, u32[]{:S(2)}) collective-permute-start(bf16[64,512]{1,0:T(8,128)(2,1)} %get-tuple-element.22), channel_id=1, source_target_pairs={{0,16},{2,18},{4,20},{6,22},{8,24},{10,26},{12,28},{14,30},{16,0},... | collective-permute-start | bytes 196616 | tf_op jit(solution)/shard_map/ppermute | solution.py:216
  6.8 5.8 %collective-permute-start = (bf16[64,512]{1,0:T(8,128)(2,1)}, bf16[64,512]{1,0:T(8,128)(2,1)S(1)}, u32[]{:S(2)}, u32[]{:S(2)}) collective-permute-start(bf16[64,512]{1,0:T(8,128)(2,1)} %get-tuple-element.22), channel_id=1, source_target_pairs={{0,8},{2,10},{4,12},{6,14},{8,0},{10,2},{12,4},{14,6},{16,24},{18,... | collective-permute-start | bytes 196616 | tf_op jit(solution)/shard_map/ppermute | solution.py:216
  7.4 6.2 %collective-permute-start.3 = (bf16[64,1024]{1,0:T(8,128)(2,1)}, bf16[64,1024]{1,0:T(8,128)(2,1)S(1)}, u32[]{:S(2)}, u32[]{:S(2)}) collective-permute-start(bf16[64,1024]{1,0:T(8,128)(2,1)} %param.14), channel_id=1, source_target_pairs={{0,1},{1,0},{2,3},{3,2},{4,5},{5,4},{6,7},{7,6},{8,9},{9,8},{10,11... | collective-permute-start | bytes 393224 | tf_op jit(solution)/shard_map/ppermute | solution.py:222
  10.2 15.0 %collective-permute-start.7 = (bf16[256,1024]{1,0:T(8,128)(2,1)S(1)}, bf16[256,1024]{1,0:T(8,128)(2,1)S(1)}, u32[]{:S(2)}, u32[]{:S(2)}) collective-permute-start(bf16[256,1024]{1,0:T(8,128)(2,1)S(1)} %constant_dynamic-slice_fusion), channel_id=1, source_target_pairs={{0,1},{1,0},{2,3},{3,2},{4,5},{5,4},{6,7},{7,6},{8,9},{9,8},{10,11... | collective-permute-start | bytes 1572872 | tf_op jit(solution)/shard_map/ppermute | solution.py:222
  13.7 6.4 %collective-permute-start.5 = (bf16[128,512]{1,0:T(8,128)(2,1)S(1)}, bf16[128,512]{1,0:T(8,128)(2,1)S(1)}, u32[]{:S(2)}, u32[]{:S(2)}) collective-permute-start(bf16[128,512]{1,0:T(8,128)(2,1)S(1)} %get-tuple-element.49), channel_id=1, source_target_pairs={{0,4},{2,6},{4,0},{6,2},{8,12},{10,14},{12,8},{14,10},{16,20},{18,... | collective-permute-start | bytes 393224 | tf_op jit(solution)/shard_map/ppermute | solution.py:216
  15.5 6.0 %collective-permute-start.4 = (bf16[128,512]{1,0:T(8,128)(2,1)S(1)}, bf16[128,512]{1,0:T(8,128)(2,1)S(1)}, u32[]{:S(2)}, u32[]{:S(2)}) collective-permute-start(bf16[128,512]{1,0:T(8,128)(2,1)S(1)} %get-tuple-element.50), channel_id=1, source_target_pairs={{0,4},{2,6},{4,0},{6,2},{8,12},{10,14},{12,8},{14,10},{16,20},{18,... | collective-permute-start | bytes 393224 | tf_op jit(solution)/shard_map/ppermute | solution.py:216
  15.8 8.0 %copy-start.4 = (bf16[64,256]{1,0:T(8,128)(2,1)S(1)}, bf16[64,256]{1,0:T(8,128)(2,1)}, u32[]{:S(2)}) copy-start(bf16[64,256]{1,0:T(8,128)(2,1)} %get-tuple-element.21) | copy-start | bytes 98308
  16.0 7.7 %collective-permute-start.8 = (bf16[32,2048]{1,0:T(8,128)(2,1)S(1)}, bf16[32,2048]{1,0:T(8,128)(2,1)S(1)}, u32[]{:S(2)}, u32[]{:S(2)}) collective-permute-start(bf16[32,2048]{1,0:T(8,128)(2,1)S(1)} %convolution_convert_fusion), channel_id=1, source_target_pairs={{0,16},{2,18},{4,20},{6,22},{8,24},{10,26},{12,28},{14,30},{16,0},... | collective-permute-start | bytes 393224 | tf_op jit(solution)/shard_map/ppermute | solution.py:216
  21.5 2.2 %collective-permute-start.6 = (bf16[512,512]{1,0:T(8,128)(2,1)S(1)}, bf16[512,512]{1,0:T(8,128)(2,1)S(1)}, u32[]{:S(2)}, u32[]{:S(2)}) collective-permute-start(bf16[512,512]{1,0:T(8,128)(2,1)S(1)} %pad_maximum_fusion.2), channel_id=1, source_target_pairs={{0,2},{2,0},{4,6},{6,4},{8,10},{10,8},{12,14},{14,12},{16,18},{18,... | collective-permute-start | bytes 1572872 | tf_op jit(solution)/shard_map/ppermute | solution.py:216
  23.7 3.3 %copy-start.7 = (s32[8]{0:T(128)S(1)}, s32[8]{0:T(128)}, u32[]{:S(2)}) copy-start(s32[8]{0:T(128)} %constant.37.clone) | copy-start | bytes 100
  23.7 3.4 %copy-start.6 = (s32[8]{0:T(128)S(1)}, s32[8]{0:T(128)}, u32[]{:S(2)}) copy-start(s32[8]{0:T(128)} %constant.36.clone) | copy-start | bytes 100
  24.7 12.9 %copy-start.1 = (bf16[512,1024]{1,0:T(8,128)(2,1)S(1)}, bf16[512,1024]{1,0:T(8,128)(2,1)}, u32[]{:S(2)}) copy-start(bf16[512,1024]{1,0:T(8,128)(2,1)} %param.18) | copy-start | bytes 3145732
  25.2 11.0 %copy-start.2 = (bf16[256,1024]{1,0:T(8,128)(2,1)}, bf16[256,1024]{1,0:T(8,128)(2,1)S(1)}, u32[]{:S(2)}) copy-start(bf16[256,1024]{1,0:T(8,128)(2,1)S(1)} %collective-permute-done.7) | copy-start | bytes 1572868
  26.0 19.7 %collective-permute-start.13 = (bf16[2048,512]{1,0:T(8,128)(2,1)}, bf16[2048,512]{1,0:T(8,128)(2,1)}, u32[]{:S(2)}, u32[]{:S(2)}) collective-permute-start(bf16[2048,512]{1,0:T(8,128)(2,1)} %bitcast.4.gate0), channel_id=1, source_target_pairs={{0,2},{2,0},{4,6},{6,4},{8,10},{10,8},{12,14},{14,12},{16,18},{18,... | collective-permute-start | bytes 6291464 | tf_op jit(solution)/shard_map/ppermute | solution.py:216
  26.0 19.7 %collective-permute-start.14 = (bf16[2048,512]{1,0:T(8,128)(2,1)}, bf16[2048,512]{1,0:T(8,128)(2,1)}, u32[]{:S(2)}, u32[]{:S(2)}) collective-permute-start(bf16[2048,512]{1,0:T(8,128)(2,1)} %bitcast.5.up0), channel_id=1, source_target_pairs={{0,2},{2,0},{4,6},{6,4},{8,10},{10,8},{12,14},{14,12},{16,18},{18,... | collective-permute-start | bytes 6291464 | tf_op jit(solution)/shard_map/ppermute | solution.py:216
  26.5 19.2 %collective-permute-start.15 = (bf16[512,2048]{1,0:T(8,128)(2,1)}, bf16[512,2048]{1,0:T(8,128)(2,1)}, u32[]{:S(2)}, u32[]{:S(2)}) collective-permute-start(bf16[512,2048]{1,0:T(8,128)(2,1)} %bitcast.6.down0), channel_id=1, source_target_pairs={{0,2},{2,0},{4,6},{6,4},{8,10},{10,8},{12,14},{14,12},{16,18},{18,... | collective-permute-start | bytes 6291464 | tf_op jit(solution)/shard_map/ppermute | solution.py:216
  26.5 9.7 %collective-permute-start.12 = (bf16[256,1024]{1,0:T(8,128)(2,1)S(1)}, bf16[256,1024]{1,0:T(8,128)(2,1)}, u32[]{:S(2)}, u32[]{:S(2)}) collective-permute-start(bf16[256,1024]{1,0:T(8,128)(2,1)S(1)} %collective-permute-done.7), channel_id=1, source_target_pairs={{0,2},{2,0},{4,6},{6,4},{8,10},{10,8},{12,14},{14,12},{16,18},{18,... | collective-permute-start | bytes 1572872 | tf_op jit(solution)/shard_map/ppermute | solution.py:216
  27.0 7.2 %collective-permute-start.9 = (bf16[64,2048]{1,0:T(8,128)(2,1)S(1)}, bf16[64,2048]{1,0:T(8,128)(2,1)S(1)}, u32[]{:S(2)}, u32[]{:S(2)}) collective-permute-start(bf16[64,2048]{1,0:T(8,128)(2,1)S(1)} %pad_maximum_fusion.4), channel_id=1, source_target_pairs={{0,8},{2,6},{4,12},{6,2},{8,0},{10,14},{12,4},{14,10},{16,24},{18,... | collective-permute-start | bytes 786440 | tf_op jit(solution)/shard_map/ppermute | solution.py:216
  27.1 17.8 %all-to-all-start = ((bf16[16,32,256]{2,1,0:T(8,128)(2,1)}), bf16[16,32,256]{2,1,0:T(8,128)(2,1)S(1)}, u32[]{:S(2)}, u32[]{:S(2)}) async-start(bf16[16,32,256]{2,1,0:T(8,128)(2,1)} %bitcast.3), calls=%async_computation | async-start | bytes 524288 | tf_op jit(solution)/shard_map/all_to_all | solution.py:306
  34.2 8.2 %collective-permute-start.10 = (bf16[64,2048]{1,0:T(8,128)(2,1)S(1)}, bf16[64,2048]{1,0:T(8,128)(2,1)S(1)}, u32[]{:S(2)}, u32[]{:S(2)}) collective-permute-start(bf16[64,2048]{1,0:T(8,128)(2,1)S(1)} %pad_maximum_fusion.4), channel_id=1, source_target_pairs={{0,4},{2,10},{4,0},{6,14},{8,12},{10,2},{12,8},{14,6},{16,20},{18,... | collective-permute-start | bytes 786440 | tf_op jit(solution)/shard_map/ppermute | solution.py:216
  36.2 9.6 %collective-permute-start.11 = (bf16[64,2048]{1,0:T(8,128)(2,1)S(1)}, bf16[64,2048]{1,0:T(8,128)(2,1)S(1)}, u32[]{:S(2)}, u32[]{:S(2)}) collective-permute-start(bf16[64,2048]{1,0:T(8,128)(2,1)S(1)} %collective-permute-done.9), channel_id=1, source_target_pairs={{0,4},{2,10},{4,0},{6,14},{8,12},{10,2},{12,8},{14,6},{16,20},{18,... | collective-permute-start | bytes 786440 | tf_op jit(solution)/shard_map/ppermute | solution.py:216
  38.1 7.6 %copy-start = (f32[2048]{0:T(1024)S(1)}, f32[2048]{0:T(1024)}, u32[]{:S(2)}) copy-start(f32[2048]{0:T(1024)} %param.19) | copy-start | bytes 24580
  52.6 6.6 %collective-permute-start.21 = (bf16[32,2048]{1,0:T(8,128)(2,1)S(1)}, bf16[32,2048]{1,0:T(8,128)(2,1)S(1)}, u32[]{:S(2)}, u32[]{:S(2)}) collective-permute-start(bf16[32,2048]{1,0:T(8,128)(2,1)S(1)} %get-tuple-element.42), channel_id=1, source_target_pairs={{0,4},{2,6},{4,0},{6,2},{8,12},{10,14},{12,8},{14,10},{16,20},{18,... | collective-permute-start | bytes 393224 | tf_op jit(solution)/shard_map/ppermute | solution.py:216
  53.8 6.3 %collective-permute-start.20 = (bf16[32,2048]{1,0:T(8,128)(2,1)S(1)}, bf16[32,2048]{1,0:T(8,128)(2,1)S(1)}, u32[]{:S(2)}, u32[]{:S(2)}) collective-permute-start(bf16[32,2048]{1,0:T(8,128)(2,1)S(1)} %get-tuple-element.43), channel_id=1, source_target_pairs={{0,8},{2,10},{4,12},{6,14},{8,0},{10,2},{12,4},{14,6},{16,24},{18,... | collective-permute-start | bytes 393224 | tf_op jit(solution)/shard_map/ppermute | solution.py:216
  55.0 8.4 %collective-permute-start.19 = (bf16[32,2048]{1,0:T(8,128)(2,1)S(1)}, bf16[32,2048]{1,0:T(8,128)(2,1)S(1)}, u32[]{:S(2)}, u32[]{:S(2)}) collective-permute-start(bf16[32,2048]{1,0:T(8,128)(2,1)S(1)} %get-tuple-element.44), channel_id=1, source_target_pairs={{0,12},{2,14},{4,8},{6,10},{8,4},{10,6},{12,0},{14,2},{16,28},{18,... | collective-permute-start | bytes 393224 | tf_op jit(solution)/shard_map/ppermute | solution.py:216
  56.1 10.0 %collective-permute-start.16 = (bf16[32,2048]{1,0:T(8,128)(2,1)S(1)}, bf16[32,2048]{1,0:T(8,128)(2,1)S(1)}, u32[]{:S(2)}, u32[]{:S(2)}) collective-permute-start(bf16[32,2048]{1,0:T(8,128)(2,1)S(1)} %get-tuple-element.41), channel_id=1, source_target_pairs={{0,12},{2,14},{4,8},{6,10},{8,4},{10,6},{12,0},{14,2},{16,28},{18,... | collective-permute-start | bytes 393224 | tf_op jit(solution)/shard_map/ppermute | solution.py:216
  57.9 9.5 %collective-permute-start.18 = (bf16[32,2048]{1,0:T(8,128)(2,1)S(1)}, bf16[32,2048]{1,0:T(8,128)(2,1)S(1)}, u32[]{:S(2)}, u32[]{:S(2)}) collective-permute-start(bf16[32,2048]{1,0:T(8,128)(2,1)S(1)} %get-tuple-element.45), channel_id=1, source_target_pairs={{0,4},{2,6},{4,0},{6,2},{8,12},{10,14},{12,8},{14,10},{16,20},{18,... | collective-permute-start | bytes 393224 | tf_op jit(solution)/shard_map/ppermute | solution.py:216
  59.2 11.6 %collective-permute-start.17 = (bf16[32,2048]{1,0:T(8,128)(2,1)S(1)}, bf16[32,2048]{1,0:T(8,128)(2,1)S(1)}, u32[]{:S(2)}, u32[]{:S(2)}) collective-permute-start(bf16[32,2048]{1,0:T(8,128)(2,1)S(1)} %get-tuple-element.46), channel_id=1, source_target_pairs={{0,8},{2,10},{4,12},{6,14},{8,0},{10,2},{12,4},{14,6},{16,24},{18,... | collective-permute-start | bytes 393224 | tf_op jit(solution)/shard_map/ppermute | solution.py:216
  63.5 7.3 %collective-permute-start.22 = (bf16[32,2048]{1,0:T(8,128)(2,1)S(1)}, bf16[32,2048]{1,0:T(8,128)(2,1)S(1)}, u32[]{:S(2)}, u32[]{:S(2)}) collective-permute-start(bf16[32,2048]{1,0:T(8,128)(2,1)S(1)} %add_convert_fusion.1), channel_id=1, source_target_pairs={{0,16},{2,18},{4,20},{6,22},{8,24},{10,26},{12,28},{14,30},{16,0},... | collective-permute-start | bytes 393224 | tf_op jit(solution)/shard_map/ppermute | solution.py:216

commit v5 on v4

--- a/solution.py
+++ b/solution.py
@@ -10,7 +10,7 @@
 
 HD = 128
 BLK = 128
-VMEM_LIMIT = 48 * 2**20
+VMEM_LIMIT = 50 * 2**20
 BF = jnp.bfloat16
 F32 = jnp.float32
 
@@ -93,14 +93,14 @@
 
 def expert_kernel(
     att_at, res_at, att, res0, res1, res2, res3, proj, gain, gate0, up0, down0, gate1, up1, down1,
-    own, keep, send, att_rows, hidden, normed, res, gates, ups, downs, sems,
+    own, keep, send, acts_out, att_rows, hidden, normed, res, gates, ups, downs, sems,
 ):
     blocks, per, feats = res.shape
     sources, _, width = att.shape
     sources //= blocks
     pieces = send.shape[0] + 1
-    size = blocks * per // pieces
-    rows = 2 * size
+    size = blocks * per // (2 * pieces)
+    rows = pieces * size
     tile = math.gcd(feats, 512)
     cols = [slice(c, c + tile) for c in range(0, feats, tile)]
     moves = [
@@ -138,7 +138,7 @@
         scale = lax.rsqrt(squares / feats + 1e-05)
         for c in cols:
             normed[span, c] = (hidden[span, c].astype(F32) * scale * gain[:, c]).astype(BF)
-    own[...] = hidden[:per, :].astype(F32)
+    own[...] = hidden[rows : rows + per, :].astype(F32)
     acts = []
     for side in (0, 1):
         moves[2 * side].wait()
@@ -146,17 +146,52 @@
         for span in spans:
             x = normed[span, :]
             acts.append((jax.nn.silu(dot(x, gates[side])) * dot(x, ups[side])).astype(BF))
+    acts_out[0] = acts[1]
+    acts_out[1] = acts[3]
     moves[4].wait()
     moves[5].wait()
-    for k in range(len(spans)):
-        for c in cols:
-            total = dot(acts[k], downs[0, :, c]) + dot(acts[len(spans) + k], downs[1, :, c])
-            for piece in (0, 1):
-                part = total[piece * size : (piece + 1) * size]
-                if 2 * k + piece == 0:
-                    keep[:, c] = part
-                else:
-                    send[2 * k + piece - 1, :, c] = part.astype(BF)
+    project_down(acts[0], acts[2], downs, keep, send, cols)
+
+
+def project_down(first, second, downs, keep, send, cols):
+    size = keep.shape[0]
+    for c in cols:
+        total = dot(first, downs[0, :, c]) + dot(second, downs[1, :, c])
+        keep[:, c] = total[:size]
+        for piece in range(send.shape[0]):
+            send[piece, :, c] = total[(piece + 1) * size : (piece + 2) * size].astype(BF)
+
+
+def rest_kernel(acts, down0, down1, keep, send, downs, sems):
+    moves = [
+        pltpu.make_async_copy(down, downs.at[side], sems.at[side])
+        for side, down in enumerate((down0, down1))
+    ]
+    for move in moves:
+        move.start()
+    for move in moves:
+        move.wait()
+    feats = downs.shape[2]
+    tile = math.gcd(feats, 512)
+    cols = [slice(c, c + tile) for c in range(0, feats, tile)]
+    project_down(acts[0], acts[1], downs, keep, send, cols)
+
+
+def rest(acts, down0, down1):
+    units, feats = down0.shape
+    size = acts.shape[1] // 4
+    vmem, hbm = pl.BlockSpec(memory_space=pltpu.VMEM), pl.BlockSpec(memory_space=pl.ANY)
+    return pl.pallas_call(
+        rest_kernel,
+        out_shape=(
+            jax.ShapeDtypeStruct((size, feats), F32),
+            jax.ShapeDtypeStruct((3, size, feats), BF),
+        ),
+        in_specs=[vmem] + [hbm] * 2,
+        out_specs=[vmem] * 2,
+        scratch_shapes=[pltpu.VMEM((2, units, feats), BF), pltpu.SemaphoreType.DMA((2,))],
+        compiler_params=pltpu.CompilerParams(vmem_limit_bytes=VMEM_LIMIT),
+    )(acts, down0, down1)
 
 
 def expert(att_at, res_at, att, res, proj, gain, near, far):
@@ -170,11 +205,12 @@
         expert_kernel,
         out_shape=(
             jax.ShapeDtypeStruct((per, feats), F32),
-            jax.ShapeDtypeStruct((rows // 4, feats), F32),
-            jax.ShapeDtypeStruct((3, rows // 4, feats), BF),
+            jax.ShapeDtypeStruct((rows // 8, feats), F32),
+            jax.ShapeDtypeStruct((3, rows // 8, feats), BF),
+            jax.ShapeDtypeStruct((2, rows // 2, units), BF),
         ),
         in_specs=[smem] * 2 + [vmem] + [hbm] * 4 + [vmem] * 2 + [hbm] * 6,
-        out_specs=[vmem] * 3,
+        out_specs=[vmem] * 4,
         scratch_shapes=[
             pltpu.VMEM((rows, proj.shape[0]), BF),
             pltpu.VMEM((rows, feats), BF),
@@ -256,7 +292,7 @@
     far_kv = swap_core(all_kv)
 
     near_w = (w_gate[0], w_up[0], w_down[0])
-    direct = experts == 2 and per % 32 == 0
+    direct = experts == 2 and per % 32 == 0 and n == 16
     if direct:
         first = exp_me == 0
 
@@ -307,13 +343,17 @@
             go, ("ctx", "exp"), split_axis=0, concat_axis=0, axis_index_groups=groups, tiled=True
         )
         order = scattered(sum_stages)
+        order = order[1::2] + order[::2]
         places = [gathered([[masks[c]] for masks in res_masks]) for c in (0, 1)]
         res_at = by_core(*(jnp.array([place.index(o) for o in order], jnp.int32) for place in places))
-        hidden, keep, send = expert(
+        hidden, keep, send, acts = expert(
             (me ^ jnp.array(order, jnp.int32)) >> 1, res_at, att_all,
             res_all, proj_all, norm_gain, near_w, far_w,
         )
-        summed = scatter(keep, [send[k] for k in range(3)], sum_stages)
+        total = scatter(keep, [send[k] for k in range(3)], sum_stages[:1]).astype(BF)
+        keep, send = rest(acts, near_w[2], far_w[2])
+        summed = scatter(keep, [send[k] for k in range(3)], sum_stages[:1])
+        summed = summed + move(total, sum_stages[1][0]).astype(F32)
     else:
         att_all = lax.all_to_all(att, "exp", split_axis=0, concat_axis=2, tiled=True)[0]
         hidden = (res_all.astype(F32) + dot(att_all, proj_all)).astype(BF).astype(F32)

time: 71.9 us -> 72.3 us (level)
  waiting for transfers between devices: 22.6 us -> 17 us
  Pallas kernels: 8.48 us -> 11.6 us
  other arithmetic: 4.74 us -> 6.15 us
  starting transfers between devices: 32.1 us -> 33.5 us
    ppermute x21, waiting for transfers between devices: 20 us -> 14.4 us  [move(): return lax.ppermute(x, 'ctx', [(i, i ^ masks[i & 1]) for i in range(n)])]
    pallas_call x0 -> x1, Pallas kernels: none -> 2.47 us  [rest(): pl.pallas_call(rest_kernel, out_shape=(jax.ShapeDtypeStruct((size, feats)...]
    ppermute x21, starting transfers between devices: 22.9 us -> 24.4 us  [move(): return lax.ppermute(x, 'ctx', [(i, i ^ masks[i & 1]) for i in range(n)])]
    concatenate x1, other arithmetic: 0.18 us -> 1.57 us  [both_halves(): jnp.concatenate([jnp.where(first, mine, theirs), jnp.where(first, theirs,...]
  transfers between devices with their start and end apart: 24 -> 24, of which waited for: 13 -> 12; matrix products, arithmetic and copies ran while one was open for 9% -> 11% of each run, Pallas kernels for 0% -> 3%
where the time goes in v5:
time: 72.3 us; the launch traced here: 71.9 us
  starting transfers between devices  33.5 us (46%)
  waiting for transfers between devices  17 us (24%)
  Pallas kernels  11.6 us (16%)
  other arithmetic  6.15 us (9%)
  local copies, waits for them, and re-layouts  2.03 us (3%)
  matrix products  1.27 us (2%)
    ppermute x21, starting transfers between devices, move(): return lax.ppermute(x, 'ctx', [(i, i ^ masks[i & 1]) for i in range(n)])  24.4 us
    ppermute x21, waiting for transfers between devices, move(): return lax.ppermute(x, 'ctx', [(i, i ^ masks[i & 1]) for i in range(n)])  14.4 us
    pallas_call x1, Pallas kernels, expert(): pl.pallas_call(expert_kernel, out_shape=(jax.ShapeDtypeStruct((per, feats...  7.4 us
    all_to_all x1, starting transfers between devices, body(): lax.all_to_all(go, ('ctx', 'exp'), split_axis=0, concat_axis=0, axis_inde...  6.99 us
    pallas_call x1, Pallas kernels, rest(): pl.pallas_call(rest_kernel, out_shape=(jax.ShapeDtypeStruct((size, feats)...  2.47 us
    all_to_all x1, waiting for transfers between devices, body(): lax.all_to_all(go, ('ctx', 'exp'), split_axis=0, concat_axis=0, axis_inde...  2.42 us
    ppermute x2, starting transfers between devices, swap_exp(): return lax.ppermute(x, 'exp', [(0, 1), (1, 0)])  2.09 us
    pallas_call x1, Pallas kernels, prepare(): pl.pallas_call(functools.partial(prepare_kernel, far=dict(experts=experts...  1.74 us
  transfers between devices with their start and end apart: 24, of which 12 were waited for; matrix products, arithmetic and copies ran while one was open for 11% of the time, Pallas kernels for 3%

profile of v5, /device:TPU:0, one launch (start us, length us, event | category | flops | bytes accessed | tf_op | source)
XLA Modules:
  0.0 71.9 jit_solution(7566860718715797956)
XLA Ops:
  0.0 1.7 %shard_map.136 = (bf16[64,512]{1,0:T(8,128)(2,1)}, bf16[64,256]{1,0:T(8,128)(2,1)}, bf16[64,64]{1,0:T(8,128)(2,1)}, s32[1,1024]{1,0:T(1,128)}) custom-call(s32[1]{0:T(128)} %bitcast.me, s32[8,8]{1,0:T(8,128)} %mask.1, bf16[64,256]{1,0:T(8,128)(2,1)} %keys.1, bf16[64,256]{1,0:T(8,128)(2,1)} %values.1, bf16[64,256]{1,0:T(8,128)(2,1)} %queries.1, s32[1,64]{1,0:T(1,128)} %bitcast.35), custom_call_target="tpu_custom_call" | custom-call | tf_op jit(solution)/shard_map/pallas_call | solution.py:72
  1.8 5.0 %collective-permute-start.2 = (bf16[64,512]{1,0:T(8,128)(2,1)}, bf16[64,512]{1,0:T(8,128)(2,1)S(1)}, u32[]{:S(2)}, u32[]{:S(2)}) collective-permute-start(bf16[64,512]{1,0:T(8,128)(2,1)} %get-tuple-element.25), channel_id=1, source_target_pairs={{0,24},{2,26},{4,28},{6,30},{8,16},{10,18},{12,20},{14,22},{16,8},... | collective-permute-start | bytes 196616 | tf_op jit(solution)/shard_map/ppermute | solution.py:252
  6.8 0.6 collective-permute-start
  7.4 1.6 %collective-permute-start.3 = (bf16[64,1024]{1,0:T(8,128)(2,1)}, bf16[64,1024]{1,0:T(8,128)(2,1)S(1)}, u32[]{:S(2)}, u32[]{:S(2)}) collective-permute-start(bf16[64,1024]{1,0:T(8,128)(2,1)} %param.14), channel_id=1, source_target_pairs={{0,1},{1,0},{2,3},{3,2},{4,5},{5,4},{6,7},{7,6},{8,9},{9,8},{10,11... | collective-permute-start | bytes 393224 | tf_op jit(solution)/shard_map/ppermute | solution.py:258
  9.1 1.1 %constant_dynamic-slice_fusion = bf16[256,1024]{1,0:T(8,128)(2,1)S(1)} fusion(bf16[512,1024]{1,0:T(8,128)(2,1)} %param.18, s32[]{:T(128)S(6)} %select_n.69), kind=kLoop, calls=%fused_computation.59 | loop fusion | bytes 1048580 | tf_op jit(solution)/shard_map/dynamic_slice | solution.py:285
  10.2 0.4 collective-permute-start.7
  10.6 0.7 compare_reduce_fusion
  11.3 1.3 %collective-permute-done.1 = bf16[64,512]{1,0:T(8,128)(2,1)S(1)} collective-permute-done((bf16[64,512]{1,0:T(8,128)(2,1)}, bf16[64,512]{1,0:T(8,128)(2,1)S(1)}, u32[]{:S(2)}, u32[]{:S(2)}) %collective-permute-start.1) | collective-permute-done | bytes 65568 | tf_op jit(solution)/shard_map/ppermute | solution.py:252
  12.6 0.9 %pad_maximum_fusion.3 = bf16[256,512]{1,0:T(8,128)(2,1)S(1)} fusion(bf16[64,512]{1,0:T(8,128)(2,1)S(1)} %collective-permute-done.2, bf16[64,512]{1,0:T(8,128)(2,1)S(1)} %collective-permute-done.1, bf16[64,512]{1,0:T(8,128)(2,1)S(1)} %collective-permute-done, bf16[64,512]{1,0:T(8,128)(2,1)} %get-tuple-element.25), kind=kLoop, calls=%fused_computation.20 | loop fusion | flops 1048576 | bytes 524288 | tf_op jit(solution)/shard_map/concatenate | solution.py:262
  13.5 0.2 collective-permute-done.3
  13.7 1.8 %collective-permute-start.5 = (bf16[128,512]{1,0:T(8,128)(2,1)S(1)}, bf16[128,512]{1,0:T(8,128)(2,1)S(1)}, u32[]{:S(2)}, u32[]{:S(2)}) collective-permute-start(bf16[128,512]{1,0:T(8,128)(2,1)S(1)} %get-tuple-element.55), channel_id=1, source_target_pairs={{0,4},{2,6},{4,0},{6,2},{8,12},{10,14},{12,8},{14,10},{16,20},{18,... | collective-permute-start | bytes 393224 | tf_op jit(solution)/shard_map/ppermute | solution.py:252
  15.5 0.3 collective-permute-start.4
  15.8 0.2 convolution_convert_fusion
  16.0 2.4 %collective-permute-start.8 = (bf16[32,2048]{1,0:T(8,128)(2,1)S(1)}, bf16[32,2048]{1,0:T(8,128)(2,1)S(1)}, u32[]{:S(2)}, u32[]{:S(2)}) collective-permute-start(bf16[32,2048]{1,0:T(8,128)(2,1)S(1)} %convolution_convert_fusion), channel_id=1, source_target_pairs={{0,16},{2,18},{4,20},{6,22},{8,24},{10,26},{12,28},{14,30},{16,0},... | collective-permute-start | bytes 393224 | tf_op jit(solution)/shard_map/ppermute | solution.py:252
  18.3 1.7 %collective-permute-done.5 = bf16[128,512]{1,0:T(8,128)(2,1)S(1)} collective-permute-done((bf16[128,512]{1,0:T(8,128)(2,1)S(1)}, bf16[128,512]{1,0:T(8,128)(2,1)S(1)}, u32[]{:S(2)}, u32[]{:S(2)}) %collective-permute-start.5) | collective-permute-done | bytes 131104 | tf_op jit(solution)/shard_map/ppermute | solution.py:252
  20.1 1.4 %collective-permute-done.4 = bf16[128,512]{1,0:T(8,128)(2,1)S(1)} collective-permute-done((bf16[128,512]{1,0:T(8,128)(2,1)S(1)}, bf16[128,512]{1,0:T(8,128)(2,1)S(1)}, u32[]{:S(2)}, u32[]{:S(2)}) %collective-permute-start.4) | collective-permute-done | bytes 131104 | tf_op jit(solution)/shard_map/ppermute | solution.py:252
  21.7 2.0 %collective-permute-done.8 = bf16[32,2048]{1,0:T(8,128)(2,1)S(1)} collective-permute-done((bf16[32,2048]{1,0:T(8,128)(2,1)S(1)}, bf16[32,2048]{1,0:T(8,128)(2,1)S(1)}, u32[]{:S(2)}, u32[]{:S(2)}) %collective-permute-start.8) | collective-permute-done | bytes 131104 | tf_op jit(solution)/shard_map/ppermute | solution.py:252
  23.8 0.3 fusion.32
  24.1 0.3 fusion.33
  24.4 0.3 fusion.11
  24.7 0.2 fusion.3
  24.9 0.2 fusion.2
  25.2 0.7 %broadcast_in_dim.54 = bf16[8,2,32,256]{3,2,1,0:T(8,128)(2,1)} broadcast(bf16[2,32,256]{2,1,0:T(8,128)(2,1)S(1)} %bitcast.34), dimensions={1,2,3} | broadcast | bytes 294912 | tf_op jit(solution)/shard_map/broadcast_in_dim | solution.py:332
  26.0 0.5 collective-permute-start.14
  26.5 0.5 collective-permute-start.12
  27.2 7.0 %all-to-all-start = ((bf16[16,32,256]{2,1,0:T(8,128)(2,1)}), bf16[16,32,256]{2,1,0:T(8,128)(2,1)S(1)}, u32[]{:S(2)}, u32[]{:S(2)}) async-start(bf16[16,32,256]{2,1,0:T(8,128)(2,1)} %bitcast.3), calls=%async_computation | async-start | bytes 524288 | tf_op jit(solution)/shard_map/all_to_all | solution.py:342
  34.2 2.0 %collective-permute-start.10 = (bf16[64,2048]{1,0:T(8,128)(2,1)S(1)}, bf16[64,2048]{1,0:T(8,128)(2,1)S(1)}, u32[]{:S(2)}, u32[]{:S(2)}) collective-permute-start(bf16[64,2048]{1,0:T(8,128)(2,1)S(1)} %pad_maximum_fusion.4), channel_id=1, source_target_pairs={{0,4},{2,10},{4,0},{6,14},{8,12},{10,2},{12,8},{14,6},{16,20},{18,... | collective-permute-start | bytes 786440 | tf_op jit(solution)/shard_map/ppermute | solution.py:252
  36.2 1.1 %collective-permute-done.12 = bf16[256,1024]{1,0:T(8,128)(2,1)} collective-permute-done((bf16[256,1024]{1,0:T(8,128)(2,1)}, bf16[256,1024]{1,0:T(8,128)(2,1)}, u32[]{:S(2)}, u32[]{:S(2)}) %collective-permute-start.12) | collective-permute-done | bytes 524320 | tf_op jit(solution)/shard_map/ppermute | solution.py:252
  37.2 1.5 %collective-permute-start.11 = (bf16[64,2048]{1,0:T(8,128)(2,1)S(1)}, bf16[64,2048]{1,0:T(8,128)(2,1)S(1)}, u32[]{:S(2)}, u32[]{:S(2)}) collective-permute-start(bf16[64,2048]{1,0:T(8,128)(2,1)S(1)} %collective-permute-done.9), channel_id=1, source_target_pairs={{0,4},{2,10},{4,0},{6,14},{8,12},{10,2},{12,8},{14,6},{16,20},{18,... | collective-permute-start | bytes 786440 | tf_op jit(solution)/shard_map/ppermute | solution.py:252
  38.7 1.3 %broadcast_select_fusion.3 = (bf16[256,1024]{1,0:T(8,128)(2,1)S(1)}, bf16[256,1024]{1,0:T(8,128)(2,1)S(1)}) fusion(bf16[256,1024]{1,0:T(8,128)(2,1)} %collective-permute-done.7, bf16[256,1024]{1,0:T(8,128)(2,1)} %collective-permute-done.12, pred[]{:T(512)S(6)} %eq.8), kind=kLoop, calls=%fused_computation.15 | loop fusion | flops 524288 | bytes 2097153 | tf_op jit(solution)/shard_map/jit(_where)/select_n | solution.py:248
  40.0 0.6 broadcast_select_fusion.1
  40.6 1.6 %pad_maximum_fusion.proj = bf16[512,2048]{1,0:T(8,128)(2,1)} fusion(bf16[512,1024]{1,0:T(8,128)(2,1)S(1)} %get-tuple-element.44, bf16[512,1024]{1,0:T(8,128)(2,1)S(1)} %get-tuple-element.43), kind=kLoop, calls=%fused_computation.1 | loop fusion | flops 4194304 | bytes 4194304 | tf_op jit(solution)/shard_map/concatenate | solution.py:300
  42.2 0.2 collective-permute-done.10
  42.4 2.4 %all-to-all-done.att = bf16[16,32,256]{2,1,0:T(8,128)(2,1)S(1)} async-done(((bf16[16,32,256]{2,1,0:T(8,128)(2,1)}), bf16[16,32,256]{2,1,0:T(8,128)(2,1)S(1)}, u32[]{:S(2)}, u32[]{:S(2)}) %all-to-all-start) | async-done | bytes 262176 | tf_op jit(solution)/shard_map/all_to_all | solution.py:342
  44.8 0.9 %collective-permute-done.11 = bf16[64,2048]{1,0:T(8,128)(2,1)S(1)} collective-permute-done((bf16[64,2048]{1,0:T(8,128)(2,1)S(1)}, bf16[64,2048]{1,0:T(8,128)(2,1)S(1)}, u32[]{:S(2)}, u32[]{:S(2)}) %collective-permute-start.11) | collective-permute-done | bytes 262176 | tf_op jit(solution)/shard_map/ppermute | solution.py:252
  45.8 7.4 %shard_map.137 = (f32[32,2048]{1,0:T(8,128)S(1)}, f32[32,2048]{1,0:T(8,128)S(1)}, bf16[3,32,2048]{2,1,0:T(8,128)(2,1)S(1)}, bf16[2,128,512]{2,1,0:T(8,128)(2,1)S(1)}) custom-call(s32[8]{0:T(128)S(1)} %xor_shift-right-arithmetic_fusion.att_at, s32[8]{0:T(128)S(1)} %broadcast_select_fusion.6.res_at, bf16[16,32,256]{2,1,0:T(8,128)(2,1)S(1)} %all-to-all-done.att, ...), custom_call_target="tpu_custom_call" | custom-call | flops 3221225472 | bytes 12582912 | tf_op jit(solution)/shard_map/pallas_call | solution.py:204
  53.2 1.8 %collective-permute-start.19 = (bf16[32,2048]{1,0:T(8,128)(2,1)S(1)}, bf16[32,2048]{1,0:T(8,128)(2,1)S(1)}, u32[]{:S(2)}, u32[]{:S(2)}) collective-permute-start(bf16[32,2048]{1,0:T(8,128)(2,1)S(1)} %get-tuple-element.50), channel_id=1, source_target_pairs={{0,12},{2,14},{4,8},{6,10},{8,4},{10,6},{12,0},{14,2},{16,28},{18,... | collective-permute-start | bytes 393224 | tf_op jit(solution)/shard_map/ppermute | solution.py:252
  55.0 1.3 %collective-permute-start.21 = (bf16[32,2048]{1,0:T(8,128)(2,1)S(1)}, bf16[32,2048]{1,0:T(8,128)(2,1)S(1)}, u32[]{:S(2)}, u32[]{:S(2)}) collective-permute-start(bf16[32,2048]{1,0:T(8,128)(2,1)S(1)} %get-tuple-element.51), channel_id=1, source_target_pairs={{0,4},{2,6},{4,0},{6,2},{8,12},{10,14},{12,8},{14,10},{16,20},{18,... | collective-permute-start | bytes 393224 | tf_op jit(solution)/shard_map/ppermute | solution.py:252
  56.3 0.5 collective-permute-start.20
  56.8 2.5 %shard_map.138 = (f32[32,2048]{1,0:T(8,128)S(1)}, bf16[3,32,2048]{2,1,0:T(8,128)(2,1)S(1)}) custom-call(bf16[2,128,512]{2,1,0:T(8,128)(2,1)S(1)} %get-tuple-element.36.acts, bf16[512,2048]{1,0:T(8,128)(2,1)S(1)} %bitcast.28, bf16[512,2048]{1,0:T(8,128)(2,1)} %collective-permute-done.15.down1), custom_call_target="tpu_custom_call" | custom-call | tf_op jit(solution)/shard_map/pallas_call | solution.py:184
  59.3 1.8 %collective-permute-start.16 = (bf16[32,2048]{1,0:T(8,128)(2,1)S(1)}, bf16[32,2048]{1,0:T(8,128)(2,1)S(1)}, u32[]{:S(2)}, u32[]{:S(2)}) collective-permute-start(bf16[32,2048]{1,0:T(8,128)(2,1)S(1)} %get-tuple-element.47), channel_id=1, source_target_pairs={{0,12},{2,14},{4,8},{6,10},{8,4},{10,6},{12,0},{14,2},{16,28},{18,... | collective-permute-start | bytes 393224 | tf_op jit(solution)/shard_map/ppermute | solution.py:252
  61.1 1.3 %collective-permute-start.18 = (bf16[32,2048]{1,0:T(8,128)(2,1)S(1)}, bf16[32,2048]{1,0:T(8,128)(2,1)S(1)}, u32[]{:S(2)}, u32[]{:S(2)}) collective-permute-start(bf16[32,2048]{1,0:T(8,128)(2,1)S(1)} %get-tuple-element.48), channel_id=1, source_target_pairs={{0,4},{2,6},{4,0},{6,2},{8,12},{10,14},{12,8},{14,10},{16,20},{18,... | collective-permute-start | bytes 393224 | tf_op jit(solution)/shard_map/ppermute | solution.py:252
  62.4 0.5 collective-permute-start.17
  62.8 0.2 collective-permute-done.21
  63.1 2.4 %collective-permute-start.22 = (bf16[32,2048]{1,0:T(8,128)(2,1)S(1)}, bf16[32,2048]{1,0:T(8,128)(2,1)S(1)}, u32[]{:S(2)}, u32[]{:S(2)}) collective-permute-start(bf16[32,2048]{1,0:T(8,128)(2,1)S(1)} %add_convert_fusion.1), channel_id=1, source_target_pairs={{0,16},{2,18},{4,20},{6,22},{8,24},{10,26},{12,28},{14,30},{16,0},... | collective-permute-start | bytes 393224 | tf_op jit(solution)/shard_map/ppermute | solution.py:252
  65.5 3.3 %collective-permute-done.16 = bf16[32,2048]{1,0:T(8,128)(2,1)S(1)} collective-permute-done((bf16[32,2048]{1,0:T(8,128)(2,1)S(1)}, bf16[32,2048]{1,0:T(8,128)(2,1)S(1)}, u32[]{:S(2)}, u32[]{:S(2)}) %collective-permute-start.16) | collective-permute-done | bytes 131104 | tf_op jit(solution)/shard_map/ppermute | solution.py:252
  68.8 2.3 %collective-permute-done.17 = bf16[32,2048]{1,0:T(8,128)(2,1)S(1)} collective-permute-done((bf16[32,2048]{1,0:T(8,128)(2,1)S(1)}, bf16[32,2048]{1,0:T(8,128)(2,1)S(1)}, u32[]{:S(2)}, u32[]{:S(2)}) %collective-permute-start.17) | collective-permute-done | bytes 131104 | tf_op jit(solution)/shard_map/ppermute | solution.py:252
  71.1 0.8 %fusion.17 = bf16[1,32,2048]{2,1,0:T(8,128)(2,1)} fusion(f32[32,2048]{1,0:T(8,128)S(1)} %get-tuple-element.35, bf16[32,2048]{1,0:T(8,128)(2,1)S(1)} %collective-permute-done.22, bf16[32,2048]{1,0:T(8,128)(2,1)S(1)} %collective-permute-done.18, bf16[32,2048]{1,0:T(8,128)(2,1)S(1)} %collective-permute-done.17, f32[32,2048]{1,0:T(8,128)S(1)} %get-tuple-element.37, ...), kind=kLoop, calls=%fused_computation.33 | loop fusion | flops 655360 | bytes 1179648 | tf_op jit(solution)/shard_map/broadcast_in_dim | solution.py:368
  (51 shorter events, 0.6 us)
Async XLA Ops:
  0.0 15.8 %copy-start.4 = (bf16[64,1024]{1,0:T(8,128)(2,1)S(1)}, bf16[64,1024]{1,0:T(8,128)(2,1)}, u32[]{:S(2)}) copy-start(bf16[64,1024]{1,0:T(8,128)(2,1)} %param.14) | copy-start | bytes 393220
  1.7 14.1 %copy-start.8 = (bf16[64,64]{1,0:T(8,128)(2,1)S(1)}, bf16[64,64]{1,0:T(8,128)(2,1)}, u32[]{:S(2)}) copy-start(bf16[64,64]{1,0:T(8,128)(2,1)} %get-tuple-element.27) | copy-start | bytes 24580
  1.8 9.6 %collective-permute-start.2 = (bf16[64,512]{1,0:T(8,128)(2,1)}, bf16[64,512]{1,0:T(8,128)(2,1)S(1)}, u32[]{:S(2)}, u32[]{:S(2)}) collective-permute-start(bf16[64,512]{1,0:T(8,128)(2,1)} %get-tuple-element.25), channel_id=1, source_target_pairs={{0,24},{2,26},{4,28},{6,30},{8,16},{10,18},{12,20},{14,22},{16,8},... | collective-permute-start | bytes 196616 | tf_op jit(solution)/shard_map/ppermute | solution.py:252
  6.8 5.8 %collective-permute-start.1 = (bf16[64,512]{1,0:T(8,128)(2,1)}, bf16[64,512]{1,0:T(8,128)(2,1)S(1)}, u32[]{:S(2)}, u32[]{:S(2)}) collective-permute-start(bf16[64,512]{1,0:T(8,128)(2,1)} %get-tuple-element.25), channel_id=1, source_target_pairs={{0,16},{2,18},{4,20},{6,22},{8,24},{10,26},{12,28},{14,30},{16,0},... | collective-permute-start | bytes 196616 | tf_op jit(solution)/shard_map/ppermute | solution.py:252
  6.8 5.8 %collective-permute-start = (bf16[64,512]{1,0:T(8,128)(2,1)}, bf16[64,512]{1,0:T(8,128)(2,1)S(1)}, u32[]{:S(2)}, u32[]{:S(2)}) collective-permute-start(bf16[64,512]{1,0:T(8,128)(2,1)} %get-tuple-element.25), channel_id=1, source_target_pairs={{0,8},{2,10},{4,12},{6,14},{8,0},{10,2},{12,4},{14,6},{16,24},{18,... | collective-permute-start | bytes 196616 | tf_op jit(solution)/shard_map/ppermute | solution.py:252
  7.4 6.2 %collective-permute-start.3 = (bf16[64,1024]{1,0:T(8,128)(2,1)}, bf16[64,1024]{1,0:T(8,128)(2,1)S(1)}, u32[]{:S(2)}, u32[]{:S(2)}) collective-permute-start(bf16[64,1024]{1,0:T(8,128)(2,1)} %param.14), channel_id=1, source_target_pairs={{0,1},{1,0},{2,3},{3,2},{4,5},{5,4},{6,7},{7,6},{8,9},{9,8},{10,11... | collective-permute-start | bytes 393224 | tf_op jit(solution)/shard_map/ppermute | solution.py:258
  10.2 15.1 %collective-permute-start.7 = (bf16[256,1024]{1,0:T(8,128)(2,1)S(1)}, bf16[256,1024]{1,0:T(8,128)(2,1)}, u32[]{:S(2)}, u32[]{:S(2)}) collective-permute-start(bf16[256,1024]{1,0:T(8,128)(2,1)S(1)} %constant_dynamic-slice_fusion), channel_id=1, source_target_pairs={{0,1},{1,0},{2,3},{3,2},{4,5},{5,4},{6,7},{7,6},{8,9},{9,8},{10,11... | collective-permute-start | bytes 1572872 | tf_op jit(solution)/shard_map/ppermute | solution.py:258
  13.7 6.4 %collective-permute-start.5 = (bf16[128,512]{1,0:T(8,128)(2,1)S(1)}, bf16[128,512]{1,0:T(8,128)(2,1)S(1)}, u32[]{:S(2)}, u32[]{:S(2)}) collective-permute-start(bf16[128,512]{1,0:T(8,128)(2,1)S(1)} %get-tuple-element.55), channel_id=1, source_target_pairs={{0,4},{2,6},{4,0},{6,2},{8,12},{10,14},{12,8},{14,10},{16,20},{18,... | collective-permute-start | bytes 393224 | tf_op jit(solution)/shard_map/ppermute | solution.py:252
  15.5 6.0 %collective-permute-start.4 = (bf16[128,512]{1,0:T(8,128)(2,1)S(1)}, bf16[128,512]{1,0:T(8,128)(2,1)S(1)}, u32[]{:S(2)}, u32[]{:S(2)}) collective-permute-start(bf16[128,512]{1,0:T(8,128)(2,1)S(1)} %get-tuple-element.56), channel_id=1, source_target_pairs={{0,4},{2,6},{4,0},{6,2},{8,12},{10,14},{12,8},{14,10},{16,20},{18,... | collective-permute-start | bytes 393224 | tf_op jit(solution)/shard_map/ppermute | solution.py:252
  15.8 8.0 %copy-start.5 = (bf16[64,256]{1,0:T(8,128)(2,1)S(1)}, bf16[64,256]{1,0:T(8,128)(2,1)}, u32[]{:S(2)}) copy-start(bf16[64,256]{1,0:T(8,128)(2,1)} %get-tuple-element.24) | copy-start | bytes 98308
  16.0 7.7 %collective-permute-start.8 = (bf16[32,2048]{1,0:T(8,128)(2,1)S(1)}, bf16[32,2048]{1,0:T(8,128)(2,1)S(1)}, u32[]{:S(2)}, u32[]{:S(2)}) collective-permute-start(bf16[32,2048]{1,0:T(8,128)(2,1)S(1)} %convolution_convert_fusion), channel_id=1, source_target_pairs={{0,16},{2,18},{4,20},{6,22},{8,24},{10,26},{12,28},{14,30},{16,0},... | collective-permute-start | bytes 393224 | tf_op jit(solution)/shard_map/ppermute | solution.py:252
  21.5 2.2 %collective-permute-start.6 = (bf16[512,512]{1,0:T(8,128)(2,1)S(1)}, bf16[512,512]{1,0:T(8,128)(2,1)S(1)}, u32[]{:S(2)}, u32[]{:S(2)}) collective-permute-start(bf16[512,512]{1,0:T(8,128)(2,1)S(1)} %pad_maximum_fusion.2), channel_id=1, source_target_pairs={{0,2},{2,0},{4,6},{6,4},{8,10},{10,8},{12,14},{14,12},{16,18},{18,... | collective-permute-start | bytes 1572872 | tf_op jit(solution)/shard_map/ppermute | solution.py:252
  23.7 2.8 %copy-start = (bf16[1,512,2048]{2,1,0:T(8,128)(2,1)S(1)}, bf16[1,512,2048]{2,1,0:T(8,128)(2,1)}, u32[]{:S(2)}) copy-start(bf16[1,512,2048]{2,1,0:T(8,128)(2,1)} %param.22) | copy-start | bytes 6291460
  23.7 3.4 %copy-start.9 = (s32[8]{0:T(128)S(1)}, s32[8]{0:T(128)}, u32[]{:S(2)}) copy-start(s32[8]{0:T(128)} %constant.38.clone) | copy-start | bytes 100
  23.7 3.4 %copy-start.6 = (s32[8]{0:T(128)S(1)}, s32[8]{0:T(128)}, u32[]{:S(2)}) copy-start(s32[8]{0:T(128)} %constant.37.clone) | copy-start | bytes 100
  23.7 3.4 %copy-start.7 = (s32[8]{0:T(128)S(1)}, s32[8]{0:T(128)}, u32[]{:S(2)}) copy-start(s32[8]{0:T(128)} %constant.36.clone) | copy-start | bytes 100
  26.0 19.8 %collective-permute-start.13 = (bf16[2048,512]{1,0:T(8,128)(2,1)}, bf16[2048,512]{1,0:T(8,128)(2,1)}, u32[]{:S(2)}, u32[]{:S(2)}) collective-permute-start(bf16[2048,512]{1,0:T(8,128)(2,1)} %bitcast.4.gate0), channel_id=1, source_target_pairs={{0,2},{2,0},{4,6},{6,4},{8,10},{10,8},{12,14},{14,12},{16,18},{18,... | collective-permute-start | bytes 6291464 | tf_op jit(solution)/shard_map/ppermute | solution.py:252
  26.0 19.8 %collective-permute-start.14 = (bf16[2048,512]{1,0:T(8,128)(2,1)}, bf16[2048,512]{1,0:T(8,128)(2,1)}, u32[]{:S(2)}, u32[]{:S(2)}) collective-permute-start(bf16[2048,512]{1,0:T(8,128)(2,1)} %bitcast.5.up0), channel_id=1, source_target_pairs={{0,2},{2,0},{4,6},{6,4},{8,10},{10,8},{12,14},{14,12},{16,18},{18,... | collective-permute-start | bytes 6291464 | tf_op jit(solution)/shard_map/ppermute | solution.py:252
  26.5 19.2 %collective-permute-start.15 = (bf16[512,2048]{1,0:T(8,128)(2,1)S(1)}, bf16[512,2048]{1,0:T(8,128)(2,1)}, u32[]{:S(2)}, u32[]{:S(2)}) collective-permute-start(bf16[512,2048]{1,0:T(8,128)(2,1)S(1)} %bitcast.27), channel_id=1, source_target_pairs={{0,2},{2,0},{4,6},{6,4},{8,10},{10,8},{12,14},{14,12},{16,18},{18,... | collective-permute-start | bytes 6291464 | tf_op jit(solution)/shard_map/ppermute | solution.py:252
  26.5 10.7 %collective-permute-start.12 = (bf16[256,1024]{1,0:T(8,128)(2,1)}, bf16[256,1024]{1,0:T(8,128)(2,1)}, u32[]{:S(2)}, u32[]{:S(2)}) collective-permute-start(bf16[256,1024]{1,0:T(8,128)(2,1)} %collective-permute-done.7), channel_id=1, source_target_pairs={{0,2},{2,0},{4,6},{6,4},{8,10},{10,8},{12,14},{14,12},{16,18},{18,... | collective-permute-start | bytes 1572872 | tf_op jit(solution)/shard_map/ppermute | solution.py:252
  27.0 7.2 %collective-permute-start.9 = (bf16[64,2048]{1,0:T(8,128)(2,1)S(1)}, bf16[64,2048]{1,0:T(8,128)(2,1)S(1)}, u32[]{:S(2)}, u32[]{:S(2)}) collective-permute-start(bf16[64,2048]{1,0:T(8,128)(2,1)S(1)} %pad_maximum_fusion.4), channel_id=1, source_target_pairs={{0,8},{2,6},{4,12},{6,2},{8,0},{10,14},{12,4},{14,10},{16,24},{18,... | collective-permute-start | bytes 786440 | tf_op jit(solution)/shard_map/ppermute | solution.py:252
  27.2 17.6 %all-to-all-start = ((bf16[16,32,256]{2,1,0:T(8,128)(2,1)}), bf16[16,32,256]{2,1,0:T(8,128)(2,1)S(1)}, u32[]{:S(2)}, u32[]{:S(2)}) async-start(bf16[16,32,256]{2,1,0:T(8,128)(2,1)} %bitcast.3), calls=%async_computation | async-start | bytes 524288 | tf_op jit(solution)/shard_map/all_to_all | solution.py:342
  34.1 5.9 %copy-start.3 = (bf16[512,1024]{1,0:T(8,128)(2,1)S(1)}, bf16[512,1024]{1,0:T(8,128)(2,1)}, u32[]{:S(2)}) copy-start(bf16[512,1024]{1,0:T(8,128)(2,1)} %param.18) | copy-start | bytes 3145732
  34.2 8.2 %collective-permute-start.10 = (bf16[64,2048]{1,0:T(8,128)(2,1)S(1)}, bf16[64,2048]{1,0:T(8,128)(2,1)S(1)}, u32[]{:S(2)}, u32[]{:S(2)}) collective-permute-start(bf16[64,2048]{1,0:T(8,128)(2,1)S(1)} %pad_maximum_fusion.4), channel_id=1, source_target_pairs={{0,4},{2,10},{4,0},{6,14},{8,12},{10,2},{12,8},{14,6},{16,20},{18,... | collective-permute-start | bytes 786440 | tf_op jit(solution)/shard_map/ppermute | solution.py:252
  37.2 8.5 %collective-permute-start.11 = (bf16[64,2048]{1,0:T(8,128)(2,1)S(1)}, bf16[64,2048]{1,0:T(8,128)(2,1)S(1)}, u32[]{:S(2)}, u32[]{:S(2)}) collective-permute-start(bf16[64,2048]{1,0:T(8,128)(2,1)S(1)} %collective-permute-done.9), channel_id=1, source_target_pairs={{0,4},{2,10},{4,0},{6,14},{8,12},{10,2},{12,8},{14,6},{16,20},{18,... | collective-permute-start | bytes 786440 | tf_op jit(solution)/shard_map/ppermute | solution.py:252
  40.6 5.1 %copy-start.2 = (f32[2048]{0:T(1024)S(1)}, f32[2048]{0:T(1024)}, u32[]{:S(2)}) copy-start(f32[2048]{0:T(1024)} %param.19) | copy-start | bytes 24580
  45.7 11.0 %copy-start.1 = (bf16[1,512,2048]{2,1,0:T(8,128)(2,1)S(1)}, bf16[1,512,2048]{2,1,0:T(8,128)(2,1)}, u32[]{:S(2)}) copy-start(bf16[1,512,2048]{2,1,0:T(8,128)(2,1)} %param.22) | copy-start | bytes 6291460
  53.2 9.2 %collective-permute-start.19 = (bf16[32,2048]{1,0:T(8,128)(2,1)S(1)}, bf16[32,2048]{1,0:T(8,128)(2,1)S(1)}, u32[]{:S(2)}, u32[]{:S(2)}) collective-permute-start(bf16[32,2048]{1,0:T(8,128)(2,1)S(1)} %get-tuple-element.50), channel_id=1, source_target_pairs={{0,12},{2,14},{4,8},{6,10},{8,4},{10,6},{12,0},{14,2},{16,28},{18,... | collective-permute-start | bytes 393224 | tf_op jit(solution)/shard_map/ppermute | solution.py:252
  55.0 8.0 %collective-permute-start.21 = (bf16[32,2048]{1,0:T(8,128)(2,1)S(1)}, bf16[32,2048]{1,0:T(8,128)(2,1)S(1)}, u32[]{:S(2)}, u32[]{:S(2)}) collective-permute-start(bf16[32,2048]{1,0:T(8,128)(2,1)S(1)} %get-tuple-element.51), channel_id=1, source_target_pairs={{0,4},{2,6},{4,0},{6,2},{8,12},{10,14},{12,8},{14,10},{16,20},{18,... | collective-permute-start | bytes 393224 | tf_op jit(solution)/shard_map/ppermute | solution.py:252
  56.3 6.8 %collective-permute-start.20 = (bf16[32,2048]{1,0:T(8,128)(2,1)S(1)}, bf16[32,2048]{1,0:T(8,128)(2,1)S(1)}, u32[]{:S(2)}, u32[]{:S(2)}) collective-permute-start(bf16[32,2048]{1,0:T(8,128)(2,1)S(1)} %get-tuple-element.52), channel_id=1, source_target_pairs={{0,8},{2,10},{4,12},{6,14},{8,0},{10,2},{12,4},{14,6},{16,24},{18,... | collective-permute-start | bytes 393224 | tf_op jit(solution)/shard_map/ppermute | solution.py:252
  59.3 9.5 %collective-permute-start.16 = (bf16[32,2048]{1,0:T(8,128)(2,1)S(1)}, bf16[32,2048]{1,0:T(8,128)(2,1)S(1)}, u32[]{:S(2)}, u32[]{:S(2)}) collective-permute-start(bf16[32,2048]{1,0:T(8,128)(2,1)S(1)} %get-tuple-element.47), channel_id=1, source_target_pairs={{0,12},{2,14},{4,8},{6,10},{8,4},{10,6},{12,0},{14,2},{16,28},{18,... | collective-permute-start | bytes 393224 | tf_op jit(solution)/shard_map/ppermute | solution.py:252
  61.1 7.7 %collective-permute-start.18 = (bf16[32,2048]{1,0:T(8,128)(2,1)S(1)}, bf16[32,2048]{1,0:T(8,128)(2,1)S(1)}, u32[]{:S(2)}, u32[]{:S(2)}) collective-permute-start(bf16[32,2048]{1,0:T(8,128)(2,1)S(1)} %get-tuple-element.48), channel_id=1, source_target_pairs={{0,4},{2,6},{4,0},{6,2},{8,12},{10,14},{12,8},{14,10},{16,20},{18,... | collective-permute-start | bytes 393224 | tf_op jit(solution)/shard_map/ppermute | solution.py:252
  62.4 8.8 %collective-permute-start.17 = (bf16[32,2048]{1,0:T(8,128)(2,1)S(1)}, bf16[32,2048]{1,0:T(8,128)(2,1)S(1)}, u32[]{:S(2)}, u32[]{:S(2)}) collective-permute-start(bf16[32,2048]{1,0:T(8,128)(2,1)S(1)} %get-tuple-element.49), channel_id=1, source_target_pairs={{0,8},{2,10},{4,12},{6,14},{8,0},{10,2},{12,4},{14,6},{16,24},{18,... | collective-permute-start | bytes 393224 | tf_op jit(solution)/shard_map/ppermute | solution.py:252
  63.1 8.0 %collective-permute-start.22 = (bf16[32,2048]{1,0:T(8,128)(2,1)S(1)}, bf16[32,2048]{1,0:T(8,128)(2,1)S(1)}, u32[]{:S(2)}, u32[]{:S(2)}) collective-permute-start(bf16[32,2048]{1,0:T(8,128)(2,1)S(1)} %add_convert_fusion.1), channel_id=1, source_target_pairs={{0,16},{2,18},{4,20},{6,22},{8,24},{10,26},{12,28},{14,30},{16,0},... | collective-permute-start | bytes 393224 | tf_op jit(solution)/shard_map/ppermute | solution.py:252
